TPU v7x, 32 devices: a whole 2x2x4 slice. The times are simulated.
32 devices in a mesh: pair: 4 (over z), row: 4 (over x, core), col: 2 (over y).
Axes of the slice: x: 2, y: 2, z: 4, core: 2. Of those that a mesh axis runs over, the one named last changes fastest.
Arguments:
- integrals: bfloat16 [3072, 4096], P(('pair', 'col')), may hold values from -0.15625 to 0.15625
- inverse_factor: bfloat16 [4096, 4096], P('row', ('pair', 'col')), may hold values from -4 to 4, as said below
- energies: float32 [3072], P('pair'), may hold values from 0.25 to 8
- frequency: float32 [1], replicated, may hold values from 0.5 to 2
Outputs:
- response: float32 [4096, 4096], P(('row', 'pair'), 'col')
Inputs may be any that keep to these rules, and one draw needn't show every extreme that they name: `inverse_factor`: zero above the diagonal; the diagonal lies between 0.5 and 3.
All inputs are finite; a program needn't handle non-finite values.
Results may differ from a plain program's by a relative error of at most 0.0025.
Values may be sent and summed in bfloat16 or wider, within the bound.
No kernel may reach another device: no remote copies, remote signals or barrier semaphores. Data moves between devices by JAX's collectives and lax.ppermute only.
A program may use at most 64 MiB of HBM per device.

v0:
```python
import jax
import jax.numpy as jnp
from jax import lax
from jax.sharding import PartitionSpec as P


def contract(x_columns, portion):
    return lax.dot_general(
        x_columns, portion, (((1,), (1,)), ((), ())), preferred_element_type=jnp.float32
    )


def on_device(integrals, inverse_factor, energies, frequency):
    n_col = lax.axis_size("col")
    aux_width = integrals.shape[1]
    q_cols = aux_width // n_col
    local_rows = contract(
        integrals, lax.all_gather(inverse_factor, ("pair", "col"), axis=1, tiled=True)
    )
    group_b = lax.all_gather(local_rows.astype(jnp.bfloat16), "col", axis=0, tiled=True)
    col_position = lax.axis_index("col")
    empty = jnp.zeros((group_b.shape[0], q_cols), jnp.bfloat16)
    portion = lax.all_gather(group_b, "row", axis=1, tiled=True)
    portion_width = portion.shape[1]
    wanted = col_position * q_cols + jnp.arange(q_cols, dtype=jnp.int32)
    inside = (wanted >= 0) & (wanted < portion_width)
    selected = jnp.take(portion, jnp.clip(wanted, 0, portion_width - 1), axis=1)
    col_b = jnp.where(inside[None, :], selected, empty)
    factor = 2.0 * energies / (energies * energies + frequency[0] * frequency[0])
    scaled = (factor[:, None] * group_b.astype(jnp.float32)).astype(jnp.bfloat16)
    return lax.psum_scatter(
        lax.dot_general(
            scaled, col_b, (((0,), (0,)), ((), ())), preferred_element_type=jnp.float32
        ),
        "pair",
        scatter_dimension=0,
        tiled=True,
    )


def solution(mesh):
    return jax.shard_map(
        on_device,
        mesh=mesh,
        in_specs=(P(("pair", "col"), None), P("row", ("pair", "col")), P("pair"), P()),
        out_specs=P(("row", "pair"), "col"),
        check_vma=False,
    )
```

profile of v0, /device:TPU:19, one launch (start us, length us, event | category | flops | bytes accessed | tf_op | source)
XLA Modules:
  0.0 399.2 jit_solution(17801880543431463129)
XLA Ops:
  6.5 0.0 copy-start
  6.5 0.0 all-gather.4.cloned.1.call-start
  6.5 0.7 all-gather.4.cloned.1.call-update
  7.3 0.0 copy-start.1
  7.3 0.0 all-gather.6.cloned.1.call-start
  7.3 127.3 %all-gather.4.cloned.1.call-done = bf16[1024,4096]{1,0:T(8,128)(2,1)} async-done(((bf16[1024,512]{1,0:T(8,128)(2,1)}), bf16[1024,4096]{1,0:T(8,128)(2,1)}) %all-gather.4.cloned.1.call-update) | async-done | bytes 8388624 | tf_op jit(solution)/shard_map/all_gather | solution.py:18
  134.6 0.0 copy-done
  134.6 6.8 %convolution_convert_fusion = bf16[384,1024]{1,0:T(8,128)(2,1)} fusion(bf16[384,4096]{1,0:T(8,128)(2,1)S(1)} %copy-done, bf16[1024,4096]{1,0:T(8,128)(2,1)} %all-gather.4.cloned.1.call-done), kind=kOutput, calls=%fused_computation.10 | convolution fusion | flops 3221618688 | bytes 12320768 | tf_op jit(solution)/shard_map/dot_general | solution.py:8
  141.4 0.0 all-gather.6.cloned.1.call-update
  141.4 0.0 all-gather.8.cloned.1.call-start
  141.5 26.8 %all-gather.6.cloned.1.call-done = bf16[768,1024]{1,0:T(8,128)(2,1)} async-done(((bf16[384,1024]{1,0:T(8,128)(2,1)}), bf16[768,1024]{1,0:T(8,128)(2,1)}) %all-gather.6.cloned.1.call-update) | async-done | bytes 1572880 | tf_op jit(solution)/shard_map/all_gather | solution.py:20
  168.3 0.0 all-gather.8.cloned.1.call-update
  168.3 0.0 reduce-scatter.2.cloned.1.call-start
  169.1 0.0 copy-done.1
  169.1 46.7 %all-gather.8.cloned.1.call-done = bf16[768,4096]{1,0:T(8,128)(2,1)} async-done(((bf16[768,1024]{1,0:T(8,128)(2,1)}), bf16[768,4096]{1,0:T(8,128)(2,1)}) %all-gather.8.cloned.1.call-update) | async-done | bytes 6291472 | tf_op jit(solution)/shard_map/all_gather | solution.py:23
  215.8 8.6 %copy.6 = bf16[768,4096]{0,1:T(8,128)(2,1)} copy(bf16[768,4096]{1,0:T(8,128)(2,1)} %all-gather.8.cloned.1.call-done) | data formatting | bytes 12582912 | tf_op jit(solution)/shard_map/all_gather | solution.py:23
  224.4 13.7 %gather_fusion = bf16[2048,768]{1,0:T(8,128)(2,1)} fusion(bf16[768,4096]{0,1:T(8,128)(2,1)} %copy.6, s32[2048]{0:T(1024)S(1)} %broadcast_clamp_fusion), kind=kCustom, calls=%fused_computation | custom fusion | bytes 6299648 | tf_op jit(solution)/shard_map/jit(_take)/gather | solution.py:27
  238.1 8.6 %fusion = f32[1024,2048]{1,0:T(8,128)} fusion(bf16[2048,768]{1,0:T(8,128)(2,1)} %gather_fusion, pred[2048]{0:T(1024)(128)(4,1)S(1)} %get-tuple-element.6, pred[2048]{0:T(1024)(128)(4,1)S(1)} %get-tuple-element.5, bf16[768,1024]{1,0:T(8,128)(2,1)} %all-gather.6.cloned.1.call-done, f32[768]{0:T(1024)S(1)} %add_divide_fusion), kind=kOutput, calls=%fused_computation.1 | convolution fusion | flops 3226730496 | bytes 13114368 | tf_op jit(solution)/shard_map/dot_general | solution.py:32
  246.8 0.0 reduce-scatter.2.cloned.1.call-update
  246.8 145.9 %reduce-scatter.2.cloned.1.call-done = f32[256,2048]{1,0:T(8,128)} async-done(((f32[1024,2048]{1,0:T(8,128)}), f32[256,2048]{1,0:T(8,128)}) %reduce-scatter.2.cloned.1.call-update) | async-done | bytes 2097168 | tf_op jit(solution)/shard_map/reduce_scatter | solution.py:31
  (4 shorter events, 0.1 us)
Async XLA Ops:
  6.5 128.0 %copy-start = (bf16[384,4096]{1,0:T(8,128)(2,1)S(1)}, bf16[384,4096]{1,0:T(8,128)(2,1)}, u32[]{:S(2)}) copy-start(bf16[384,4096]{1,0:T(8,128)(2,1)} %param.4) | copy-start | bytes 9437188
  6.5 128.0 %all-gather.4.cloned.1.call-start = ((), (), s32[]{:S(2)}) async-start(), calls=%async_computation.1 | async-start | bytes 9437184 | tf_op jit(solution)/shard_map/all_gather | solution.py:18
  7.3 161.8 %copy-start.1 = (f32[768]{0:T(1024)S(1)}, f32[768]{0:T(1024)}, u32[]{:S(2)}) copy-start(f32[768]{0:T(1024)} %param.6) | copy-start | bytes 9220
  7.3 161.0 %all-gather.6.cloned.1.call-start = ((), (), s32[]{:S(2)}) async-start(), calls=%async_computation.2 | async-start | bytes 2359296 | tf_op jit(solution)/shard_map/all_gather | solution.py:20
  141.4 74.3 %all-gather.8.cloned.1.call-start = ((), (), s32[]{:S(2)}) async-start(), calls=%async_computation.3 | async-start | bytes 7864320 | tf_op jit(solution)/shard_map/all_gather | solution.py:23
  168.3 224.4 %reduce-scatter.2.cloned.1.call-start = ((), (), s32[]{:S(2)}) async-start(), calls=%async_computation.4 | async-start | bytes 10485760 | tf_op jit(solution)/shard_map/reduce_scatter | solution.py:31
Sparse Core Ops, SparseCore 0:
  9.4 125.1 all-gather.3
  141.6 26.6 all-gather.5
  169.8 45.8 all-gather.7
  246.9 145.7 reduce-scatter.1
where the time goes:
time: 400 us; the launch traced here: 399 us
  waiting for transfers between devices  347 us (87%)
  local copies, waits for them, and re-layouts  22.4 us (6%)
  matrix products  15.5 us (4%)
  between operations  13.8 us (3%)
    reduce_scatter x1, waiting for transfers between devices, on_device(): lax.psum_scatter(lax.dot_general(scaled, col_b, (((0,), (0,)), ((), ())),...  146 us
    all_gather x1, waiting for transfers between devices, on_device(): lax.all_gather(inverse_factor, ('pair', 'col'), axis=1, tiled=True)  127 us
    all_gather x1, waiting for transfers between devices, on_device(): portion = lax.all_gather(group_b, 'row', axis=1, tiled=True)  46.7 us
    all_gather x1, waiting for transfers between devices, on_device(): lax.all_gather(local_rows.astype(jnp.bfloat16), 'col', axis=0, tiled=True)  26.8 us
    gather x1, local copies, waits for them, and re-layouts, on_device(): selected = jnp.take(portion, jnp.clip(wanted, 0, portion_width - 1), axis=1)  13.7 us
    all_gather x1, local copies, waits for them, and re-layouts, on_device(): portion = lax.all_gather(group_b, 'row', axis=1, tiled=True)  8.64 us
    dot_general x1, matrix products, on_device(): lax.dot_general(scaled, col_b, (((0,), (0,)), ((), ())), preferred_elemen...  8.63 us
  transfers between devices with their start and end apart: 4, of which 4 were waited for; matrix products, arithmetic and copies ran while one was open for 0% of the time, Pallas kernels for 0%

commit v1 on v0

v1 whole, which is shorter than its diff:
```python
import jax
import jax.numpy as jnp
from jax import lax
from jax.sharding import PartitionSpec as P

AXES = ("pair", "row", "col")
BF16 = jnp.bfloat16
F32 = jnp.float32


def rows_by_rows(a, b):
    return lax.dot_general(a, b, (((1,), (1,)), ((), ())), preferred_element_type=F32)


def columns_by_columns(a, b):
    return lax.dot_general(a, b, (((0,), (0,)), ((), ())), preferred_element_type=F32)


def scale_of(energies, frequency):
    return 2.0 * energies / (energies * energies + frequency[0] * frequency[0])


def any_mesh(integrals, inverse_factor, energies, frequency):
    n_col = lax.axis_size("col")
    q_cols = integrals.shape[1] // n_col
    local_rows = rows_by_rows(
        integrals, lax.all_gather(inverse_factor, ("pair", "col"), axis=1, tiled=True)
    )
    group_b = lax.all_gather(local_rows.astype(BF16), "col", axis=0, tiled=True)
    portion = lax.all_gather(group_b, "row", axis=1, tiled=True)
    col_b = lax.dynamic_slice_in_dim(
        portion, lax.axis_index("col") * q_cols, q_cols, axis=1
    )
    factor = scale_of(energies, frequency)
    scaled = (factor[:, None] * group_b.astype(F32)).astype(BF16)
    return lax.psum_scatter(
        columns_by_columns(scaled, col_b), "pair", scatter_dimension=0, tiled=True
    )


def route(target):
    def index(z, x, k, y):
        return ((z * 2 + x) * 2 + k) * 2 + y

    pairs = []
    for z in range(4):
        for x in range(2):
            for k in range(2):
                for y in range(2):
                    to = target(z, x, k, y)
                    if to is not None:
                        pairs.append((index(z, x, k, y), index(*to)))
    return pairs


def send(value, pairs):
    return lax.ppermute(value, AXES, pairs)


OVER_X = route(lambda z, x, k, y: (z, 1 - x, k, y))
OVER_Y = route(lambda z, x, k, y: (z, x, k, 1 - y))
OVER_XY = route(lambda z, x, k, y: (z, 1 - x, k, 1 - y))
OVER_CORE = route(lambda z, x, k, y: (z, x, 1 - k, y))


def along_z(step, allowed):
    def target(z, x, k, y):
        if 0 <= z + step < 4 and allowed(z, k):
            return (z + step, x, k, y)
        return None

    return route(target)


def four_planes(integrals, inverse_factor, energies, frequency):
    z = lax.axis_index("pair")
    row = lax.axis_index("row")
    x, k = row // 2, row % 2
    y = lax.axis_index("col")
    chip = 2 * x + y
    mine = integrals
    n_rows, width = inverse_factor.shape
    piece = n_rows // 4

    half = mine.shape[0] // 2
    from_y = send(lax.dynamic_slice_in_dim(mine, k * half, half, 0), OVER_Y)
    from_core = send(from_y, OVER_CORE)
    theirs = jnp.concatenate(
        [jnp.where(k == 0, from_y, from_core), jnp.where(k == 0, from_core, from_y)], 0
    )

    def quarter(c):
        return lax.dynamic_slice_in_dim(inverse_factor, c * piece, piece, 0)

    own = quarter(chip)
    got_y = send(quarter(chip ^ 1), OVER_Y)
    got_x = send(quarter(chip ^ 2), OVER_X)
    got_xy = send(quarter(chip ^ 3), OVER_XY)

    def by_y(a, b):
        return jnp.concatenate([jnp.where(y == 0, a, b), jnp.where(y == 0, b, a)], 1)

    same, other = by_y(own, got_y), by_y(got_x, got_xy)
    parts = [jnp.where(x == 0, same, other), jnp.where(x == 0, other, same)]

    def term(values, plane):
        at = jnp.clip(plane, 0, 3) * 2 * width
        return [
            rows_by_rows(lax.dynamic_slice_in_dim(a, at, 2 * width, 1), values)
            for a in (mine, theirs)
        ]

    totals = [term(parts[p], z) for p in range(2)]
    moving = [[parts[p], parts[p]] for p in range(2)]
    for step in range(1, 4):
        for d in (0, 1):
            sign = 1 - 2 * d
            for p in range(2):

                def allowed(at, core):
                    source = at - sign * (step - 1)
                    return 0 <= source < 4 and source <= 2 * p + core

                pairs = along_z(sign, allowed)
                if not pairs:
                    continue
                moving[p][d] = send(moving[p][d], pairs)
                more = term(moving[p][d], z - sign * step)
                totals[p] = [t + m for t, m in zip(totals[p], more)]

    def ordered(a, b):
        a, b = a.astype(BF16), b.astype(BF16)
        return jnp.concatenate([jnp.where(y == 0, a, b), jnp.where(y == 0, b, a)], 0)

    low, high = ordered(*totals[0]), ordered(*totals[1])

    low_y, high_y = send(low, OVER_Y), send(high, OVER_Y)
    low_x, high_x = send(low, OVER_X), send(high, OVER_X)
    low_xy, high_xy = send(low_y, OVER_X), send(high_x, OVER_Y)
    lows = [low, low_y, low_x, low_xy]
    highs = [high, high_y, high_x, high_xy]
    row_parts = [jnp.where(x == 0, a, b) for a, b in zip(lows, highs)]
    col_parts = [jnp.where(y == 0, a, b) for a, b in zip(lows, highs)]
    columns = jnp.concatenate(col_parts, 1)
    core_columns = send(columns, OVER_CORE)

    factor = scale_of(energies, frequency)
    rows = jnp.concatenate(row_parts, 1)
    scaled = (factor[:, None] * rows.astype(F32)).astype(BF16)

    def block(plane, cols):
        at = (plane ^ chip) * piece
        return columns_by_columns(lax.dynamic_slice_in_dim(scaled, at, piece, 1), cols)

    def to_right(hop):
        return along_z(1, lambda at, core: at < hop)

    def to_left(hop):
        return along_z(-1, lambda at, core: at > 3 - hop)

    def summed(cols):
        far = block(z ^ 3, cols)
        right = send(far.astype(BF16), to_right(1))
        left = send(far.astype(BF16), to_left(1))
        next_far = block(z ^ 2, cols)
        right = send((next_far + right.astype(F32)).astype(BF16), to_right(2))
        left = send((next_far + left.astype(F32)).astype(BF16), to_left(2))
        near = block(z ^ 1, cols)
        right = (jnp.where(z == 1, far, near) + right.astype(F32)).astype(BF16)
        left = (jnp.where(z == 2, far, near) + left.astype(F32)).astype(BF16)
        right, left = send(right, to_right(3)), send(left, to_left(3))
        return block(z, cols) + right.astype(F32) + left.astype(F32)

    sums = jnp.stack([summed(columns), summed(core_columns)])
    out = [
        lax.dynamic_slice(
            sums, (c ^ k, 0, (q ^ chip) * piece), (1, piece, piece)
        ).reshape(piece, piece)
        for c in range(2)
        for q in range(4)
    ]
    return jnp.concatenate(out, 1)


def solution(mesh):
    planes = tuple(mesh.shape[a] for a in AXES) == (4, 4, 2)
    return jax.shard_map(
        four_planes if planes else any_mesh,
        mesh=mesh,
        in_specs=(P(("pair", "col"), None), P("row", ("pair", "col")), P("pair"), P()),
        out_specs=P(("row", "pair"), "col"),
        check_vma=False,
    )
```

time: 400 us -> 204 us (0.51)
  waiting for transfers between devices: 347 us -> 79.6 us
  starting transfers between devices: 0.12 us -> 62.2 us
  matrix products: 15.5 us -> 38.5 us
  local copies, waits for them, and re-layouts: 22.4 us -> 3.81 us
  other arithmetic: 0.06 us -> 16.3 us
  between operations: 13.8 us -> 1.49 us
    all_gather x3 -> x0, waiting for transfers between devices: 201 us -> none  [the longest x1 127 us: on_device(): lax.all_gather(inverse_factor, ('pair', 'col'), axis=1, tiled=True)]
    reduce_scatter x1 -> x0, waiting for transfers between devices: 146 us -> none  [on_device(): lax.psum_scatter(lax.dot_general(scaled, col_b, (((0,), (0,)), ((), ())),...]
    ppermute x0 -> x34, waiting for transfers between devices: none -> 79.6 us  [send(): return lax.ppermute(value, AXES, pairs)]
    ppermute x0 -> x34, starting transfers between devices: none -> 62.2 us  [send(): return lax.ppermute(value, AXES, pairs)]
    dot_general x2 -> x32, matrix products: 15.5 us -> 38.5 us  [the longest x8 20.3 us: columns_by_columns(): lax.dot_general(a, b, (((0,), (0,)), ((), ())), preferred_element_type=F32)]
    gather x1 -> x0, local copies, waits for them, and re-layouts: 13.7 us -> none  [on_device(): selected = jnp.take(portion, jnp.clip(wanted, 0, portion_width - 1), axis=1)]
    select_n x1 -> x8, other arithmetic: 0.03 us -> 10.3 us  [the longest x4 3.38 us: four_planes(): col_parts = [jnp.where(y == 0, a, b) for a, b in zip(lows, highs)]]
    all_gather x1 -> x0, local copies, waits for them, and re-layouts: 8.64 us -> none  [on_device(): portion = lax.all_gather(group_b, 'row', axis=1, tiled=True)]
  transfers between devices with their start and end apart: 4 -> 34, of which waited for: 4 -> 18; matrix products, arithmetic and copies ran while one was open for 0% -> 23% of each run, Pallas kernels for 0% -> 0%
where the time goes in v1:
time: 204 us; the launch traced here: 202 us
  waiting for transfers between devices  79.6 us (39%)
  starting transfers between devices  62.2 us (30%)
  matrix products  38.5 us (19%)
  other arithmetic  16.3 us (8%)
  local copies, waits for them, and re-layouts  3.81 us (2%)
    ppermute x34, waiting for transfers between devices, send(): return lax.ppermute(value, AXES, pairs)  79.6 us
    ppermute x34, starting transfers between devices, send(): return lax.ppermute(value, AXES, pairs)  62.2 us
    dot_general x8, matrix products, columns_by_columns(): lax.dot_general(a, b, (((0,), (0,)), ((), ())), preferred_element_type=F32)  20.3 us
    dot_general x24, matrix products, rows_by_rows(): lax.dot_general(a, b, (((1,), (1,)), ((), ())), preferred_element_type=F32)  18.2 us
  transfers between devices with their start and end apart: 34, of which 18 were waited for; matrix products, arithmetic and copies ran while one was open for 23% of the time, Pallas kernels for 0%

profile of v1, /device:TPU:19, one launch (start us, length us, event | category | flops | bytes accessed | tf_op | source)
XLA Modules:
  0.0 201.9 jit_solution(2197706116384132413)
XLA Ops:
  2.4 6.0 %collective-permute-done = bf16[256,512]{1,0:T(8,128)(2,1)} collective-permute-done((bf16[256,512]{1,0:T(8,128)(2,1)S(1)}, bf16[256,512]{1,0:T(8,128)(2,1)}, u32[]{:S(2)}, u32[]{:S(2)}) %collective-permute-start) | collective-permute-done | bytes 262176 | tf_op jit(solution)/shard_map/ppermute | solution.py:57
  17.1 6.6 %collective-permute-done.2 = bf16[256,512]{1,0:T(8,128)(2,1)} collective-permute-done((bf16[256,512]{1,0:T(8,128)(2,1)}, bf16[256,512]{1,0:T(8,128)(2,1)}, u32[]{:S(2)}, u32[]{:S(2)}) %collective-permute-start.2) | collective-permute-done | bytes 262176 | tf_op jit(solution)/shard_map/ppermute | solution.py:57
  28.3 3.4 %collective-permute-start.9 = (bf16[256,1024]{1,0:T(8,128)(2,1)}, bf16[256,1024]{1,0:T(8,128)(2,1)}, u32[]{:S(2)}, u32[]{:S(2)}) collective-permute-start(bf16[256,1024]{1,0:T(8,128)(2,1)} %get-tuple-element.19), channel_id=1, source_target_pairs={{0,8},{1,9},{2,10},{3,11},{4,12},{5,13},{6,14},{7,15},{8,16},{9,17... | collective-permute-start | bytes 1572872 | tf_op jit(solution)/shard_map/ppermute | solution.py:57
  32.4 6.0 %collective-permute-start.10 = (bf16[256,1024]{1,0:T(8,128)(2,1)}, bf16[256,1024]{1,0:T(8,128)(2,1)S(1)}, u32[]{:S(2)}, u32[]{:S(2)}) collective-permute-start(bf16[256,1024]{1,0:T(8,128)(2,1)} %get-tuple-element.19), channel_id=1, source_target_pairs={{8,0},{9,1},{10,2},{11,3},{12,4},{13,5},{14,6},{15,7},{16,8},{17,9... | collective-permute-start | bytes 1572872 | tf_op jit(solution)/shard_map/ppermute | solution.py:57
  43.5 5.3 %collective-permute-done.9 = bf16[256,1024]{1,0:T(8,128)(2,1)} collective-permute-done((bf16[256,1024]{1,0:T(8,128)(2,1)}, bf16[256,1024]{1,0:T(8,128)(2,1)}, u32[]{:S(2)}, u32[]{:S(2)}) %collective-permute-start.9) | collective-permute-done | bytes 524320 | tf_op jit(solution)/shard_map/ppermute | solution.py:57
  52.2 4.1 %collective-permute-start.12 = (bf16[256,1024]{1,0:T(8,128)(2,1)S(1)}, bf16[256,1024]{1,0:T(8,128)(2,1)S(1)}, u32[]{:S(2)}, u32[]{:S(2)}) collective-permute-start(bf16[256,1024]{1,0:T(8,128)(2,1)S(1)} %collective-permute-done.10), channel_id=1, source_target_pairs={{8,0},{9,1},{10,2},{11,3},{12,4},{13,5},{14,6},{15,7},{18,10},{19,... | collective-permute-start | bytes 1572872 | tf_op jit(solution)/shard_map/ppermute | solution.py:57
  59.3 3.2 %collective-permute-start.6 = (bf16[256,1024]{1,0:T(8,128)(2,1)S(1)}, bf16[256,1024]{1,0:T(8,128)(2,1)S(1)}, u32[]{:S(2)}, u32[]{:S(2)}) collective-permute-start(bf16[256,1024]{1,0:T(8,128)(2,1)S(1)} %collective-permute-done.5), channel_id=1, source_target_pairs={{16,24},{17,25},{18,26},{19,27},{20,28},{21,29},{22,30},{23,31}} | collective-permute-start | bytes 1572872 | tf_op jit(solution)/shard_map/ppermute | solution.py:57
  63.3 6.8 %collective-permute-done.11 = bf16[256,1024]{1,0:T(8,128)(2,1)S(1)} collective-permute-done((bf16[256,1024]{1,0:T(8,128)(2,1)}, bf16[256,1024]{1,0:T(8,128)(2,1)S(1)}, u32[]{:S(2)}, u32[]{:S(2)}) %collective-permute-start.11) | collective-permute-done | bytes 524320 | tf_op jit(solution)/shard_map/ppermute | solution.py:57
  91.0 7.0 %collective-permute-done.15 = bf16[768,256]{1,0:T(8,128)(2,1)S(1)} collective-permute-done((bf16[768,256]{1,0:T(8,128)(2,1)S(1)}, bf16[768,256]{1,0:T(8,128)(2,1)S(1)}, u32[]{:S(2)}, u32[]{:S(2)}) %collective-permute-start.15) | collective-permute-done | bytes 393248 | tf_op jit(solution)/shard_map/ppermute | solution.py:57
  99.2 7.3 %collective-permute-done.16 = bf16[768,256]{1,0:T(8,128)(2,1)S(1)} collective-permute-done((bf16[768,256]{1,0:T(8,128)(2,1)S(1)}, bf16[768,256]{1,0:T(8,128)(2,1)S(1)}, u32[]{:S(2)}, u32[]{:S(2)}) %collective-permute-start.16) | collective-permute-done | bytes 393248 | tf_op jit(solution)/shard_map/ppermute | solution.py:57
  108.1 6.8 %collective-permute-done.19 = bf16[768,256]{1,0:T(8,128)(2,1)S(1)} collective-permute-done((bf16[768,256]{1,0:T(8,128)(2,1)S(1)}, bf16[768,256]{1,0:T(8,128)(2,1)S(1)}, u32[]{:S(2)}, u32[]{:S(2)}) %collective-permute-start.19) | collective-permute-done | bytes 393248 | tf_op jit(solution)/shard_map/ppermute | solution.py:57
  126.0 3.4 %fusion.110 = (bf16[256,1024]{1,0:T(8,128)(2,1)}, f32[256,1024]{1,0:T(8,128)}) fusion(bf16[768,1024]{1,0:T(8,128)(2,1)} %collective-permute-done.27, bf16[768,1024]{1,0:T(8,128)(2,1)} %copy-done.1, s32[]{:T(128)S(6)} %select_n.266), kind=kOutput, calls=%fused_computation.187 | convolution fusion | flops 402915328 | bytes 3538948 | tf_op jit(solution)/shard_map/dot_general | solution.py:16
  132.1 8.5 %collective-permute-done.24 = bf16[256,1024]{1,0:T(8,128)(2,1)} collective-permute-done((bf16[256,1024]{1,0:T(8,128)(2,1)}, bf16[256,1024]{1,0:T(8,128)(2,1)}, u32[]{:S(2)}, u32[]{:S(2)}) %collective-permute-start.24) | collective-permute-done | bytes 524320 | tf_op jit(solution)/shard_map/ppermute | solution.py:57
  140.6 3.1 %add_convert_fusion.7 = (bf16[256,1024]{1,0:T(8,128)(2,1)}, bf16[256,1024]{1,0:T(8,128)(2,1)}) fusion(bf16[256,1024]{1,0:T(8,128)(2,1)} %collective-permute-done.21, bf16[256,1024]{1,0:T(8,128)(2,1)} %collective-permute-done.24, bf16[768,256]{1,0:T(8,128)(2,1)S(1)} %copy-done.10, bf16[768,256]{1,0:T(8,128)(2,1)S(1)} %copy-done.6, ...), kind=kOutput, calls=%fused_computation.71 | convolution fusion | flops 410517504 | bytes 4063236 | tf_op jit(solution)/shard_map/dot_general | solution.py:16
  145.0 4.0 %collective-permute-start.25 = (bf16[256,1024]{1,0:T(8,128)(2,1)}, bf16[256,1024]{1,0:T(8,128)(2,1)}, u32[]{:S(2)}, u32[]{:S(2)}) collective-permute-start(bf16[256,1024]{1,0:T(8,128)(2,1)} %get-tuple-element.18), channel_id=1, source_target_pairs={{16,8},{17,9},{18,10},{19,11},{20,12},{21,13},{22,14},{23,15},{24,... | collective-permute-start | bytes 1572872 | tf_op jit(solution)/shard_map/ppermute | solution.py:57
  149.1 2.8 %collective-permute-done.31 = bf16[256,1024]{1,0:T(8,128)(2,1)} collective-permute-done((bf16[256,1024]{1,0:T(8,128)(2,1)}, bf16[256,1024]{1,0:T(8,128)(2,1)}, u32[]{:S(2)}, u32[]{:S(2)}) %collective-permute-start.31) | collective-permute-done | bytes 524320 | tf_op jit(solution)/shard_map/ppermute | solution.py:57
  155.6 4.0 %collective-permute-start.32 = (bf16[256,1024]{1,0:T(8,128)(2,1)S(1)}, bf16[256,1024]{1,0:T(8,128)(2,1)S(1)}, u32[]{:S(2)}, u32[]{:S(2)}) collective-permute-start(bf16[256,1024]{1,0:T(8,128)(2,1)S(1)} %get-tuple-element.16), channel_id=1, source_target_pairs={{16,8},{17,9},{18,10},{19,11},{20,12},{21,13},{22,14},{23,15},{24,... | collective-permute-start | bytes 1572872 | tf_op jit(solution)/shard_map/ppermute | solution.py:57
  159.6 3.5 %collective-permute-done.25 = bf16[256,1024]{1,0:T(8,128)(2,1)} collective-permute-done((bf16[256,1024]{1,0:T(8,128)(2,1)}, bf16[256,1024]{1,0:T(8,128)(2,1)}, u32[]{:S(2)}, u32[]{:S(2)}) %collective-permute-start.25) | collective-permute-done | bytes 524320 | tf_op jit(solution)/shard_map/ppermute | solution.py:57
  163.1 3.0 %add_convert_fusion.6 = (bf16[256,1024]{1,0:T(8,128)(2,1)}, bf16[256,1024]{1,0:T(8,128)(2,1)}) fusion(bf16[256,1024]{1,0:T(8,128)(2,1)} %collective-permute-done.22, f32[256,1024]{1,0:T(8,128)S(1)} %copy-done.18, pred[]{:T(512)S(6)} %eq.15, bf16[256,1024]{1,0:T(8,128)(2,1)} %collective-permute-done.25, pred[]{:T(512)S(6)} %eq.16, ...), kind=kOutput, calls=%fused_computation.70 | convolution fusion | flops 411041792 | bytes 5111814 | tf_op jit(solution)/shard_map/dot_general | solution.py:16
  168.2 3.6 %collective-permute-start.26 = (bf16[256,1024]{1,0:T(8,128)(2,1)}, bf16[256,1024]{1,0:T(8,128)(2,1)}, u32[]{:S(2)}, u32[]{:S(2)}) collective-permute-start(bf16[256,1024]{1,0:T(8,128)(2,1)} %get-tuple-element.12), channel_id=1, source_target_pairs={{8,0},{9,1},{10,2},{11,3},{12,4},{13,5},{14,6},{15,7},{16,8},{17,9... | collective-permute-start | bytes 1572872 | tf_op jit(solution)/shard_map/ppermute | solution.py:57
  177.7 3.3 %collective-permute-start.33 = (bf16[256,1024]{1,0:T(8,128)(2,1)}, bf16[256,1024]{1,0:T(8,128)(2,1)}, u32[]{:S(2)}, u32[]{:S(2)}) collective-permute-start(bf16[256,1024]{1,0:T(8,128)(2,1)} %get-tuple-element.10), channel_id=1, source_target_pairs={{8,0},{9,1},{10,2},{11,3},{12,4},{13,5},{14,6},{15,7},{16,8},{17,9... | collective-permute-start | bytes 1572872 | tf_op jit(solution)/shard_map/ppermute | solution.py:57
  181.1 4.5 %collective-permute-done.26 = bf16[256,1024]{1,0:T(8,128)(2,1)} collective-permute-done((bf16[256,1024]{1,0:T(8,128)(2,1)}, bf16[256,1024]{1,0:T(8,128)(2,1)}, u32[]{:S(2)}, u32[]{:S(2)}) %collective-permute-start.26) | collective-permute-done | bytes 524320 | tf_op jit(solution)/shard_map/ppermute | solution.py:57
  187.9 4.3 %collective-permute-done.30 = bf16[256,1024]{1,0:T(8,128)(2,1)} collective-permute-done((bf16[256,1024]{1,0:T(8,128)(2,1)}, bf16[256,1024]{1,0:T(8,128)(2,1)}, u32[]{:S(2)}, u32[]{:S(2)}) %collective-permute-start.30) | collective-permute-done | bytes 524320 | tf_op jit(solution)/shard_map/ppermute | solution.py:57
  192.2 4.6 %collective-permute-done.33 = bf16[256,1024]{1,0:T(8,128)(2,1)} collective-permute-done((bf16[256,1024]{1,0:T(8,128)(2,1)}, bf16[256,1024]{1,0:T(8,128)(2,1)}, u32[]{:S(2)}, u32[]{:S(2)}) %collective-permute-start.33) | collective-permute-done | bytes 524320 | tf_op jit(solution)/shard_map/ppermute | solution.py:57
  (137 shorter events, 85.4 us)
Async XLA Ops:
  14.3 42.0 %collective-permute-start.7 = (bf16[192,4096]{1,0:T(8,128)(2,1)}, bf16[192,4096]{1,0:T(8,128)(2,1)}, u32[]{:S(2)}, u32[]{:S(2)}) collective-permute-start(bf16[192,4096]{1,0:T(8,128)(2,1)} %constant_dynamic-slice_fusion), channel_id=1, source_target_pairs={{0,1},{1,0},{2,3},{3,2},{4,5},{5,4},{6,7},{7,6},{8,9},{9,8},{10,11... | collective-permute-start | bytes 4718600 | tf_op jit(solution)/shard_map/ppermute | solution.py:57
  28.3 20.5 %collective-permute-start.9 = (bf16[256,1024]{1,0:T(8,128)(2,1)}, bf16[256,1024]{1,0:T(8,128)(2,1)}, u32[]{:S(2)}, u32[]{:S(2)}) collective-permute-start(bf16[256,1024]{1,0:T(8,128)(2,1)} %get-tuple-element.19), channel_id=1, source_target_pairs={{0,8},{1,9},{2,10},{3,11},{4,12},{5,13},{6,14},{7,15},{8,16},{9,17... | collective-permute-start | bytes 1572872 | tf_op jit(solution)/shard_map/ppermute | solution.py:57
  31.7 27.2 %collective-permute-start.4 = (bf16[256,1024]{1,0:T(8,128)(2,1)}, bf16[256,1024]{1,0:T(8,128)(2,1)S(1)}, u32[]{:S(2)}, u32[]{:S(2)}) collective-permute-start(bf16[256,1024]{1,0:T(8,128)(2,1)} %get-tuple-element.20), channel_id=1, source_target_pairs={{10,2},{11,3},{14,6},{15,7}} | collective-permute-start | bytes 1572872 | tf_op jit(solution)/shard_map/ppermute | solution.py:57
  32.4 19.7 %collective-permute-start.10 = (bf16[256,1024]{1,0:T(8,128)(2,1)}, bf16[256,1024]{1,0:T(8,128)(2,1)S(1)}, u32[]{:S(2)}, u32[]{:S(2)}) collective-permute-start(bf16[256,1024]{1,0:T(8,128)(2,1)} %get-tuple-element.19), channel_id=1, source_target_pairs={{8,0},{9,1},{10,2},{11,3},{12,4},{13,5},{14,6},{15,7},{16,8},{17,9... | collective-permute-start | bytes 1572872 | tf_op jit(solution)/shard_map/ppermute | solution.py:57
  38.6 20.7 %collective-permute-start.5 = (bf16[256,1024]{1,0:T(8,128)(2,1)}, bf16[256,1024]{1,0:T(8,128)(2,1)S(1)}, u32[]{:S(2)}, u32[]{:S(2)}) collective-permute-start(bf16[256,1024]{1,0:T(8,128)(2,1)} %collective-permute-done.3), channel_id=1, source_target_pairs={{8,16},{9,17},{10,18},{11,19},{12,20},{13,21},{14,22},{15,23},{18,... | collective-permute-start | bytes 1572872 | tf_op jit(solution)/shard_map/ppermute | solution.py:57
  50.2 19.8 %collective-permute-start.11 = (bf16[256,1024]{1,0:T(8,128)(2,1)}, bf16[256,1024]{1,0:T(8,128)(2,1)S(1)}, u32[]{:S(2)}, u32[]{:S(2)}) collective-permute-start(bf16[256,1024]{1,0:T(8,128)(2,1)} %collective-permute-done.9), channel_id=1, source_target_pairs={{8,16},{9,17},{10,18},{11,19},{12,20},{13,21},{14,22},{15,23},{16,... | collective-permute-start | bytes 1572872 | tf_op jit(solution)/shard_map/ppermute | solution.py:57
  56.2 17.0 %collective-permute-start.8 = (bf16[192,4096]{1,0:T(8,128)(2,1)}, bf16[192,4096]{1,0:T(8,128)(2,1)S(1)}, u32[]{:S(2)}, u32[]{:S(2)}) collective-permute-start(bf16[192,4096]{1,0:T(8,128)(2,1)} %collective-permute-done.7), channel_id=1, source_target_pairs={{0,2},{1,3},{2,0},{3,1},{4,6},{5,7},{6,4},{7,5},{8,10},{9,11},{10,... | collective-permute-start | bytes 4718600 | tf_op jit(solution)/shard_map/ppermute | solution.py:57
  59.3 23.6 %collective-permute-start.6 = (bf16[256,1024]{1,0:T(8,128)(2,1)S(1)}, bf16[256,1024]{1,0:T(8,128)(2,1)S(1)}, u32[]{:S(2)}, u32[]{:S(2)}) collective-permute-start(bf16[256,1024]{1,0:T(8,128)(2,1)S(1)} %collective-permute-done.5), channel_id=1, source_target_pairs={{16,24},{17,25},{18,26},{19,27},{20,28},{21,29},{22,30},{23,31}} | collective-permute-start | bytes 1572872 | tf_op jit(solution)/shard_map/ppermute | solution.py:57
  70.1 16.2 %collective-permute-start.13 = (bf16[256,1024]{1,0:T(8,128)(2,1)S(1)}, bf16[256,1024]{1,0:T(8,128)(2,1)S(1)}, u32[]{:S(2)}, u32[]{:S(2)}) collective-permute-start(bf16[256,1024]{1,0:T(8,128)(2,1)S(1)} %collective-permute-done.11), channel_id=1, source_target_pairs={{16,24},{17,25},{18,26},{19,27},{20,28},{21,29},{22,30},{23,31}} | collective-permute-start | bytes 1572872 | tf_op jit(solution)/shard_map/ppermute | solution.py:57
  88.5 17.9 %collective-permute-start.16 = (bf16[768,256]{1,0:T(8,128)(2,1)S(1)}, bf16[768,256]{1,0:T(8,128)(2,1)S(1)}, u32[]{:S(2)}, u32[]{:S(2)}) collective-permute-start(bf16[768,256]{1,0:T(8,128)(2,1)S(1)} %get-tuple-element.34), channel_id=1, source_target_pairs={{0,1},{1,0},{2,3},{3,2},{4,5},{5,4},{6,7},{7,6},{8,9},{9,8},{10,11... | collective-permute-start | bytes 1179656 | tf_op jit(solution)/shard_map/ppermute | solution.py:57
  89.8 17.5 %collective-permute-start.17 = (bf16[768,256]{1,0:T(8,128)(2,1)S(1)}, bf16[768,256]{1,0:T(8,128)(2,1)S(1)}, u32[]{:S(2)}, u32[]{:S(2)}) collective-permute-start(bf16[768,256]{1,0:T(8,128)(2,1)S(1)} %get-tuple-element.33), channel_id=1, source_target_pairs={{0,4},{1,5},{2,6},{3,7},{4,0},{5,1},{6,2},{7,3},{8,12},{9,13},{10,... | collective-permute-start | bytes 1179656 | tf_op jit(solution)/shard_map/ppermute | solution.py:57
  98.0 16.8 %collective-permute-start.19 = (bf16[768,256]{1,0:T(8,128)(2,1)S(1)}, bf16[768,256]{1,0:T(8,128)(2,1)S(1)}, u32[]{:S(2)}, u32[]{:S(2)}) collective-permute-start(bf16[768,256]{1,0:T(8,128)(2,1)S(1)} %collective-permute-done.15), channel_id=1, source_target_pairs={{0,4},{1,5},{2,6},{3,7},{4,0},{5,1},{6,2},{7,3},{8,12},{9,13},{10,... | collective-permute-start | bytes 1179656 | tf_op jit(solution)/shard_map/ppermute | solution.py:57
  98.3 16.6 %collective-permute-start.20 = (bf16[768,256]{1,0:T(8,128)(2,1)S(1)}, bf16[768,256]{1,0:T(8,128)(2,1)S(1)}, u32[]{:S(2)}, u32[]{:S(2)}) collective-permute-start(bf16[768,256]{1,0:T(8,128)(2,1)S(1)} %collective-permute-done.18), channel_id=1, source_target_pairs={{0,1},{1,0},{2,3},{3,2},{4,5},{5,4},{6,7},{7,6},{8,9},{9,8},{10,11... | collective-permute-start | bytes 1179656 | tf_op jit(solution)/shard_map/ppermute | solution.py:57
  124.6 16.0 %collective-permute-start.24 = (bf16[256,1024]{1,0:T(8,128)(2,1)}, bf16[256,1024]{1,0:T(8,128)(2,1)}, u32[]{:S(2)}, u32[]{:S(2)}) collective-permute-start(bf16[256,1024]{1,0:T(8,128)(2,1)} %get-tuple-element.39), channel_id=1, source_target_pairs={{24,16},{25,17},{26,18},{27,19},{28,20},{29,21},{30,22},{31,23}} | collective-permute-start | bytes 1572872 | tf_op jit(solution)/shard_map/ppermute | solution.py:57
  129.4 19.7 %collective-permute-start.28 = (bf16[256,1024]{1,0:T(8,128)(2,1)}, bf16[256,1024]{1,0:T(8,128)(2,1)}, u32[]{:S(2)}, u32[]{:S(2)}) collective-permute-start(bf16[256,1024]{1,0:T(8,128)(2,1)} %get-tuple-element.41), channel_id=1, source_target_pairs={{0,8},{1,9},{2,10},{3,11},{4,12},{5,13},{6,14},{7,15}} | collective-permute-start | bytes 1572872 | tf_op jit(solution)/shard_map/ppermute | solution.py:57
  130.8 21.1 %collective-permute-start.31 = (bf16[256,1024]{1,0:T(8,128)(2,1)}, bf16[256,1024]{1,0:T(8,128)(2,1)}, u32[]{:S(2)}, u32[]{:S(2)}) collective-permute-start(bf16[256,1024]{1,0:T(8,128)(2,1)} %get-tuple-element.41), channel_id=1, source_target_pairs={{24,16},{25,17},{26,18},{27,19},{28,20},{29,21},{30,22},{31,23}} | collective-permute-start | bytes 1572872 | tf_op jit(solution)/shard_map/ppermute | solution.py:57
  143.7 15.9 %collective-permute-start.22 = (bf16[256,1024]{1,0:T(8,128)(2,1)}, bf16[256,1024]{1,0:T(8,128)(2,1)}, u32[]{:S(2)}, u32[]{:S(2)}) collective-permute-start(bf16[256,1024]{1,0:T(8,128)(2,1)} %get-tuple-element.17), channel_id=1, source_target_pairs={{0,8},{1,9},{2,10},{3,11},{4,12},{5,13},{6,14},{7,15},{8,16},{9,17... | collective-permute-start | bytes 1572872 | tf_op jit(solution)/shard_map/ppermute | solution.py:57
  145.0 18.1 %collective-permute-start.25 = (bf16[256,1024]{1,0:T(8,128)(2,1)}, bf16[256,1024]{1,0:T(8,128)(2,1)}, u32[]{:S(2)}, u32[]{:S(2)}) collective-permute-start(bf16[256,1024]{1,0:T(8,128)(2,1)} %get-tuple-element.18), channel_id=1, source_target_pairs={{16,8},{17,9},{18,10},{19,11},{20,12},{21,13},{22,14},{23,15},{24,... | collective-permute-start | bytes 1572872 | tf_op jit(solution)/shard_map/ppermute | solution.py:57
  154.3 19.4 %collective-permute-start.29 = (bf16[256,1024]{1,0:T(8,128)(2,1)S(1)}, bf16[256,1024]{1,0:T(8,128)(2,1)S(1)}, u32[]{:S(2)}, u32[]{:S(2)}) collective-permute-start(bf16[256,1024]{1,0:T(8,128)(2,1)S(1)} %get-tuple-element.15), channel_id=1, source_target_pairs={{0,8},{1,9},{2,10},{3,11},{4,12},{5,13},{6,14},{7,15},{8,16},{9,17... | collective-permute-start | bytes 1572872 | tf_op jit(solution)/shard_map/ppermute | solution.py:57
  155.6 18.7 %collective-permute-start.32 = (bf16[256,1024]{1,0:T(8,128)(2,1)S(1)}, bf16[256,1024]{1,0:T(8,128)(2,1)S(1)}, u32[]{:S(2)}, u32[]{:S(2)}) collective-permute-start(bf16[256,1024]{1,0:T(8,128)(2,1)S(1)} %get-tuple-element.16), channel_id=1, source_target_pairs={{16,8},{17,9},{18,10},{19,11},{20,12},{21,13},{22,14},{23,15},{24,... | collective-permute-start | bytes 1572872 | tf_op jit(solution)/shard_map/ppermute | solution.py:57
  166.1 14.9 %collective-permute-start.23 = (bf16[256,1024]{1,0:T(8,128)(2,1)}, bf16[256,1024]{1,0:T(8,128)(2,1)}, u32[]{:S(2)}, u32[]{:S(2)}) collective-permute-start(bf16[256,1024]{1,0:T(8,128)(2,1)} %get-tuple-element.11), channel_id=1, source_target_pairs={{0,8},{1,9},{2,10},{3,11},{4,12},{5,13},{6,14},{7,15},{8,16},{9,17... | collective-permute-start | bytes 1572872 | tf_op jit(solution)/shard_map/ppermute | solution.py:57
  168.2 17.4 %collective-permute-start.26 = (bf16[256,1024]{1,0:T(8,128)(2,1)}, bf16[256,1024]{1,0:T(8,128)(2,1)}, u32[]{:S(2)}, u32[]{:S(2)}) collective-permute-start(bf16[256,1024]{1,0:T(8,128)(2,1)} %get-tuple-element.12), channel_id=1, source_target_pairs={{8,0},{9,1},{10,2},{11,3},{12,4},{13,5},{14,6},{15,7},{16,8},{17,9... | collective-permute-start | bytes 1572872 | tf_op jit(solution)/shard_map/ppermute | solution.py:57
  175.7 16.4 %collective-permute-start.30 = (bf16[256,1024]{1,0:T(8,128)(2,1)}, bf16[256,1024]{1,0:T(8,128)(2,1)}, u32[]{:S(2)}, u32[]{:S(2)}) collective-permute-start(bf16[256,1024]{1,0:T(8,128)(2,1)} %get-tuple-element.9), channel_id=1, source_target_pairs={{0,8},{1,9},{2,10},{3,11},{4,12},{5,13},{6,14},{7,15},{8,16},{9,17... | collective-permute-start | bytes 1572872 | tf_op jit(solution)/shard_map/ppermute | solution.py:57
  177.7 19.1 %collective-permute-start.33 = (bf16[256,1024]{1,0:T(8,128)(2,1)}, bf16[256,1024]{1,0:T(8,128)(2,1)}, u32[]{:S(2)}, u32[]{:S(2)}) collective-permute-start(bf16[256,1024]{1,0:T(8,128)(2,1)} %get-tuple-element.10), channel_id=1, source_target_pairs={{8,0},{9,1},{10,2},{11,3},{12,4},{13,5},{14,6},{15,7},{16,8},{17,9... | collective-permute-start | bytes 1572872 | tf_op jit(solution)/shard_map/ppermute | solution.py:57
  (29 other events, 283.0 us)

commit v2 on v1

--- a/solution.py
+++ b/solution.py
@@ -78,36 +78,39 @@
     x, k = row // 2, row % 2
     y = lax.axis_index("col")
     chip = 2 * x + y
-    mine = integrals
     n_rows, width = inverse_factor.shape
     piece = n_rows // 4
 
-    half = mine.shape[0] // 2
-    from_y = send(lax.dynamic_slice_in_dim(mine, k * half, half, 0), OVER_Y)
+    quarters = lax.optimization_barrier(
+        [
+            lax.dynamic_slice_in_dim(inverse_factor, (chip ^ c) * piece, piece, 0)
+            for c in range(4)
+        ]
+    )
+    own = quarters[0]
+    got_y = send(quarters[1], OVER_Y)
+    got_x = send(quarters[2], OVER_X)
+    got_xy = send(quarters[3], OVER_XY)
+
+    half = integrals.shape[0] // 2
+    from_y = send(lax.dynamic_slice_in_dim(integrals, k * half, half, 0), OVER_Y)
     from_core = send(from_y, OVER_CORE)
     theirs = jnp.concatenate(
         [jnp.where(k == 0, from_y, from_core), jnp.where(k == 0, from_core, from_y)], 0
     )
-
-    def quarter(c):
-        return lax.dynamic_slice_in_dim(inverse_factor, c * piece, piece, 0)
-
-    own = quarter(chip)
-    got_y = send(quarter(chip ^ 1), OVER_Y)
-    got_x = send(quarter(chip ^ 2), OVER_X)
-    got_xy = send(quarter(chip ^ 3), OVER_XY)
-
-    def by_y(a, b):
-        return jnp.concatenate([jnp.where(y == 0, a, b), jnp.where(y == 0, b, a)], 1)
-
-    same, other = by_y(own, got_y), by_y(got_x, got_xy)
+    factors = scale_of(lax.all_gather(energies, "pair"), frequency)
+
+    def by_y(a, b, axis):
+        return jnp.concatenate([jnp.where(y == 0, a, b), jnp.where(y == 0, b, a)], axis)
+
+    same, other = by_y(own, got_y, 1), by_y(got_x, got_xy, 1)
     parts = [jnp.where(x == 0, same, other), jnp.where(x == 0, other, same)]
 
     def term(values, plane):
         at = jnp.clip(plane, 0, 3) * 2 * width
         return [
-            rows_by_rows(lax.dynamic_slice_in_dim(a, at, 2 * width, 1), values)
-            for a in (mine, theirs)
+            rows_by_rows(values, lax.dynamic_slice_in_dim(a, at, 2 * width, 1))
+            for a in (integrals, theirs)
         ]
 
     totals = [term(parts[p], z) for p in range(2)]
@@ -128,58 +131,62 @@
                 more = term(moving[p][d], z - sign * step)
                 totals[p] = [t + m for t, m in zip(totals[p], more)]
 
-    def ordered(a, b):
-        a, b = a.astype(BF16), b.astype(BF16)
-        return jnp.concatenate([jnp.where(y == 0, a, b), jnp.where(y == 0, b, a)], 0)
-
-    low, high = ordered(*totals[0]), ordered(*totals[1])
-
-    low_y, high_y = send(low, OVER_Y), send(high, OVER_Y)
-    low_x, high_x = send(low, OVER_X), send(high, OVER_X)
-    low_xy, high_xy = send(low_y, OVER_X), send(high_x, OVER_Y)
-    lows = [low, low_y, low_x, low_xy]
-    highs = [high, high_y, high_x, high_xy]
-    row_parts = [jnp.where(x == 0, a, b) for a, b in zip(lows, highs)]
-    col_parts = [jnp.where(y == 0, a, b) for a, b in zip(lows, highs)]
-    columns = jnp.concatenate(col_parts, 1)
-    core_columns = send(columns, OVER_CORE)
-
-    factor = scale_of(energies, frequency)
-    rows = jnp.concatenate(row_parts, 1)
-    scaled = (factor[:, None] * rows.astype(F32)).astype(BF16)
-
-    def block(plane, cols):
-        at = (plane ^ chip) * piece
-        return columns_by_columns(lax.dynamic_slice_in_dim(scaled, at, piece, 1), cols)
-
-    def to_right(hop):
-        return along_z(1, lambda at, core: at < hop)
-
-    def to_left(hop):
-        return along_z(-1, lambda at, core: at > 3 - hop)
-
-    def summed(cols):
-        far = block(z ^ 3, cols)
-        right = send(far.astype(BF16), to_right(1))
-        left = send(far.astype(BF16), to_left(1))
-        next_far = block(z ^ 2, cols)
-        right = send((next_far + right.astype(F32)).astype(BF16), to_right(2))
-        left = send((next_far + left.astype(F32)).astype(BF16), to_left(2))
-        near = block(z ^ 1, cols)
-        right = (jnp.where(z == 1, far, near) + right.astype(F32)).astype(BF16)
-        left = (jnp.where(z == 2, far, near) + left.astype(F32)).astype(BF16)
-        right, left = send(right, to_right(3)), send(left, to_left(3))
-        return block(z, cols) + right.astype(F32) + left.astype(F32)
-
-    sums = jnp.stack([summed(columns), summed(core_columns)])
-    out = [
-        lax.dynamic_slice(
-            sums, (c ^ k, 0, (q ^ chip) * piece), (1, piece, piece)
-        ).reshape(piece, piece)
-        for c in range(2)
-        for q in range(4)
+    low, high = [
+        by_y(totals[p][0].astype(BF16), totals[p][1].astype(BF16), 1) for p in range(2)
     ]
-    return jnp.concatenate(out, 1)
+
+    keep, give = jnp.where(y == 0, low, high), jnp.where(y == 0, high, low)
+    plane = by_y(keep, send(give, OVER_Y), 0)
+
+    def hops(step):
+        last = plane
+        for hop in range(3):
+            here = (lambda at, core: at >= hop) if step == 1 else (lambda at, core: at <= 3 - hop)
+            last = send(last, along_z(step, here))
+            yield last
+
+    right, left = list(hops(1)), list(hops(-1))
+    planes = [
+        plane,
+        jnp.where(z % 2 == 1, right[0], left[0]),
+        jnp.where(z < 2, left[1], right[1]),
+        jnp.where(
+            z < 2,
+            jnp.where(z == 0, left[2], left[0]),
+            jnp.where(z == 2, right[0], right[2]),
+        ),
+    ]
+
+    def to_rows(zz, xx, kk, yy):
+        at = zz // 2
+        if xx != at:
+            return None
+        return (zz, at, kk, 1 - at) if yy == at else (zz, 1 - at, kk, at)
+
+    blocks = [0.0] * 4
+    for i, mine in enumerate(planes):
+        beside = send(mine, OVER_X)
+        core_mine, core_beside = send(mine, OVER_CORE), send(beside, OVER_CORE)
+
+        def chunk(a):
+            return lax.dynamic_slice_in_dim(a, (z % 2) * piece, piece, 0)
+
+        there = send(chunk(mine), route(to_rows))
+        rows = jnp.where(
+            x != y, there, jnp.where(x == z // 2, chunk(mine), chunk(beside))
+        )
+        factor = lax.dynamic_slice_in_dim(factors, z ^ i, 1, 0)
+        scaled = (factor * rows.astype(F32)).astype(BF16)
+        blocks = [
+            b + rows_by_rows(scaled, columns)
+            for b, columns in zip(blocks, (mine, beside, core_mine, core_beside))
+        ]
+
+    def at(core, side):
+        by_x = [jnp.where(x == side, blocks[2 * c], blocks[2 * c + 1]) for c in (0, 1)]
+        return jnp.where(k == core, by_x[0], by_x[1])
+
+    return jnp.concatenate([at(c, s) for c in (0, 1) for s in (0, 1)], 1)
 
 
 def solution(mesh):

time: 204 us -> 247 us (1.21); the launches traced: 202 us -> 242 us
  waiting for transfers between devices: 79.6 us -> 108 us
  blocking collectives: 0 us -> 18.2 us
  matrix products: 38.5 us -> 26.2 us
  starting transfers between devices: 62.2 us -> 72.2 us
  other arithmetic: 16.3 us -> 11.5 us
    ppermute x34 -> x38, waiting for transfers between devices: 79.6 us -> 108 us  [send(): return lax.ppermute(value, AXES, pairs)]
    dot_general x8 -> x0, matrix products: 20.3 us -> none  [columns_by_columns(): lax.dot_general(a, b, (((0,), (0,)), ((), ())), preferred_element_type=F32)]
    all_gather x0 -> x1, blocking collectives: none -> 18.2 us  [four_planes(): factors = scale_of(lax.all_gather(energies, 'pair'), frequency)]
    ppermute x34 -> x38, starting transfers between devices: 62.2 us -> 72.2 us  [send(): return lax.ppermute(value, AXES, pairs)]
    dot_general x24 -> x40, matrix products: 18.2 us -> 26.2 us  [rows_by_rows(): lax.dot_general(a, b, (((1,), (1,)), ((), ())), preferred_element_type=F32)]
  transfers between devices with their start and end apart: 34 -> 38, of which waited for: 18 -> 14; matrix products, arithmetic and copies ran while one was open for 23% -> 14% of each run, Pallas kernels for 0% -> 0%
where the time goes in v2:
time: 247 us; the launch traced here: 242 us
  waiting for transfers between devices  108 us (44%)
  starting transfers between devices  72.2 us (29%)
  matrix products  26.2 us (11%)
  blocking collectives  18.2 us (7%)
  other arithmetic  11.5 us (5%)
  local copies, waits for them, and re-layouts  4.84 us (2%)
    ppermute x38, waiting for transfers between devices, send(): return lax.ppermute(value, AXES, pairs)  108 us
    ppermute x38, starting transfers between devices, send(): return lax.ppermute(value, AXES, pairs)  72.2 us
    dot_general x40, matrix products, rows_by_rows(): lax.dot_general(a, b, (((1,), (1,)), ((), ())), preferred_element_type=F32)  26.2 us
    all_gather x1, blocking collectives, four_planes(): factors = scale_of(lax.all_gather(energies, 'pair'), frequency)  18.2 us
  transfers between devices with their start and end apart: 38, of which 14 were waited for; matrix products, arithmetic and copies ran while one was open for 14% of the time, Pallas kernels for 0%

profile of v2, /device:TPU:19, one launch (start us, length us, event | category | flops | bytes accessed | tf_op | source)
XLA Modules:
  0.0 242.4 jit_solution(7184814629140000133)
XLA Ops:
  7.4 2.3 collective-permute-done.1
  9.7 6.6 %collective-permute-done.2 = bf16[256,512]{1,0:T(8,128)(2,1)} collective-permute-done((bf16[256,512]{1,0:T(8,128)(2,1)}, bf16[256,512]{1,0:T(8,128)(2,1)}, u32[]{:S(2)}, u32[]{:S(2)}) %collective-permute-start.2) | collective-permute-done | bytes 262176 | tf_op jit(solution)/shard_map/ppermute | solution.py:57
  19.7 3.2 %collective-permute-start.9 = (bf16[256,1024]{1,0:T(8,128)(2,1)}, bf16[256,1024]{1,0:T(8,128)(2,1)}, u32[]{:S(2)}, u32[]{:S(2)}) collective-permute-start(bf16[256,1024]{1,0:T(8,128)(2,1)} %get-tuple-element.30), channel_id=1, source_target_pairs={{0,8},{1,9},{2,10},{3,11},{4,12},{5,13},{6,14},{7,15},{8,16},{9,17... | collective-permute-start | bytes 1572872 | tf_op jit(solution)/shard_map/ppermute | solution.py:57
  24.2 4.0 %collective-permute-start.10 = (bf16[256,1024]{1,0:T(8,128)(2,1)}, bf16[256,1024]{1,0:T(8,128)(2,1)S(1)}, u32[]{:S(2)}, u32[]{:S(2)}) collective-permute-start(bf16[256,1024]{1,0:T(8,128)(2,1)} %get-tuple-element.30), channel_id=1, source_target_pairs={{8,0},{9,1},{10,2},{11,3},{12,4},{13,5},{14,6},{15,7},{16,8},{17,9... | collective-permute-start | bytes 1572872 | tf_op jit(solution)/shard_map/ppermute | solution.py:57
  28.9 2.7 %collective-permute-done.9 = bf16[256,1024]{1,0:T(8,128)(2,1)} collective-permute-done((bf16[256,1024]{1,0:T(8,128)(2,1)}, bf16[256,1024]{1,0:T(8,128)(2,1)}, u32[]{:S(2)}, u32[]{:S(2)}) %collective-permute-start.9) | collective-permute-done | bytes 524320 | tf_op jit(solution)/shard_map/ppermute | solution.py:57
  31.6 3.2 %collective-permute-start.11 = (bf16[256,1024]{1,0:T(8,128)(2,1)}, bf16[256,1024]{1,0:T(8,128)(2,1)S(1)}, u32[]{:S(2)}, u32[]{:S(2)}) collective-permute-start(bf16[256,1024]{1,0:T(8,128)(2,1)} %collective-permute-done.9), channel_id=1, source_target_pairs={{8,16},{9,17},{10,18},{11,19},{12,20},{13,21},{14,22},{15,23},{16,... | collective-permute-start | bytes 1572872 | tf_op jit(solution)/shard_map/ppermute | solution.py:57
  36.4 5.1 %collective-permute-done.3 = bf16[256,1024]{1,0:T(8,128)(2,1)} collective-permute-done((bf16[256,1024]{1,0:T(8,128)(2,1)}, bf16[256,1024]{1,0:T(8,128)(2,1)}, u32[]{:S(2)}, u32[]{:S(2)}) %collective-permute-start.3) | collective-permute-done | bytes 524320 | tf_op jit(solution)/shard_map/ppermute | solution.py:57
  46.4 3.4 %collective-permute-start.12 = (bf16[256,1024]{1,0:T(8,128)(2,1)S(1)}, bf16[256,1024]{1,0:T(8,128)(2,1)S(1)}, u32[]{:S(2)}, u32[]{:S(2)}) collective-permute-start(bf16[256,1024]{1,0:T(8,128)(2,1)S(1)} %collective-permute-done.10), channel_id=1, source_target_pairs={{8,0},{9,1},{10,2},{11,3},{12,4},{13,5},{14,6},{15,7},{18,10},{19,... | collective-permute-start | bytes 1572872 | tf_op jit(solution)/shard_map/ppermute | solution.py:57
  56.6 2.9 %collective-permute-start.13 = (bf16[256,1024]{1,0:T(8,128)(2,1)S(1)}, bf16[256,1024]{1,0:T(8,128)(2,1)S(1)}, u32[]{:S(2)}, u32[]{:S(2)}) collective-permute-start(bf16[256,1024]{1,0:T(8,128)(2,1)S(1)} %collective-permute-done.11), channel_id=1, source_target_pairs={{16,24},{17,25},{18,26},{19,27},{20,28},{21,29},{22,30},{23,31}} | collective-permute-start | bytes 1572872 | tf_op jit(solution)/shard_map/ppermute | solution.py:57
  72.9 9.1 %collective-permute-done.6 = bf16[256,1024]{1,0:T(8,128)(2,1)S(1)} collective-permute-done((bf16[256,1024]{1,0:T(8,128)(2,1)S(1)}, bf16[256,1024]{1,0:T(8,128)(2,1)S(1)}, u32[]{:S(2)}, u32[]{:S(2)}) %collective-permute-start.6) | collective-permute-done | bytes 524320 | tf_op jit(solution)/shard_map/ppermute | solution.py:57
  84.9 9.7 %collective-permute-done.15 = bf16[256,768]{1,0:T(8,128)(2,1)S(1)} collective-permute-done((bf16[256,768]{1,0:T(8,128)(2,1)S(1)}, bf16[256,768]{1,0:T(8,128)(2,1)S(1)}, u32[]{:S(2)}, u32[]{:S(2)}) %collective-permute-start.15) | collective-permute-done | bytes 393248 | tf_op jit(solution)/shard_map/ppermute | solution.py:57
  95.6 4.1 %collective-permute-start.18 = (bf16[512,768]{1,0:T(8,128)(2,1)}, bf16[512,768]{1,0:T(8,128)(2,1)S(1)}, u32[]{:S(2)}, u32[]{:S(2)}) collective-permute-start(bf16[512,768]{1,0:T(8,128)(2,1)} %pad_maximum_fusion.1), channel_id=1, source_target_pairs={{0,8},{1,9},{2,10},{3,11},{4,12},{5,13},{6,14},{7,15},{8,16},{9,17... | collective-permute-start | bytes 2359304 | tf_op jit(solution)/shard_map/ppermute | solution.py:57
  101.9 13.3 %collective-permute-done.18 = bf16[512,768]{1,0:T(8,128)(2,1)S(1)} collective-permute-done((bf16[512,768]{1,0:T(8,128)(2,1)}, bf16[512,768]{1,0:T(8,128)(2,1)S(1)}, u32[]{:S(2)}, u32[]{:S(2)}) %collective-permute-start.18) | collective-permute-done | bytes 786464 | tf_op jit(solution)/shard_map/ppermute | solution.py:57
  115.2 4.0 %collective-permute-start.23 = (bf16[512,768]{1,0:T(8,128)(2,1)S(1)}, bf16[512,768]{1,0:T(8,128)(2,1)}, u32[]{:S(2)}, u32[]{:S(2)}) collective-permute-start(bf16[512,768]{1,0:T(8,128)(2,1)S(1)} %collective-permute-done.18), channel_id=1, source_target_pairs={{8,16},{9,17},{10,18},{11,19},{12,20},{13,21},{14,22},{15,23},{16,... | collective-permute-start | bytes 2359304 | tf_op jit(solution)/shard_map/ppermute | solution.py:57
  119.2 3.0 %collective-permute-start.22 = (bf16[512,768]{1,0:T(8,128)(2,1)}, bf16[512,768]{1,0:T(8,128)(2,1)}, u32[]{:S(2)}, u32[]{:S(2)}) collective-permute-start(bf16[512,768]{1,0:T(8,128)(2,1)} %collective-permute-done.19), channel_id=1, source_target_pairs={{8,0},{9,1},{10,2},{11,3},{12,4},{13,5},{14,6},{15,7},{16,8},{17,9... | collective-permute-start | bytes 2359304 | tf_op jit(solution)/shard_map/ppermute | solution.py:57
  123.1 18.2 %all-gather.1 = f32[4,1,768]{2,1,0:T(1,128)S(1)} all-gather(f32[1,1,768]{2,1,0:T(1,128)S(1)} %reshape.8), channel_id=2, replica_groups=mesh['pair'=4,'row'=4,'col'=2] {'pair'}, dimensions={0}, use_global_device_ids=true | all-gather | bytes 15360 | tf_op jit(solution)/shard_map/all_gather | solution.py:101
  143.8 4.1 %collective-permute-start.27 = (bf16[512,768]{1,0:T(8,128)(2,1)}, bf16[512,768]{1,0:T(8,128)(2,1)}, u32[]{:S(2)}, u32[]{:S(2)}) collective-permute-start(bf16[512,768]{1,0:T(8,128)(2,1)} %collective-permute-done.23), channel_id=1, source_target_pairs={{16,24},{17,25},{18,26},{19,27},{20,28},{21,29},{22,30},{23,31}} | collective-permute-start | bytes 2359304 | tf_op jit(solution)/shard_map/ppermute | solution.py:57
  149.6 5.7 %collective-permute-start.30 = (bf16[512,768]{1,0:T(8,128)(2,1)}, bf16[512,768]{1,0:T(8,128)(2,1)S(1)}, u32[]{:S(2)}, u32[]{:S(2)}) collective-permute-start(bf16[512,768]{1,0:T(8,128)(2,1)} %pad_maximum_fusion.1), channel_id=1, source_target_pairs={{0,2},{1,3},{2,0},{3,1},{4,6},{5,7},{6,4},{7,5},{8,10},{9,11},{10,... | collective-permute-start | bytes 2359304 | tf_op jit(solution)/shard_map/ppermute | solution.py:57
  158.8 2.9 %collective-permute-start.24 = (bf16[256,768]{1,0:T(8,128)(2,1)S(1)}, bf16[256,768]{1,0:T(8,128)(2,1)S(1)}, u32[]{:S(2)}, u32[]{:S(2)}) collective-permute-start(bf16[256,768]{1,0:T(8,128)(2,1)S(1)} %constant_dynamic-slice_fusion.2), channel_id=1, source_target_pairs={{0,1},{1,4},{2,3},{3,6},{8,9},{9,12},{10,11},{11,14},{20,17},{21,2... | collective-permute-start | bytes 1179656 | tf_op jit(solution)/shard_map/ppermute | solution.py:57
  163.2 19.1 %collective-permute-done.24 = bf16[256,768]{1,0:T(8,128)(2,1)S(1)} collective-permute-done((bf16[256,768]{1,0:T(8,128)(2,1)S(1)}, bf16[256,768]{1,0:T(8,128)(2,1)S(1)}, u32[]{:S(2)}, u32[]{:S(2)}) %collective-permute-start.24) | collective-permute-done | bytes 393248 | tf_op jit(solution)/shard_map/ppermute | solution.py:57
  182.3 5.0 %collective-permute-start.20 = (bf16[256,768]{1,0:T(8,128)(2,1)S(1)}, bf16[256,768]{1,0:T(8,128)(2,1)S(1)}, u32[]{:S(2)}, u32[]{:S(2)}) collective-permute-start(bf16[256,768]{1,0:T(8,128)(2,1)S(1)} %constant_dynamic-slice_fusion.4), channel_id=1, source_target_pairs={{0,1},{1,4},{2,3},{3,6},{8,9},{9,12},{10,11},{11,14},{20,17},{21,2... | collective-permute-start | bytes 1179656 | tf_op jit(solution)/shard_map/ppermute | solution.py:57
  189.6 18.0 %collective-permute-done.20 = bf16[256,768]{1,0:T(8,128)(2,1)S(1)} collective-permute-done((bf16[256,768]{1,0:T(8,128)(2,1)S(1)}, bf16[256,768]{1,0:T(8,128)(2,1)S(1)}, u32[]{:S(2)}, u32[]{:S(2)}) %collective-permute-start.20) | collective-permute-done | bytes 393248 | tf_op jit(solution)/shard_map/ppermute | solution.py:57
  208.4 5.0 %collective-permute-start.28 = (bf16[256,768]{1,0:T(8,128)(2,1)S(1)}, bf16[256,768]{1,0:T(8,128)(2,1)S(1)}, u32[]{:S(2)}, u32[]{:S(2)}) collective-permute-start(bf16[256,768]{1,0:T(8,128)(2,1)S(1)} %constant_dynamic-slice_fusion), channel_id=1, source_target_pairs={{0,1},{1,4},{2,3},{3,6},{8,9},{9,12},{10,11},{11,14},{20,17},{21,2... | collective-permute-start | bytes 1179656 | tf_op jit(solution)/shard_map/ppermute | solution.py:57
  214.4 18.5 %collective-permute-done.28 = bf16[256,768]{1,0:T(8,128)(2,1)S(1)} collective-permute-done((bf16[256,768]{1,0:T(8,128)(2,1)S(1)}, bf16[256,768]{1,0:T(8,128)(2,1)S(1)}, u32[]{:S(2)}, u32[]{:S(2)}) %collective-permute-start.28) | collective-permute-done | bytes 393248 | tf_op jit(solution)/shard_map/ppermute | solution.py:57
  (127 shorter events, 67.7 us)
Async XLA Ops:
  6.2 44.7 %collective-permute-start.7 = (bf16[192,4096]{1,0:T(8,128)(2,1)}, bf16[192,4096]{1,0:T(8,128)(2,1)}, u32[]{:S(2)}, u32[]{:S(2)}) collective-permute-start(bf16[192,4096]{1,0:T(8,128)(2,1)} %constant_dynamic-slice_fusion.6), channel_id=1, source_target_pairs={{0,1},{1,0},{2,3},{3,2},{4,5},{5,4},{6,7},{7,6},{8,9},{9,8},{10,11... | collective-permute-start | bytes 4718600 | tf_op jit(solution)/shard_map/ppermute | solution.py:57
  22.9 18.6 %collective-permute-start.3 = (bf16[256,1024]{1,0:T(8,128)(2,1)}, bf16[256,1024]{1,0:T(8,128)(2,1)}, u32[]{:S(2)}, u32[]{:S(2)}) collective-permute-start(bf16[256,1024]{1,0:T(8,128)(2,1)} %get-tuple-element.29), channel_id=1, source_target_pairs={{0,8},{1,9},{2,10},{3,11},{4,12},{5,13},{6,14},{7,15},{10,18},{11,... | collective-permute-start | bytes 1572872 | tf_op jit(solution)/shard_map/ppermute | solution.py:57
  24.2 22.2 %collective-permute-start.10 = (bf16[256,1024]{1,0:T(8,128)(2,1)}, bf16[256,1024]{1,0:T(8,128)(2,1)S(1)}, u32[]{:S(2)}, u32[]{:S(2)}) collective-permute-start(bf16[256,1024]{1,0:T(8,128)(2,1)} %get-tuple-element.30), channel_id=1, source_target_pairs={{8,0},{9,1},{10,2},{11,3},{12,4},{13,5},{14,6},{15,7},{16,8},{17,9... | collective-permute-start | bytes 1572872 | tf_op jit(solution)/shard_map/ppermute | solution.py:57
  28.2 26.8 %collective-permute-start.4 = (bf16[256,1024]{1,0:T(8,128)(2,1)}, bf16[256,1024]{1,0:T(8,128)(2,1)S(1)}, u32[]{:S(2)}, u32[]{:S(2)}) collective-permute-start(bf16[256,1024]{1,0:T(8,128)(2,1)} %get-tuple-element.29), channel_id=1, source_target_pairs={{10,2},{11,3},{14,6},{15,7}} | collective-permute-start | bytes 1572872 | tf_op jit(solution)/shard_map/ppermute | solution.py:57
  31.6 24.9 %collective-permute-start.11 = (bf16[256,1024]{1,0:T(8,128)(2,1)}, bf16[256,1024]{1,0:T(8,128)(2,1)S(1)}, u32[]{:S(2)}, u32[]{:S(2)}) collective-permute-start(bf16[256,1024]{1,0:T(8,128)(2,1)} %collective-permute-done.9), channel_id=1, source_target_pairs={{8,16},{9,17},{10,18},{11,19},{12,20},{13,21},{14,22},{15,23},{16,... | collective-permute-start | bytes 1572872 | tf_op jit(solution)/shard_map/ppermute | solution.py:57
  41.4 18.1 %collective-permute-start.5 = (bf16[256,1024]{1,0:T(8,128)(2,1)}, bf16[256,1024]{1,0:T(8,128)(2,1)S(1)}, u32[]{:S(2)}, u32[]{:S(2)}) collective-permute-start(bf16[256,1024]{1,0:T(8,128)(2,1)} %collective-permute-done.3), channel_id=1, source_target_pairs={{8,16},{9,17},{10,18},{11,19},{12,20},{13,21},{14,22},{15,23},{18,... | collective-permute-start | bytes 1572872 | tf_op jit(solution)/shard_map/ppermute | solution.py:57
  56.6 26.9 %collective-permute-start.13 = (bf16[256,1024]{1,0:T(8,128)(2,1)S(1)}, bf16[256,1024]{1,0:T(8,128)(2,1)S(1)}, u32[]{:S(2)}, u32[]{:S(2)}) collective-permute-start(bf16[256,1024]{1,0:T(8,128)(2,1)S(1)} %collective-permute-done.11), channel_id=1, source_target_pairs={{16,24},{17,25},{18,26},{19,27},{20,28},{21,29},{22,30},{23,31}} | collective-permute-start | bytes 1572872 | tf_op jit(solution)/shard_map/ppermute | solution.py:57
  59.5 22.5 %collective-permute-start.6 = (bf16[256,1024]{1,0:T(8,128)(2,1)S(1)}, bf16[256,1024]{1,0:T(8,128)(2,1)S(1)}, u32[]{:S(2)}, u32[]{:S(2)}) collective-permute-start(bf16[256,1024]{1,0:T(8,128)(2,1)S(1)} %collective-permute-done.5), channel_id=1, source_target_pairs={{16,24},{17,25},{18,26},{19,27},{20,28},{21,29},{22,30},{23,31}} | collective-permute-start | bytes 1572872 | tf_op jit(solution)/shard_map/ppermute | solution.py:57
  95.6 19.6 %collective-permute-start.18 = (bf16[512,768]{1,0:T(8,128)(2,1)}, bf16[512,768]{1,0:T(8,128)(2,1)S(1)}, u32[]{:S(2)}, u32[]{:S(2)}) collective-permute-start(bf16[512,768]{1,0:T(8,128)(2,1)} %pad_maximum_fusion.1), channel_id=1, source_target_pairs={{0,8},{1,9},{2,10},{3,11},{4,12},{5,13},{6,14},{7,15},{8,16},{9,17... | collective-permute-start | bytes 2359304 | tf_op jit(solution)/shard_map/ppermute | solution.py:57
  99.7 19.5 %collective-permute-start.19 = (bf16[512,768]{1,0:T(8,128)(2,1)}, bf16[512,768]{1,0:T(8,128)(2,1)}, u32[]{:S(2)}, u32[]{:S(2)}) collective-permute-start(bf16[512,768]{1,0:T(8,128)(2,1)} %pad_maximum_fusion.1), channel_id=1, source_target_pairs={{8,0},{9,1},{10,2},{11,3},{12,4},{13,5},{14,6},{15,7},{16,8},{17,9... | collective-permute-start | bytes 2359304 | tf_op jit(solution)/shard_map/ppermute | solution.py:57
  115.2 28.6 %collective-permute-start.23 = (bf16[512,768]{1,0:T(8,128)(2,1)S(1)}, bf16[512,768]{1,0:T(8,128)(2,1)}, u32[]{:S(2)}, u32[]{:S(2)}) collective-permute-start(bf16[512,768]{1,0:T(8,128)(2,1)S(1)} %collective-permute-done.18), channel_id=1, source_target_pairs={{8,16},{9,17},{10,18},{11,19},{12,20},{13,21},{14,22},{15,23},{16,... | collective-permute-start | bytes 2359304 | tf_op jit(solution)/shard_map/ppermute | solution.py:57
  119.2 28.7 %collective-permute-start.22 = (bf16[512,768]{1,0:T(8,128)(2,1)}, bf16[512,768]{1,0:T(8,128)(2,1)}, u32[]{:S(2)}, u32[]{:S(2)}) collective-permute-start(bf16[512,768]{1,0:T(8,128)(2,1)} %collective-permute-done.19), channel_id=1, source_target_pairs={{8,0},{9,1},{10,2},{11,3},{12,4},{13,5},{14,6},{15,7},{16,8},{17,9... | collective-permute-start | bytes 2359304 | tf_op jit(solution)/shard_map/ppermute | solution.py:57
  122.2 34.5 %collective-permute-start.17 = (bf16[512,768]{1,0:T(8,128)(2,1)}, bf16[512,768]{1,0:T(8,128)(2,1)S(1)}, u32[]{:S(2)}, u32[]{:S(2)}) collective-permute-start(bf16[512,768]{1,0:T(8,128)(2,1)} %pad_maximum_fusion.1), channel_id=1, source_target_pairs={{0,4},{1,5},{2,6},{3,7},{4,0},{5,1},{6,2},{7,3},{8,12},{9,13},{10,... | collective-permute-start | bytes 2359304 | tf_op jit(solution)/shard_map/ppermute | solution.py:57
  143.8 15.0 %collective-permute-start.27 = (bf16[512,768]{1,0:T(8,128)(2,1)}, bf16[512,768]{1,0:T(8,128)(2,1)}, u32[]{:S(2)}, u32[]{:S(2)}) collective-permute-start(bf16[512,768]{1,0:T(8,128)(2,1)} %collective-permute-done.23), channel_id=1, source_target_pairs={{16,24},{17,25},{18,26},{19,27},{20,28},{21,29},{22,30},{23,31}} | collective-permute-start | bytes 2359304 | tf_op jit(solution)/shard_map/ppermute | solution.py:57
  149.6 86.3 %collective-permute-start.30 = (bf16[512,768]{1,0:T(8,128)(2,1)}, bf16[512,768]{1,0:T(8,128)(2,1)S(1)}, u32[]{:S(2)}, u32[]{:S(2)}) collective-permute-start(bf16[512,768]{1,0:T(8,128)(2,1)} %pad_maximum_fusion.1), channel_id=1, source_target_pairs={{0,2},{1,3},{2,0},{3,1},{4,6},{5,7},{6,4},{7,5},{8,10},{9,11},{10,... | collective-permute-start | bytes 2359304 | tf_op jit(solution)/shard_map/ppermute | solution.py:57
  156.6 30.7 %collective-permute-start.25 = (bf16[512,768]{1,0:T(8,128)(2,1)S(1)}, bf16[512,768]{1,0:T(8,128)(2,1)S(1)}, u32[]{:S(2)}, u32[]{:S(2)}) collective-permute-start(bf16[512,768]{1,0:T(8,128)(2,1)S(1)} %broadcast_select_fusion.2), channel_id=1, source_target_pairs={{0,4},{1,5},{2,6},{3,7},{4,0},{5,1},{6,2},{7,3},{8,12},{9,13},{10,... | collective-permute-start | bytes 2359304 | tf_op jit(solution)/shard_map/ppermute | solution.py:57
  156.9 31.1 %collective-permute-start.32 = (bf16[512,768]{1,0:T(8,128)(2,1)S(1)}, bf16[512,768]{1,0:T(8,128)(2,1)S(1)}, u32[]{:S(2)}, u32[]{:S(2)}) collective-permute-start(bf16[512,768]{1,0:T(8,128)(2,1)S(1)} %broadcast_select_fusion.2), channel_id=1, source_target_pairs={{0,2},{1,3},{2,0},{3,1},{4,6},{5,7},{6,4},{7,5},{8,10},{9,11},{10,... | collective-permute-start | bytes 2359304 | tf_op jit(solution)/shard_map/ppermute | solution.py:57
  158.8 23.5 %collective-permute-start.24 = (bf16[256,768]{1,0:T(8,128)(2,1)S(1)}, bf16[256,768]{1,0:T(8,128)(2,1)S(1)}, u32[]{:S(2)}, u32[]{:S(2)}) collective-permute-start(bf16[256,768]{1,0:T(8,128)(2,1)S(1)} %constant_dynamic-slice_fusion.2), channel_id=1, source_target_pairs={{0,1},{1,4},{2,3},{3,6},{8,9},{9,12},{10,11},{11,14},{20,17},{21,2... | collective-permute-start | bytes 1179656 | tf_op jit(solution)/shard_map/ppermute | solution.py:57
  163.1 45.3 %collective-permute-start.21 = (bf16[512,768]{1,0:T(8,128)(2,1)S(1)}, bf16[512,768]{1,0:T(8,128)(2,1)S(1)}, u32[]{:S(2)}, u32[]{:S(2)}) collective-permute-start(bf16[512,768]{1,0:T(8,128)(2,1)S(1)} %get-tuple-element.26), channel_id=1, source_target_pairs={{0,4},{1,5},{2,6},{3,7},{4,0},{5,1},{6,2},{7,3},{8,12},{9,13},{10,... | collective-permute-start | bytes 2359304 | tf_op jit(solution)/shard_map/ppermute | solution.py:57
  182.3 25.3 %collective-permute-start.20 = (bf16[256,768]{1,0:T(8,128)(2,1)S(1)}, bf16[256,768]{1,0:T(8,128)(2,1)S(1)}, u32[]{:S(2)}, u32[]{:S(2)}) collective-permute-start(bf16[256,768]{1,0:T(8,128)(2,1)S(1)} %constant_dynamic-slice_fusion.4), channel_id=1, source_target_pairs={{0,1},{1,4},{2,3},{3,6},{8,9},{9,12},{10,11},{11,14},{20,17},{21,2... | collective-permute-start | bytes 1179656 | tf_op jit(solution)/shard_map/ppermute | solution.py:57
  187.3 46.1 %collective-permute-start.29 = (bf16[512,768]{1,0:T(8,128)(2,1)S(1)}, bf16[512,768]{1,0:T(8,128)(2,1)S(1)}, u32[]{:S(2)}, u32[]{:S(2)}) collective-permute-start(bf16[512,768]{1,0:T(8,128)(2,1)S(1)} %get-tuple-element.25), channel_id=1, source_target_pairs={{0,4},{1,5},{2,6},{3,7},{4,0},{5,1},{6,2},{7,3},{8,12},{9,13},{10,... | collective-permute-start | bytes 2359304 | tf_op jit(solution)/shard_map/ppermute | solution.py:57
  188.0 46.0 %collective-permute-start.33 = (bf16[512,768]{1,0:T(8,128)(2,1)S(1)}, bf16[512,768]{1,0:T(8,128)(2,1)S(1)}, u32[]{:S(2)}, u32[]{:S(2)}) collective-permute-start(bf16[512,768]{1,0:T(8,128)(2,1)S(1)} %get-tuple-element.25), channel_id=1, source_target_pairs={{0,2},{1,3},{2,0},{3,1},{4,6},{5,7},{6,4},{7,5},{8,10},{9,11},{10,... | collective-permute-start | bytes 2359304 | tf_op jit(solution)/shard_map/ppermute | solution.py:57
  207.5 27.5 %collective-permute-start.31 = (bf16[512,768]{1,0:T(8,128)(2,1)S(1)}, bf16[512,768]{1,0:T(8,128)(2,1)S(1)}, u32[]{:S(2)}, u32[]{:S(2)}) collective-permute-start(bf16[512,768]{1,0:T(8,128)(2,1)S(1)} %get-tuple-element.26), channel_id=1, source_target_pairs={{0,2},{1,3},{2,0},{3,1},{4,6},{5,7},{6,4},{7,5},{8,10},{9,11},{10,... | collective-permute-start | bytes 2359304 | tf_op jit(solution)/shard_map/ppermute | solution.py:57
  208.4 24.5 %collective-permute-start.28 = (bf16[256,768]{1,0:T(8,128)(2,1)S(1)}, bf16[256,768]{1,0:T(8,128)(2,1)S(1)}, u32[]{:S(2)}, u32[]{:S(2)}) collective-permute-start(bf16[256,768]{1,0:T(8,128)(2,1)S(1)} %constant_dynamic-slice_fusion), channel_id=1, source_target_pairs={{0,1},{1,4},{2,3},{3,6},{8,9},{9,12},{10,11},{11,14},{20,17},{21,2... | collective-permute-start | bytes 1179656 | tf_op jit(solution)/shard_map/ppermute | solution.py:57
  (19 other events, 215.5 us)

commit v3 on v1

--- a/solution.py
+++ b/solution.py
@@ -82,20 +82,23 @@
     n_rows, width = inverse_factor.shape
     piece = n_rows // 4
 
+    own, *others = lax.optimization_barrier(
+        [
+            lax.dynamic_slice_in_dim(inverse_factor, (chip ^ c) * piece, piece, 0)
+            for c in range(4)
+        ]
+    )
+    got_y, got_x, got_xy = (
+        send(q, r) for q, r in zip(others, (OVER_Y, OVER_X, OVER_XY))
+    )
+
     half = mine.shape[0] // 2
-    from_y = send(lax.dynamic_slice_in_dim(mine, k * half, half, 0), OVER_Y)
+    give = lax.dynamic_slice_in_dim(mine, k * half, half, 0)
+    from_y = send(lax.optimization_barrier((give, got_y, got_x, got_xy))[0], OVER_Y)
     from_core = send(from_y, OVER_CORE)
     theirs = jnp.concatenate(
         [jnp.where(k == 0, from_y, from_core), jnp.where(k == 0, from_core, from_y)], 0
     )
-
-    def quarter(c):
-        return lax.dynamic_slice_in_dim(inverse_factor, c * piece, piece, 0)
-
-    own = quarter(chip)
-    got_y = send(quarter(chip ^ 1), OVER_Y)
-    got_x = send(quarter(chip ^ 2), OVER_X)
-    got_xy = send(quarter(chip ^ 3), OVER_XY)
 
     def by_y(a, b):
         return jnp.concatenate([jnp.where(y == 0, a, b), jnp.where(y == 0, b, a)], 1)

time: 204 us -> 200 us (0.980)
  waiting for transfers between devices: 79.6 us -> 74.5 us
  starting transfers between devices: 62.2 us -> 64.4 us
    ppermute x34, waiting for transfers between devices: 79.6 us -> 74.5 us  [send(): return lax.ppermute(value, AXES, pairs)]
    ppermute x34, starting transfers between devices: 62.2 us -> 64.4 us  [send(): return lax.ppermute(value, AXES, pairs)]
  transfers between devices with their start and end apart: 34 -> 34, of which waited for: 18 -> 20; matrix products, arithmetic and copies ran while one was open for 23% -> 23% of each run, Pallas kernels for 0% -> 0%
where the time goes in v3:
time: 200 us; the launch traced here: 198 us
  waiting for transfers between devices  74.5 us (37%)
  starting transfers between devices  64.4 us (32%)
  matrix products  38.5 us (19%)
  other arithmetic  14.3 us (7%)
  local copies, waits for them, and re-layouts  4.96 us (2%)
    ppermute x34, waiting for transfers between devices, send(): return lax.ppermute(value, AXES, pairs)  74.5 us
    ppermute x34, starting transfers between devices, send(): return lax.ppermute(value, AXES, pairs)  64.4 us
    dot_general x8, matrix products, columns_by_columns(): lax.dot_general(a, b, (((0,), (0,)), ((), ())), preferred_element_type=F32)  20.3 us
    dot_general x24, matrix products, rows_by_rows(): lax.dot_general(a, b, (((1,), (1,)), ((), ())), preferred_element_type=F32)  18.2 us
  transfers between devices with their start and end apart: 34, of which 20 were waited for; matrix products, arithmetic and copies ran while one was open for 23% of the time, Pallas kernels for 0%

profile of v3, /device:TPU:19, one launch (start us, length us, event | category | flops | bytes accessed | tf_op | source)
XLA Modules:
  0.0 198.1 jit_solution(2058598711933553683)
XLA Ops:
  6.2 3.5 %collective-permute-done = bf16[256,512]{1,0:T(8,128)(2,1)} collective-permute-done((bf16[256,512]{1,0:T(8,128)(2,1)}, bf16[256,512]{1,0:T(8,128)(2,1)}, u32[]{:S(2)}, u32[]{:S(2)}) %collective-permute-start) | collective-permute-done | bytes 262176 | tf_op jit(solution)/shard_map/ppermute | solution.py:57
  10.7 5.6 %collective-permute-done.2 = bf16[256,512]{1,0:T(8,128)(2,1)} collective-permute-done((bf16[256,512]{1,0:T(8,128)(2,1)}, bf16[256,512]{1,0:T(8,128)(2,1)}, u32[]{:S(2)}, u32[]{:S(2)}) %collective-permute-start.2) | collective-permute-done | bytes 262176 | tf_op jit(solution)/shard_map/ppermute | solution.py:57
  22.1 3.4 %collective-permute-start.9 = (bf16[256,1024]{1,0:T(8,128)(2,1)}, bf16[256,1024]{1,0:T(8,128)(2,1)}, u32[]{:S(2)}, u32[]{:S(2)}) collective-permute-start(bf16[256,1024]{1,0:T(8,128)(2,1)} %get-tuple-element.27), channel_id=1, source_target_pairs={{0,8},{1,9},{2,10},{3,11},{4,12},{5,13},{6,14},{7,15},{8,16},{9,17... | collective-permute-start | bytes 1572872 | tf_op jit(solution)/shard_map/ppermute | solution.py:57
  26.2 6.0 %collective-permute-start.10 = (bf16[256,1024]{1,0:T(8,128)(2,1)}, bf16[256,1024]{1,0:T(8,128)(2,1)S(1)}, u32[]{:S(2)}, u32[]{:S(2)}) collective-permute-start(bf16[256,1024]{1,0:T(8,128)(2,1)} %get-tuple-element.27), channel_id=1, source_target_pairs={{8,0},{9,1},{10,2},{11,3},{12,4},{13,5},{14,6},{15,7},{16,8},{17,9... | collective-permute-start | bytes 1572872 | tf_op jit(solution)/shard_map/ppermute | solution.py:57
  37.6 4.9 %collective-permute-done.9 = bf16[256,1024]{1,0:T(8,128)(2,1)} collective-permute-done((bf16[256,1024]{1,0:T(8,128)(2,1)}, bf16[256,1024]{1,0:T(8,128)(2,1)}, u32[]{:S(2)}, u32[]{:S(2)}) %collective-permute-start.9) | collective-permute-done | bytes 524320 | tf_op jit(solution)/shard_map/ppermute | solution.py:57
  45.9 4.5 %collective-permute-start.12 = (bf16[256,1024]{1,0:T(8,128)(2,1)S(1)}, bf16[256,1024]{1,0:T(8,128)(2,1)S(1)}, u32[]{:S(2)}, u32[]{:S(2)}) collective-permute-start(bf16[256,1024]{1,0:T(8,128)(2,1)S(1)} %collective-permute-done.10), channel_id=1, source_target_pairs={{8,0},{9,1},{10,2},{11,3},{12,4},{13,5},{14,6},{15,7},{18,10},{19,... | collective-permute-start | bytes 1572872 | tf_op jit(solution)/shard_map/ppermute | solution.py:57
  55.7 3.2 %collective-permute-start.6 = (bf16[256,1024]{1,0:T(8,128)(2,1)S(1)}, bf16[256,1024]{1,0:T(8,128)(2,1)S(1)}, u32[]{:S(2)}, u32[]{:S(2)}) collective-permute-start(bf16[256,1024]{1,0:T(8,128)(2,1)S(1)} %collective-permute-done.5), channel_id=1, source_target_pairs={{16,24},{17,25},{18,26},{19,27},{20,28},{21,29},{22,30},{23,31}} | collective-permute-start | bytes 1572872 | tf_op jit(solution)/shard_map/ppermute | solution.py:57
  59.6 4.6 %collective-permute-done.11 = bf16[256,1024]{1,0:T(8,128)(2,1)S(1)} collective-permute-done((bf16[256,1024]{1,0:T(8,128)(2,1)}, bf16[256,1024]{1,0:T(8,128)(2,1)S(1)}, u32[]{:S(2)}, u32[]{:S(2)}) %collective-permute-start.11) | collective-permute-done | bytes 524320 | tf_op jit(solution)/shard_map/ppermute | solution.py:57
  78.3 3.1 %collective-permute-done.13 = bf16[256,1024]{1,0:T(8,128)(2,1)S(1)} collective-permute-done((bf16[256,1024]{1,0:T(8,128)(2,1)S(1)}, bf16[256,1024]{1,0:T(8,128)(2,1)S(1)}, u32[]{:S(2)}, u32[]{:S(2)}) %collective-permute-start.13) | collective-permute-done | bytes 524320 | tf_op jit(solution)/shard_map/ppermute | solution.py:57
  86.2 6.9 %collective-permute-done.15 = bf16[768,256]{1,0:T(8,128)(2,1)S(1)} collective-permute-done((bf16[768,256]{1,0:T(8,128)(2,1)S(1)}, bf16[768,256]{1,0:T(8,128)(2,1)S(1)}, u32[]{:S(2)}, u32[]{:S(2)}) %collective-permute-start.15) | collective-permute-done | bytes 393248 | tf_op jit(solution)/shard_map/ppermute | solution.py:57
  94.6 6.9 %collective-permute-done.16 = bf16[768,256]{1,0:T(8,128)(2,1)S(1)} collective-permute-done((bf16[768,256]{1,0:T(8,128)(2,1)S(1)}, bf16[768,256]{1,0:T(8,128)(2,1)S(1)}, u32[]{:S(2)}, u32[]{:S(2)}) %collective-permute-start.16) | collective-permute-done | bytes 393248 | tf_op jit(solution)/shard_map/ppermute | solution.py:57
  103.3 7.6 %collective-permute-done.19 = bf16[768,256]{1,0:T(8,128)(2,1)S(1)} collective-permute-done((bf16[768,256]{1,0:T(8,128)(2,1)S(1)}, bf16[768,256]{1,0:T(8,128)(2,1)S(1)}, u32[]{:S(2)}, u32[]{:S(2)}) %collective-permute-start.19) | collective-permute-done | bytes 393248 | tf_op jit(solution)/shard_map/ppermute | solution.py:57
  122.2 3.4 %fusion.110 = (bf16[256,1024]{1,0:T(8,128)(2,1)}, f32[256,1024]{1,0:T(8,128)}) fusion(bf16[768,1024]{1,0:T(8,128)(2,1)} %collective-permute-done.27, bf16[768,1024]{1,0:T(8,128)(2,1)} %copy-done.1, s32[]{:T(128)S(6)} %select_n.266), kind=kOutput, calls=%fused_computation.188 | convolution fusion | flops 402915328 | bytes 3538948 | tf_op jit(solution)/shard_map/dot_general | solution.py:16
  128.4 8.5 %collective-permute-done.24 = bf16[256,1024]{1,0:T(8,128)(2,1)} collective-permute-done((bf16[256,1024]{1,0:T(8,128)(2,1)}, bf16[256,1024]{1,0:T(8,128)(2,1)}, u32[]{:S(2)}, u32[]{:S(2)}) %collective-permute-start.24) | collective-permute-done | bytes 524320 | tf_op jit(solution)/shard_map/ppermute | solution.py:57
  136.9 3.0 %add_convert_fusion.7 = (bf16[256,1024]{1,0:T(8,128)(2,1)}, bf16[256,1024]{1,0:T(8,128)(2,1)}) fusion(bf16[256,1024]{1,0:T(8,128)(2,1)} %collective-permute-done.21, bf16[256,1024]{1,0:T(8,128)(2,1)} %collective-permute-done.24, bf16[768,256]{1,0:T(8,128)(2,1)S(1)} %copy-done.10, bf16[768,256]{1,0:T(8,128)(2,1)S(1)} %copy-done.6, ...), kind=kOutput, calls=%fused_computation.71 | convolution fusion | flops 410517504 | bytes 4063236 | tf_op jit(solution)/shard_map/dot_general | solution.py:16
  141.2 4.0 %collective-permute-start.25 = (bf16[256,1024]{1,0:T(8,128)(2,1)}, bf16[256,1024]{1,0:T(8,128)(2,1)}, u32[]{:S(2)}, u32[]{:S(2)}) collective-permute-start(bf16[256,1024]{1,0:T(8,128)(2,1)} %get-tuple-element.26), channel_id=1, source_target_pairs={{16,8},{17,9},{18,10},{19,11},{20,12},{21,13},{22,14},{23,15},{24,... | collective-permute-start | bytes 1572872 | tf_op jit(solution)/shard_map/ppermute | solution.py:57
  151.8 4.0 %collective-permute-start.32 = (bf16[256,1024]{1,0:T(8,128)(2,1)S(1)}, bf16[256,1024]{1,0:T(8,128)(2,1)S(1)}, u32[]{:S(2)}, u32[]{:S(2)}) collective-permute-start(bf16[256,1024]{1,0:T(8,128)(2,1)S(1)} %get-tuple-element.24), channel_id=1, source_target_pairs={{16,8},{17,9},{18,10},{19,11},{20,12},{21,13},{22,14},{23,15},{24,... | collective-permute-start | bytes 1572872 | tf_op jit(solution)/shard_map/ppermute | solution.py:57
  155.9 3.5 %collective-permute-done.25 = bf16[256,1024]{1,0:T(8,128)(2,1)} collective-permute-done((bf16[256,1024]{1,0:T(8,128)(2,1)}, bf16[256,1024]{1,0:T(8,128)(2,1)}, u32[]{:S(2)}, u32[]{:S(2)}) %collective-permute-start.25) | collective-permute-done | bytes 524320 | tf_op jit(solution)/shard_map/ppermute | solution.py:57
  159.4 3.0 %add_convert_fusion.6 = (bf16[256,1024]{1,0:T(8,128)(2,1)}, bf16[256,1024]{1,0:T(8,128)(2,1)}) fusion(bf16[256,1024]{1,0:T(8,128)(2,1)} %collective-permute-done.22, f32[256,1024]{1,0:T(8,128)S(1)} %copy-done.18, pred[]{:T(512)S(6)} %eq.15, bf16[256,1024]{1,0:T(8,128)(2,1)} %collective-permute-done.25, pred[]{:T(512)S(6)} %eq.16, ...), kind=kOutput, calls=%fused_computation.70 | convolution fusion | flops 411041792 | bytes 5111814 | tf_op jit(solution)/shard_map/dot_general | solution.py:16
  164.4 3.6 %collective-permute-start.26 = (bf16[256,1024]{1,0:T(8,128)(2,1)}, bf16[256,1024]{1,0:T(8,128)(2,1)}, u32[]{:S(2)}, u32[]{:S(2)}) collective-permute-start(bf16[256,1024]{1,0:T(8,128)(2,1)} %get-tuple-element.22), channel_id=1, source_target_pairs={{8,0},{9,1},{10,2},{11,3},{12,4},{13,5},{14,6},{15,7},{16,8},{17,9... | collective-permute-start | bytes 1572872 | tf_op jit(solution)/shard_map/ppermute | solution.py:57
  173.9 3.3 %collective-permute-start.33 = (bf16[256,1024]{1,0:T(8,128)(2,1)}, bf16[256,1024]{1,0:T(8,128)(2,1)}, u32[]{:S(2)}, u32[]{:S(2)}) collective-permute-start(bf16[256,1024]{1,0:T(8,128)(2,1)} %get-tuple-element.20), channel_id=1, source_target_pairs={{8,0},{9,1},{10,2},{11,3},{12,4},{13,5},{14,6},{15,7},{16,8},{17,9... | collective-permute-start | bytes 1572872 | tf_op jit(solution)/shard_map/ppermute | solution.py:57
  177.3 4.5 %collective-permute-done.26 = bf16[256,1024]{1,0:T(8,128)(2,1)} collective-permute-done((bf16[256,1024]{1,0:T(8,128)(2,1)}, bf16[256,1024]{1,0:T(8,128)(2,1)}, u32[]{:S(2)}, u32[]{:S(2)}) %collective-permute-start.26) | collective-permute-done | bytes 524320 | tf_op jit(solution)/shard_map/ppermute | solution.py:57
  184.1 4.3 %collective-permute-done.30 = bf16[256,1024]{1,0:T(8,128)(2,1)} collective-permute-done((bf16[256,1024]{1,0:T(8,128)(2,1)}, bf16[256,1024]{1,0:T(8,128)(2,1)}, u32[]{:S(2)}, u32[]{:S(2)}) %collective-permute-start.30) | collective-permute-done | bytes 524320 | tf_op jit(solution)/shard_map/ppermute | solution.py:57
  188.4 4.6 %collective-permute-done.33 = bf16[256,1024]{1,0:T(8,128)(2,1)} collective-permute-done((bf16[256,1024]{1,0:T(8,128)(2,1)}, bf16[256,1024]{1,0:T(8,128)(2,1)}, u32[]{:S(2)}, u32[]{:S(2)}) %collective-permute-start.33) | collective-permute-done | bytes 524320 | tf_op jit(solution)/shard_map/ppermute | solution.py:57
  (137 shorter events, 86.7 us)
Async XLA Ops:
  16.2 34.3 %collective-permute-start.7 = (bf16[192,4096]{1,0:T(8,128)(2,1)}, bf16[192,4096]{1,0:T(8,128)(2,1)}, u32[]{:S(2)}, u32[]{:S(2)}) collective-permute-start(bf16[192,4096]{1,0:T(8,128)(2,1)} %constant_dynamic-slice_fusion), channel_id=1, source_target_pairs={{0,1},{1,0},{2,3},{3,2},{4,5},{5,4},{6,7},{7,6},{8,9},{9,8},{10,11... | collective-permute-start | bytes 4718600 | tf_op jit(solution)/shard_map/ppermute | solution.py:57
  22.1 20.5 %collective-permute-start.9 = (bf16[256,1024]{1,0:T(8,128)(2,1)}, bf16[256,1024]{1,0:T(8,128)(2,1)}, u32[]{:S(2)}, u32[]{:S(2)}) collective-permute-start(bf16[256,1024]{1,0:T(8,128)(2,1)} %get-tuple-element.27), channel_id=1, source_target_pairs={{0,8},{1,9},{2,10},{3,11},{4,12},{5,13},{6,14},{7,15},{8,16},{9,17... | collective-permute-start | bytes 1572872 | tf_op jit(solution)/shard_map/ppermute | solution.py:57
  25.5 29.8 %collective-permute-start.4 = (bf16[256,1024]{1,0:T(8,128)(2,1)}, bf16[256,1024]{1,0:T(8,128)(2,1)S(1)}, u32[]{:S(2)}, u32[]{:S(2)}) collective-permute-start(bf16[256,1024]{1,0:T(8,128)(2,1)} %get-tuple-element.28), channel_id=1, source_target_pairs={{10,2},{11,3},{14,6},{15,7}} | collective-permute-start | bytes 1572872 | tf_op jit(solution)/shard_map/ppermute | solution.py:57
  26.2 19.7 %collective-permute-start.10 = (bf16[256,1024]{1,0:T(8,128)(2,1)}, bf16[256,1024]{1,0:T(8,128)(2,1)S(1)}, u32[]{:S(2)}, u32[]{:S(2)}) collective-permute-start(bf16[256,1024]{1,0:T(8,128)(2,1)} %get-tuple-element.27), channel_id=1, source_target_pairs={{8,0},{9,1},{10,2},{11,3},{12,4},{13,5},{14,6},{15,7},{16,8},{17,9... | collective-permute-start | bytes 1572872 | tf_op jit(solution)/shard_map/ppermute | solution.py:57
  32.8 22.9 %collective-permute-start.5 = (bf16[256,1024]{1,0:T(8,128)(2,1)}, bf16[256,1024]{1,0:T(8,128)(2,1)S(1)}, u32[]{:S(2)}, u32[]{:S(2)}) collective-permute-start(bf16[256,1024]{1,0:T(8,128)(2,1)} %collective-permute-done.3), channel_id=1, source_target_pairs={{8,16},{9,17},{10,18},{11,19},{12,20},{13,21},{14,22},{15,23},{18,... | collective-permute-start | bytes 1572872 | tf_op jit(solution)/shard_map/ppermute | solution.py:57
  44.0 20.2 %collective-permute-start.11 = (bf16[256,1024]{1,0:T(8,128)(2,1)}, bf16[256,1024]{1,0:T(8,128)(2,1)S(1)}, u32[]{:S(2)}, u32[]{:S(2)}) collective-permute-start(bf16[256,1024]{1,0:T(8,128)(2,1)} %collective-permute-done.9), channel_id=1, source_target_pairs={{8,16},{9,17},{10,18},{11,19},{12,20},{13,21},{14,22},{15,23},{16,... | collective-permute-start | bytes 1572872 | tf_op jit(solution)/shard_map/ppermute | solution.py:57
  50.6 16.8 %collective-permute-start.8 = (bf16[192,4096]{1,0:T(8,128)(2,1)}, bf16[192,4096]{1,0:T(8,128)(2,1)S(1)}, u32[]{:S(2)}, u32[]{:S(2)}) collective-permute-start(bf16[192,4096]{1,0:T(8,128)(2,1)} %collective-permute-done.7), channel_id=1, source_target_pairs={{0,2},{1,3},{2,0},{3,1},{4,6},{5,7},{6,4},{7,5},{8,10},{9,11},{10,... | collective-permute-start | bytes 4718600 | tf_op jit(solution)/shard_map/ppermute | solution.py:57
  55.7 21.4 %collective-permute-start.6 = (bf16[256,1024]{1,0:T(8,128)(2,1)S(1)}, bf16[256,1024]{1,0:T(8,128)(2,1)S(1)}, u32[]{:S(2)}, u32[]{:S(2)}) collective-permute-start(bf16[256,1024]{1,0:T(8,128)(2,1)S(1)} %collective-permute-done.5), channel_id=1, source_target_pairs={{16,24},{17,25},{18,26},{19,27},{20,28},{21,29},{22,30},{23,31}} | collective-permute-start | bytes 1572872 | tf_op jit(solution)/shard_map/ppermute | solution.py:57
  64.2 17.3 %collective-permute-start.13 = (bf16[256,1024]{1,0:T(8,128)(2,1)S(1)}, bf16[256,1024]{1,0:T(8,128)(2,1)S(1)}, u32[]{:S(2)}, u32[]{:S(2)}) collective-permute-start(bf16[256,1024]{1,0:T(8,128)(2,1)S(1)} %collective-permute-done.11), channel_id=1, source_target_pairs={{16,24},{17,25},{18,26},{19,27},{20,28},{21,29},{22,30},{23,31}} | collective-permute-start | bytes 1572872 | tf_op jit(solution)/shard_map/ppermute | solution.py:57
  84.8 16.8 %collective-permute-start.16 = (bf16[768,256]{1,0:T(8,128)(2,1)S(1)}, bf16[768,256]{1,0:T(8,128)(2,1)S(1)}, u32[]{:S(2)}, u32[]{:S(2)}) collective-permute-start(bf16[768,256]{1,0:T(8,128)(2,1)S(1)} %get-tuple-element.46), channel_id=1, source_target_pairs={{0,1},{1,0},{2,3},{3,2},{4,5},{5,4},{6,7},{7,6},{8,9},{9,8},{10,11... | collective-permute-start | bytes 1179656 | tf_op jit(solution)/shard_map/ppermute | solution.py:57
  85.0 17.5 %collective-permute-start.17 = (bf16[768,256]{1,0:T(8,128)(2,1)S(1)}, bf16[768,256]{1,0:T(8,128)(2,1)S(1)}, u32[]{:S(2)}, u32[]{:S(2)}) collective-permute-start(bf16[768,256]{1,0:T(8,128)(2,1)S(1)} %get-tuple-element.45), channel_id=1, source_target_pairs={{0,4},{1,5},{2,6},{3,7},{4,0},{5,1},{6,2},{7,3},{8,12},{9,13},{10,... | collective-permute-start | bytes 1179656 | tf_op jit(solution)/shard_map/ppermute | solution.py:57
  93.1 17.8 %collective-permute-start.19 = (bf16[768,256]{1,0:T(8,128)(2,1)S(1)}, bf16[768,256]{1,0:T(8,128)(2,1)S(1)}, u32[]{:S(2)}, u32[]{:S(2)}) collective-permute-start(bf16[768,256]{1,0:T(8,128)(2,1)S(1)} %collective-permute-done.15), channel_id=1, source_target_pairs={{0,4},{1,5},{2,6},{3,7},{4,0},{5,1},{6,2},{7,3},{8,12},{9,13},{10,... | collective-permute-start | bytes 1179656 | tf_op jit(solution)/shard_map/ppermute | solution.py:57
  94.1 16.9 %collective-permute-start.20 = (bf16[768,256]{1,0:T(8,128)(2,1)S(1)}, bf16[768,256]{1,0:T(8,128)(2,1)S(1)}, u32[]{:S(2)}, u32[]{:S(2)}) collective-permute-start(bf16[768,256]{1,0:T(8,128)(2,1)S(1)} %collective-permute-done.18), channel_id=1, source_target_pairs={{0,1},{1,0},{2,3},{3,2},{4,5},{5,4},{6,7},{7,6},{8,9},{9,8},{10,11... | collective-permute-start | bytes 1179656 | tf_op jit(solution)/shard_map/ppermute | solution.py:57
  120.9 16.0 %collective-permute-start.24 = (bf16[256,1024]{1,0:T(8,128)(2,1)}, bf16[256,1024]{1,0:T(8,128)(2,1)}, u32[]{:S(2)}, u32[]{:S(2)}) collective-permute-start(bf16[256,1024]{1,0:T(8,128)(2,1)} %get-tuple-element.51), channel_id=1, source_target_pairs={{24,16},{25,17},{26,18},{27,19},{28,20},{29,21},{30,22},{31,23}} | collective-permute-start | bytes 1572872 | tf_op jit(solution)/shard_map/ppermute | solution.py:57
  125.6 19.7 %collective-permute-start.28 = (bf16[256,1024]{1,0:T(8,128)(2,1)}, bf16[256,1024]{1,0:T(8,128)(2,1)}, u32[]{:S(2)}, u32[]{:S(2)}) collective-permute-start(bf16[256,1024]{1,0:T(8,128)(2,1)} %get-tuple-element.53), channel_id=1, source_target_pairs={{0,8},{1,9},{2,10},{3,11},{4,12},{5,13},{6,14},{7,15}} | collective-permute-start | bytes 1572872 | tf_op jit(solution)/shard_map/ppermute | solution.py:57
  127.1 21.0 %collective-permute-start.31 = (bf16[256,1024]{1,0:T(8,128)(2,1)}, bf16[256,1024]{1,0:T(8,128)(2,1)}, u32[]{:S(2)}, u32[]{:S(2)}) collective-permute-start(bf16[256,1024]{1,0:T(8,128)(2,1)} %get-tuple-element.53), channel_id=1, source_target_pairs={{24,16},{25,17},{26,18},{27,19},{28,20},{29,21},{30,22},{31,23}} | collective-permute-start | bytes 1572872 | tf_op jit(solution)/shard_map/ppermute | solution.py:57
  139.9 15.9 %collective-permute-start.22 = (bf16[256,1024]{1,0:T(8,128)(2,1)}, bf16[256,1024]{1,0:T(8,128)(2,1)}, u32[]{:S(2)}, u32[]{:S(2)}) collective-permute-start(bf16[256,1024]{1,0:T(8,128)(2,1)} %get-tuple-element.25), channel_id=1, source_target_pairs={{0,8},{1,9},{2,10},{3,11},{4,12},{5,13},{6,14},{7,15},{8,16},{9,17... | collective-permute-start | bytes 1572872 | tf_op jit(solution)/shard_map/ppermute | solution.py:57
  141.2 18.1 %collective-permute-start.25 = (bf16[256,1024]{1,0:T(8,128)(2,1)}, bf16[256,1024]{1,0:T(8,128)(2,1)}, u32[]{:S(2)}, u32[]{:S(2)}) collective-permute-start(bf16[256,1024]{1,0:T(8,128)(2,1)} %get-tuple-element.26), channel_id=1, source_target_pairs={{16,8},{17,9},{18,10},{19,11},{20,12},{21,13},{22,14},{23,15},{24,... | collective-permute-start | bytes 1572872 | tf_op jit(solution)/shard_map/ppermute | solution.py:57
  150.5 19.4 %collective-permute-start.29 = (bf16[256,1024]{1,0:T(8,128)(2,1)S(1)}, bf16[256,1024]{1,0:T(8,128)(2,1)S(1)}, u32[]{:S(2)}, u32[]{:S(2)}) collective-permute-start(bf16[256,1024]{1,0:T(8,128)(2,1)S(1)} %get-tuple-element.23), channel_id=1, source_target_pairs={{0,8},{1,9},{2,10},{3,11},{4,12},{5,13},{6,14},{7,15},{8,16},{9,17... | collective-permute-start | bytes 1572872 | tf_op jit(solution)/shard_map/ppermute | solution.py:57
  151.8 18.7 %collective-permute-start.32 = (bf16[256,1024]{1,0:T(8,128)(2,1)S(1)}, bf16[256,1024]{1,0:T(8,128)(2,1)S(1)}, u32[]{:S(2)}, u32[]{:S(2)}) collective-permute-start(bf16[256,1024]{1,0:T(8,128)(2,1)S(1)} %get-tuple-element.24), channel_id=1, source_target_pairs={{16,8},{17,9},{18,10},{19,11},{20,12},{21,13},{22,14},{23,15},{24,... | collective-permute-start | bytes 1572872 | tf_op jit(solution)/shard_map/ppermute | solution.py:57
  162.3 14.9 %collective-permute-start.23 = (bf16[256,1024]{1,0:T(8,128)(2,1)}, bf16[256,1024]{1,0:T(8,128)(2,1)}, u32[]{:S(2)}, u32[]{:S(2)}) collective-permute-start(bf16[256,1024]{1,0:T(8,128)(2,1)} %get-tuple-element.21), channel_id=1, source_target_pairs={{0,8},{1,9},{2,10},{3,11},{4,12},{5,13},{6,14},{7,15},{8,16},{9,17... | collective-permute-start | bytes 1572872 | tf_op jit(solution)/shard_map/ppermute | solution.py:57
  164.4 17.4 %collective-permute-start.26 = (bf16[256,1024]{1,0:T(8,128)(2,1)}, bf16[256,1024]{1,0:T(8,128)(2,1)}, u32[]{:S(2)}, u32[]{:S(2)}) collective-permute-start(bf16[256,1024]{1,0:T(8,128)(2,1)} %get-tuple-element.22), channel_id=1, source_target_pairs={{8,0},{9,1},{10,2},{11,3},{12,4},{13,5},{14,6},{15,7},{16,8},{17,9... | collective-permute-start | bytes 1572872 | tf_op jit(solution)/shard_map/ppermute | solution.py:57
  172.0 16.4 %collective-permute-start.30 = (bf16[256,1024]{1,0:T(8,128)(2,1)}, bf16[256,1024]{1,0:T(8,128)(2,1)}, u32[]{:S(2)}, u32[]{:S(2)}) collective-permute-start(bf16[256,1024]{1,0:T(8,128)(2,1)} %get-tuple-element.19), channel_id=1, source_target_pairs={{0,8},{1,9},{2,10},{3,11},{4,12},{5,13},{6,14},{7,15},{8,16},{9,17... | collective-permute-start | bytes 1572872 | tf_op jit(solution)/shard_map/ppermute | solution.py:57
  173.9 19.1 %collective-permute-start.33 = (bf16[256,1024]{1,0:T(8,128)(2,1)}, bf16[256,1024]{1,0:T(8,128)(2,1)}, u32[]{:S(2)}, u32[]{:S(2)}) collective-permute-start(bf16[256,1024]{1,0:T(8,128)(2,1)} %get-tuple-element.20), channel_id=1, source_target_pairs={{8,0},{9,1},{10,2},{11,3},{12,4},{13,5},{14,6},{15,7},{16,8},{17,9... | collective-permute-start | bytes 1572872 | tf_op jit(solution)/shard_map/ppermute | solution.py:57
  (29 other events, 277.6 us)

commit v4 on v3

--- a/solution.py
+++ b/solution.py
@@ -72,15 +72,33 @@
     return route(target)
 
 
+def row_block(stream, x, k):
+    return 2 * (x if stream == 0 else 1 - x) + k
+
+
+def z_hops(part, sign, step):
+    def target(z, x, k, y):
+        source, p = z - sign * (step - 1), part
+        if 0 <= z + sign < 4 and 0 <= source < 4 and source <= 2 * p + k:
+            return (z + sign, x, k, y)
+        return None
+
+    return route(target)
+
+
 def four_planes(integrals, inverse_factor, energies, frequency):
     z = lax.axis_index("pair")
     row = lax.axis_index("row")
     x, k = row // 2, row % 2
     y = lax.axis_index("col")
     chip = 2 * x + y
-    mine = integrals
     n_rows, width = inverse_factor.shape
     piece = n_rows // 4
+
+    def ordered(flag, a, b, axis):
+        return jnp.concatenate(
+            [jnp.where(flag == 0, a, b), jnp.where(flag == 0, b, a)], axis
+        )
 
     own, *others = lax.optimization_barrier(
         [
@@ -88,67 +106,53 @@
             for c in range(4)
         ]
     )
-    got_y, got_x, got_xy = (
-        send(q, r) for q, r in zip(others, (OVER_Y, OVER_X, OVER_XY))
-    )
-
-    half = mine.shape[0] // 2
-    give = lax.dynamic_slice_in_dim(mine, k * half, half, 0)
-    from_y = send(lax.optimization_barrier((give, got_y, got_x, got_xy))[0], OVER_Y)
+    got = [send(q, r) for q, r in zip(others, (OVER_Y, OVER_X, OVER_XY))]
+    same, other = ordered(y, own, got[0], 1), ordered(y, got[1], got[2], 1)
+    parts = [jnp.where(x == 0, same, other), jnp.where(x == 0, other, same)]
+    half = integrals.shape[0] // 2
+    give = lax.dynamic_slice_in_dim(integrals, k * half, half, 0)
+    from_y = send(give, OVER_Y)
     from_core = send(from_y, OVER_CORE)
-    theirs = jnp.concatenate(
-        [jnp.where(k == 0, from_y, from_core), jnp.where(k == 0, from_core, from_y)], 0
-    )
-
-    def by_y(a, b):
-        return jnp.concatenate([jnp.where(y == 0, a, b), jnp.where(y == 0, b, a)], 1)
-
-    same, other = by_y(own, got_y), by_y(got_x, got_xy)
-    parts = [jnp.where(x == 0, same, other), jnp.where(x == 0, other, same)]
-
-    def term(values, plane):
-        at = jnp.clip(plane, 0, 3) * 2 * width
+    theirs = ordered(k, from_y, from_core, 0)
+
+    def term(values, away):
+        at = jnp.clip(z + away, 0, 3) * 2 * width
         return [
             rows_by_rows(lax.dynamic_slice_in_dim(a, at, 2 * width, 1), values)
-            for a in (mine, theirs)
+            for a in (integrals, theirs)
         ]
 
-    totals = [term(parts[p], z) for p in range(2)]
+    came = [[(parts[p], 0)] for p in range(2)]
     moving = [[parts[p], parts[p]] for p in range(2)]
-    for step in range(1, 4):
+    for step in (1, 2, 3):
         for d in (0, 1):
-            sign = 1 - 2 * d
-            for p in range(2):
-
-                def allowed(at, core):
-                    source = at - sign * (step - 1)
-                    return 0 <= source < 4 and source <= 2 * p + core
-
-                pairs = along_z(sign, allowed)
-                if not pairs:
-                    continue
-                moving[p][d] = send(moving[p][d], pairs)
-                more = term(moving[p][d], z - sign * step)
-                totals[p] = [t + m for t, m in zip(totals[p], more)]
-
-    def ordered(a, b):
-        a, b = a.astype(BF16), b.astype(BF16)
-        return jnp.concatenate([jnp.where(y == 0, a, b), jnp.where(y == 0, b, a)], 0)
-
-    low, high = ordered(*totals[0]), ordered(*totals[1])
-
-    low_y, high_y = send(low, OVER_Y), send(high, OVER_Y)
-    low_x, high_x = send(low, OVER_X), send(high, OVER_X)
-    low_xy, high_xy = send(low_y, OVER_X), send(high_x, OVER_Y)
-    lows = [low, low_y, low_x, low_xy]
-    highs = [high, high_y, high_x, high_xy]
-    row_parts = [jnp.where(x == 0, a, b) for a, b in zip(lows, highs)]
-    col_parts = [jnp.where(y == 0, a, b) for a, b in zip(lows, highs)]
-    columns = jnp.concatenate(col_parts, 1)
+            for p in (0, 1):
+                sign = 1 - 2 * d
+                pairs = z_hops(p, sign, step)
+                if pairs:
+                    moving[p][d] = send(moving[p][d], pairs)
+                    came[p].append((moving[p][d], -sign * step))
+    totals = []
+    for p in range(2):
+        total = term(*came[p][0])
+        for value, away in came[p][1:]:
+            total = [t + m for t, m in zip(total, term(value, away))]
+        totals.append(total)
+    straight, across = [
+        ordered(y, t[0].astype(BF16), t[1].astype(BF16), 0) for t in totals
+    ]
+
+    straight_y, across_y = send(straight, OVER_Y), send(across, OVER_Y)
+    straight_x, across_x = send(straight, OVER_X), send(across, OVER_X)
+    straight_xy, across_xy = send(straight_y, OVER_X), send(across_x, OVER_Y)
+    lows = [straight, straight_y, straight_x, straight_xy]
+    highs = [across, across_y, across_x, across_xy]
+    rows = jnp.concatenate([jnp.where(x == 0, a, b) for a, b in zip(lows, highs)], 1)
+    columns = jnp.concatenate(
+        [jnp.where(y == 0, a, b) for a, b in zip(lows, highs)], 1
+    )
     core_columns = send(columns, OVER_CORE)
-
     factor = scale_of(energies, frequency)
-    rows = jnp.concatenate(row_parts, 1)
     scaled = (factor[:, None] * rows.astype(F32)).astype(BF16)
 
     def block(plane, cols):

time: 200 us -> 198 us (0.990)
  transfers between devices with their start and end apart: 34 -> 34, of which waited for: 20 -> 19; matrix products, arithmetic and copies ran while one was open for 23% -> 24% of each run, Pallas kernels for 0% -> 0%
where the time goes in v4:
time: 198 us; the launch traced here: 195 us
  waiting for transfers between devices  72.8 us (37%)
  starting transfers between devices  63.3 us (32%)
  matrix products  38.5 us (19%)
  other arithmetic  14.3 us (7%)
  local copies, waits for them, and re-layouts  4.94 us (2%)
    ppermute x34, waiting for transfers between devices, send(): return lax.ppermute(value, AXES, pairs)  72.8 us
    ppermute x34, starting transfers between devices, send(): return lax.ppermute(value, AXES, pairs)  63.3 us
    dot_general x8, matrix products, columns_by_columns(): lax.dot_general(a, b, (((0,), (0,)), ((), ())), preferred_element_type=F32)  20.3 us
    dot_general x24, matrix products, rows_by_rows(): lax.dot_general(a, b, (((1,), (1,)), ((), ())), preferred_element_type=F32)  18.2 us
  transfers between devices with their start and end apart: 34, of which 19 were waited for; matrix products, arithmetic and copies ran while one was open for 24% of the time, Pallas kernels for 0%

profile of v4, /device:TPU:19, one launch (start us, length us, event | category | flops | bytes accessed | tf_op | source)
XLA Modules:
  0.0 195.3 jit_solution(3871231338442392442)
XLA Ops:
  10.8 5.5 %collective-permute-done.2 = bf16[256,512]{1,0:T(8,128)(2,1)} collective-permute-done((bf16[256,512]{1,0:T(8,128)(2,1)}, bf16[256,512]{1,0:T(8,128)(2,1)}, u32[]{:S(2)}, u32[]{:S(2)}) %collective-permute-start.2) | collective-permute-done | bytes 262176 | tf_op jit(solution)/shard_map/ppermute | solution.py:57
  19.9 3.4 %collective-permute-start.9 = (bf16[256,1024]{1,0:T(8,128)(2,1)}, bf16[256,1024]{1,0:T(8,128)(2,1)}, u32[]{:S(2)}, u32[]{:S(2)}) collective-permute-start(bf16[256,1024]{1,0:T(8,128)(2,1)} %get-tuple-element.25), channel_id=1, source_target_pairs={{0,8},{1,9},{2,10},{3,11},{4,12},{5,13},{6,14},{7,15},{8,16},{9,17... | collective-permute-start | bytes 1572872 | tf_op jit(solution)/shard_map/ppermute | solution.py:57
  24.0 6.0 %collective-permute-start.10 = (bf16[256,1024]{1,0:T(8,128)(2,1)}, bf16[256,1024]{1,0:T(8,128)(2,1)S(1)}, u32[]{:S(2)}, u32[]{:S(2)}) collective-permute-start(bf16[256,1024]{1,0:T(8,128)(2,1)} %get-tuple-element.25), channel_id=1, source_target_pairs={{8,0},{9,1},{10,2},{11,3},{12,4},{13,5},{14,6},{15,7},{16,8},{17,9... | collective-permute-start | bytes 1572872 | tf_op jit(solution)/shard_map/ppermute | solution.py:57
  35.6 4.7 %collective-permute-done.9 = bf16[256,1024]{1,0:T(8,128)(2,1)} collective-permute-done((bf16[256,1024]{1,0:T(8,128)(2,1)}, bf16[256,1024]{1,0:T(8,128)(2,1)}, u32[]{:S(2)}, u32[]{:S(2)}) %collective-permute-start.9) | collective-permute-done | bytes 524320 | tf_op jit(solution)/shard_map/ppermute | solution.py:57
  43.7 4.7 %collective-permute-start.12 = (bf16[256,1024]{1,0:T(8,128)(2,1)S(1)}, bf16[256,1024]{1,0:T(8,128)(2,1)S(1)}, u32[]{:S(2)}, u32[]{:S(2)}) collective-permute-start(bf16[256,1024]{1,0:T(8,128)(2,1)S(1)} %collective-permute-done.10), channel_id=1, source_target_pairs={{8,0},{9,1},{10,2},{11,3},{12,4},{13,5},{14,6},{15,7},{18,10},{19,... | collective-permute-start | bytes 1572872 | tf_op jit(solution)/shard_map/ppermute | solution.py:57
  52.9 3.2 %collective-permute-start.6 = (bf16[256,1024]{1,0:T(8,128)(2,1)S(1)}, bf16[256,1024]{1,0:T(8,128)(2,1)S(1)}, u32[]{:S(2)}, u32[]{:S(2)}) collective-permute-start(bf16[256,1024]{1,0:T(8,128)(2,1)S(1)} %collective-permute-done.5), channel_id=1, source_target_pairs={{16,24},{17,25},{18,26},{19,27},{20,28},{21,29},{22,30},{23,31}} | collective-permute-start | bytes 1572872 | tf_op jit(solution)/shard_map/ppermute | solution.py:57
  56.9 5.3 %collective-permute-done.11 = bf16[256,1024]{1,0:T(8,128)(2,1)S(1)} collective-permute-done((bf16[256,1024]{1,0:T(8,128)(2,1)}, bf16[256,1024]{1,0:T(8,128)(2,1)S(1)}, u32[]{:S(2)}, u32[]{:S(2)}) %collective-permute-start.11) | collective-permute-done | bytes 524320 | tf_op jit(solution)/shard_map/ppermute | solution.py:57
  83.5 6.9 %collective-permute-done.15 = bf16[768,256]{1,0:T(8,128)(2,1)S(1)} collective-permute-done((bf16[768,256]{1,0:T(8,128)(2,1)S(1)}, bf16[768,256]{1,0:T(8,128)(2,1)S(1)}, u32[]{:S(2)}, u32[]{:S(2)}) %collective-permute-start.15) | collective-permute-done | bytes 393248 | tf_op jit(solution)/shard_map/ppermute | solution.py:57
  91.9 6.9 %collective-permute-done.16 = bf16[768,256]{1,0:T(8,128)(2,1)S(1)} collective-permute-done((bf16[768,256]{1,0:T(8,128)(2,1)S(1)}, bf16[768,256]{1,0:T(8,128)(2,1)S(1)}, u32[]{:S(2)}, u32[]{:S(2)}) %collective-permute-start.16) | collective-permute-done | bytes 393248 | tf_op jit(solution)/shard_map/ppermute | solution.py:57
  100.5 7.6 %collective-permute-done.19 = bf16[768,256]{1,0:T(8,128)(2,1)S(1)} collective-permute-done((bf16[768,256]{1,0:T(8,128)(2,1)S(1)}, bf16[768,256]{1,0:T(8,128)(2,1)S(1)}, u32[]{:S(2)}, u32[]{:S(2)}) %collective-permute-start.19) | collective-permute-done | bytes 393248 | tf_op jit(solution)/shard_map/ppermute | solution.py:57
  119.5 3.4 %fusion.110 = (bf16[256,1024]{1,0:T(8,128)(2,1)}, f32[256,1024]{1,0:T(8,128)}) fusion(bf16[768,1024]{1,0:T(8,128)(2,1)} %collective-permute-done.27, bf16[768,1024]{1,0:T(8,128)(2,1)} %copy-done.1, s32[]{:T(128)S(6)} %select_n.266), kind=kOutput, calls=%fused_computation.188 | convolution fusion | flops 402915328 | bytes 3538948 | tf_op jit(solution)/shard_map/dot_general | solution.py:16
  125.6 8.4 %collective-permute-done.24 = bf16[256,1024]{1,0:T(8,128)(2,1)} collective-permute-done((bf16[256,1024]{1,0:T(8,128)(2,1)}, bf16[256,1024]{1,0:T(8,128)(2,1)}, u32[]{:S(2)}, u32[]{:S(2)}) %collective-permute-start.24) | collective-permute-done | bytes 524320 | tf_op jit(solution)/shard_map/ppermute | solution.py:57
  134.1 3.0 %add_convert_fusion.7 = (bf16[256,1024]{1,0:T(8,128)(2,1)}, bf16[256,1024]{1,0:T(8,128)(2,1)}) fusion(bf16[256,1024]{1,0:T(8,128)(2,1)} %collective-permute-done.21, bf16[256,1024]{1,0:T(8,128)(2,1)} %collective-permute-done.24, bf16[768,256]{1,0:T(8,128)(2,1)S(1)} %copy-done.10, bf16[768,256]{1,0:T(8,128)(2,1)S(1)} %copy-done.6, ...), kind=kOutput, calls=%fused_computation.71 | convolution fusion | flops 410517504 | bytes 4063236 | tf_op jit(solution)/shard_map/dot_general | solution.py:16
  138.4 4.0 %collective-permute-start.25 = (bf16[256,1024]{1,0:T(8,128)(2,1)}, bf16[256,1024]{1,0:T(8,128)(2,1)}, u32[]{:S(2)}, u32[]{:S(2)}) collective-permute-start(bf16[256,1024]{1,0:T(8,128)(2,1)} %get-tuple-element.24), channel_id=1, source_target_pairs={{16,8},{17,9},{18,10},{19,11},{20,12},{21,13},{22,14},{23,15},{24,... | collective-permute-start | bytes 1572872 | tf_op jit(solution)/shard_map/ppermute | solution.py:57
  142.5 2.8 %collective-permute-done.31 = bf16[256,1024]{1,0:T(8,128)(2,1)} collective-permute-done((bf16[256,1024]{1,0:T(8,128)(2,1)}, bf16[256,1024]{1,0:T(8,128)(2,1)}, u32[]{:S(2)}, u32[]{:S(2)}) %collective-permute-start.31) | collective-permute-done | bytes 524320 | tf_op jit(solution)/shard_map/ppermute | solution.py:57
  145.3 2.4 %add_convert_fusion.3 = (bf16[256,1024]{1,0:T(8,128)(2,1)S(1)}, bf16[256,1024]{1,0:T(8,128)(2,1)S(1)}) fusion(bf16[256,1024]{1,0:T(8,128)(2,1)} %collective-permute-done.28, bf16[256,1024]{1,0:T(8,128)(2,1)} %collective-permute-done.31, bf16[768,1024]{1,0:T(8,128)(2,1)} %collective-permute-done.27, bf16[768,1024]{1,0:T(8,128)(2,1)} %copy-done.1, ...), kind=kOutput, calls=%fused_computation.67 | convolution fusion | flops 404226048 | bytes 4063236 | tf_op jit(solution)/shard_map/dot_general | solution.py:16
  149.0 4.0 %collective-permute-start.32 = (bf16[256,1024]{1,0:T(8,128)(2,1)S(1)}, bf16[256,1024]{1,0:T(8,128)(2,1)S(1)}, u32[]{:S(2)}, u32[]{:S(2)}) collective-permute-start(bf16[256,1024]{1,0:T(8,128)(2,1)S(1)} %get-tuple-element.22), channel_id=1, source_target_pairs={{16,8},{17,9},{18,10},{19,11},{20,12},{21,13},{22,14},{23,15},{24,... | collective-permute-start | bytes 1572872 | tf_op jit(solution)/shard_map/ppermute | solution.py:57
  153.0 3.5 %collective-permute-done.25 = bf16[256,1024]{1,0:T(8,128)(2,1)} collective-permute-done((bf16[256,1024]{1,0:T(8,128)(2,1)}, bf16[256,1024]{1,0:T(8,128)(2,1)}, u32[]{:S(2)}, u32[]{:S(2)}) %collective-permute-start.25) | collective-permute-done | bytes 524320 | tf_op jit(solution)/shard_map/ppermute | solution.py:57
  156.5 3.0 %add_convert_fusion.6 = (bf16[256,1024]{1,0:T(8,128)(2,1)}, bf16[256,1024]{1,0:T(8,128)(2,1)}) fusion(bf16[256,1024]{1,0:T(8,128)(2,1)} %collective-permute-done.22, f32[256,1024]{1,0:T(8,128)S(1)} %copy-done.18, pred[]{:T(512)S(6)} %eq.15, bf16[256,1024]{1,0:T(8,128)(2,1)} %collective-permute-done.25, pred[]{:T(512)S(6)} %eq.16, ...), kind=kOutput, calls=%fused_computation.70 | convolution fusion | flops 411041792 | bytes 5111814 | tf_op jit(solution)/shard_map/dot_general | solution.py:16
  161.6 3.6 %collective-permute-start.26 = (bf16[256,1024]{1,0:T(8,128)(2,1)}, bf16[256,1024]{1,0:T(8,128)(2,1)}, u32[]{:S(2)}, u32[]{:S(2)}) collective-permute-start(bf16[256,1024]{1,0:T(8,128)(2,1)} %get-tuple-element.20), channel_id=1, source_target_pairs={{8,0},{9,1},{10,2},{11,3},{12,4},{13,5},{14,6},{15,7},{16,8},{17,9... | collective-permute-start | bytes 1572872 | tf_op jit(solution)/shard_map/ppermute | solution.py:57
  171.1 3.3 %collective-permute-start.33 = (bf16[256,1024]{1,0:T(8,128)(2,1)}, bf16[256,1024]{1,0:T(8,128)(2,1)}, u32[]{:S(2)}, u32[]{:S(2)}) collective-permute-start(bf16[256,1024]{1,0:T(8,128)(2,1)} %get-tuple-element.18), channel_id=1, source_target_pairs={{8,0},{9,1},{10,2},{11,3},{12,4},{13,5},{14,6},{15,7},{16,8},{17,9... | collective-permute-start | bytes 1572872 | tf_op jit(solution)/shard_map/ppermute | solution.py:57
  174.5 4.5 %collective-permute-done.26 = bf16[256,1024]{1,0:T(8,128)(2,1)} collective-permute-done((bf16[256,1024]{1,0:T(8,128)(2,1)}, bf16[256,1024]{1,0:T(8,128)(2,1)}, u32[]{:S(2)}, u32[]{:S(2)}) %collective-permute-start.26) | collective-permute-done | bytes 524320 | tf_op jit(solution)/shard_map/ppermute | solution.py:57
  181.3 4.1 %collective-permute-done.30 = bf16[256,1024]{1,0:T(8,128)(2,1)} collective-permute-done((bf16[256,1024]{1,0:T(8,128)(2,1)}, bf16[256,1024]{1,0:T(8,128)(2,1)}, u32[]{:S(2)}, u32[]{:S(2)}) %collective-permute-start.30) | collective-permute-done | bytes 524320 | tf_op jit(solution)/shard_map/ppermute | solution.py:57
  185.4 4.8 %collective-permute-done.33 = bf16[256,1024]{1,0:T(8,128)(2,1)} collective-permute-done((bf16[256,1024]{1,0:T(8,128)(2,1)}, bf16[256,1024]{1,0:T(8,128)(2,1)}, u32[]{:S(2)}, u32[]{:S(2)}) %collective-permute-start.33) | collective-permute-done | bytes 524320 | tf_op jit(solution)/shard_map/ppermute | solution.py:57
  (137 shorter events, 84.6 us)
Async XLA Ops:
  6.2 42.9 %collective-permute-start.7 = (bf16[192,4096]{1,0:T(8,128)(2,1)}, bf16[192,4096]{1,0:T(8,128)(2,1)}, u32[]{:S(2)}, u32[]{:S(2)}) collective-permute-start(bf16[192,4096]{1,0:T(8,128)(2,1)} %constant_dynamic-slice_fusion), channel_id=1, source_target_pairs={{0,1},{1,0},{2,3},{3,2},{4,5},{5,4},{6,7},{7,6},{8,9},{9,8},{10,11... | collective-permute-start | bytes 4718600 | tf_op jit(solution)/shard_map/ppermute | solution.py:57
  19.9 20.5 %collective-permute-start.9 = (bf16[256,1024]{1,0:T(8,128)(2,1)}, bf16[256,1024]{1,0:T(8,128)(2,1)}, u32[]{:S(2)}, u32[]{:S(2)}) collective-permute-start(bf16[256,1024]{1,0:T(8,128)(2,1)} %get-tuple-element.25), channel_id=1, source_target_pairs={{0,8},{1,9},{2,10},{3,11},{4,12},{5,13},{6,14},{7,15},{8,16},{9,17... | collective-permute-start | bytes 1572872 | tf_op jit(solution)/shard_map/ppermute | solution.py:57
  23.3 29.2 %collective-permute-start.4 = (bf16[256,1024]{1,0:T(8,128)(2,1)}, bf16[256,1024]{1,0:T(8,128)(2,1)S(1)}, u32[]{:S(2)}, u32[]{:S(2)}) collective-permute-start(bf16[256,1024]{1,0:T(8,128)(2,1)} %get-tuple-element.26), channel_id=1, source_target_pairs={{10,2},{11,3},{14,6},{15,7}} | collective-permute-start | bytes 1572872 | tf_op jit(solution)/shard_map/ppermute | solution.py:57
  24.0 19.8 %collective-permute-start.10 = (bf16[256,1024]{1,0:T(8,128)(2,1)}, bf16[256,1024]{1,0:T(8,128)(2,1)S(1)}, u32[]{:S(2)}, u32[]{:S(2)}) collective-permute-start(bf16[256,1024]{1,0:T(8,128)(2,1)} %get-tuple-element.25), channel_id=1, source_target_pairs={{8,0},{9,1},{10,2},{11,3},{12,4},{13,5},{14,6},{15,7},{16,8},{17,9... | collective-permute-start | bytes 1572872 | tf_op jit(solution)/shard_map/ppermute | solution.py:57
  30.8 22.1 %collective-permute-start.5 = (bf16[256,1024]{1,0:T(8,128)(2,1)}, bf16[256,1024]{1,0:T(8,128)(2,1)S(1)}, u32[]{:S(2)}, u32[]{:S(2)}) collective-permute-start(bf16[256,1024]{1,0:T(8,128)(2,1)} %collective-permute-done.3), channel_id=1, source_target_pairs={{8,16},{9,17},{10,18},{11,19},{12,20},{13,21},{14,22},{15,23},{18,... | collective-permute-start | bytes 1572872 | tf_op jit(solution)/shard_map/ppermute | solution.py:57
  41.8 20.4 %collective-permute-start.11 = (bf16[256,1024]{1,0:T(8,128)(2,1)}, bf16[256,1024]{1,0:T(8,128)(2,1)S(1)}, u32[]{:S(2)}, u32[]{:S(2)}) collective-permute-start(bf16[256,1024]{1,0:T(8,128)(2,1)} %collective-permute-done.9), channel_id=1, source_target_pairs={{8,16},{9,17},{10,18},{11,19},{12,20},{13,21},{14,22},{15,23},{16,... | collective-permute-start | bytes 1572872 | tf_op jit(solution)/shard_map/ppermute | solution.py:57
  49.1 16.3 %collective-permute-start.8 = (bf16[192,4096]{1,0:T(8,128)(2,1)}, bf16[192,4096]{1,0:T(8,128)(2,1)S(1)}, u32[]{:S(2)}, u32[]{:S(2)}) collective-permute-start(bf16[192,4096]{1,0:T(8,128)(2,1)} %collective-permute-done.7), channel_id=1, source_target_pairs={{0,2},{1,3},{2,0},{3,1},{4,6},{5,7},{6,4},{7,5},{8,10},{9,11},{10,... | collective-permute-start | bytes 4718600 | tf_op jit(solution)/shard_map/ppermute | solution.py:57
  52.9 22.2 %collective-permute-start.6 = (bf16[256,1024]{1,0:T(8,128)(2,1)S(1)}, bf16[256,1024]{1,0:T(8,128)(2,1)S(1)}, u32[]{:S(2)}, u32[]{:S(2)}) collective-permute-start(bf16[256,1024]{1,0:T(8,128)(2,1)S(1)} %collective-permute-done.5), channel_id=1, source_target_pairs={{16,24},{17,25},{18,26},{19,27},{20,28},{21,29},{22,30},{23,31}} | collective-permute-start | bytes 1572872 | tf_op jit(solution)/shard_map/ppermute | solution.py:57
  62.2 16.5 %collective-permute-start.13 = (bf16[256,1024]{1,0:T(8,128)(2,1)S(1)}, bf16[256,1024]{1,0:T(8,128)(2,1)S(1)}, u32[]{:S(2)}, u32[]{:S(2)}) collective-permute-start(bf16[256,1024]{1,0:T(8,128)(2,1)S(1)} %collective-permute-done.11), channel_id=1, source_target_pairs={{16,24},{17,25},{18,26},{19,27},{20,28},{21,29},{22,30},{23,31}} | collective-permute-start | bytes 1572872 | tf_op jit(solution)/shard_map/ppermute | solution.py:57
  82.0 16.8 %collective-permute-start.16 = (bf16[768,256]{1,0:T(8,128)(2,1)S(1)}, bf16[768,256]{1,0:T(8,128)(2,1)S(1)}, u32[]{:S(2)}, u32[]{:S(2)}) collective-permute-start(bf16[768,256]{1,0:T(8,128)(2,1)S(1)} %get-tuple-element.44), channel_id=1, source_target_pairs={{0,1},{1,0},{2,3},{3,2},{4,5},{5,4},{6,7},{7,6},{8,9},{9,8},{10,11... | collective-permute-start | bytes 1179656 | tf_op jit(solution)/shard_map/ppermute | solution.py:57
  82.2 17.5 %collective-permute-start.17 = (bf16[768,256]{1,0:T(8,128)(2,1)S(1)}, bf16[768,256]{1,0:T(8,128)(2,1)S(1)}, u32[]{:S(2)}, u32[]{:S(2)}) collective-permute-start(bf16[768,256]{1,0:T(8,128)(2,1)S(1)} %get-tuple-element.43), channel_id=1, source_target_pairs={{0,4},{1,5},{2,6},{3,7},{4,0},{5,1},{6,2},{7,3},{8,12},{9,13},{10,... | collective-permute-start | bytes 1179656 | tf_op jit(solution)/shard_map/ppermute | solution.py:57
  90.4 17.8 %collective-permute-start.19 = (bf16[768,256]{1,0:T(8,128)(2,1)S(1)}, bf16[768,256]{1,0:T(8,128)(2,1)S(1)}, u32[]{:S(2)}, u32[]{:S(2)}) collective-permute-start(bf16[768,256]{1,0:T(8,128)(2,1)S(1)} %collective-permute-done.15), channel_id=1, source_target_pairs={{0,4},{1,5},{2,6},{3,7},{4,0},{5,1},{6,2},{7,3},{8,12},{9,13},{10,... | collective-permute-start | bytes 1179656 | tf_op jit(solution)/shard_map/ppermute | solution.py:57
  91.3 16.9 %collective-permute-start.20 = (bf16[768,256]{1,0:T(8,128)(2,1)S(1)}, bf16[768,256]{1,0:T(8,128)(2,1)S(1)}, u32[]{:S(2)}, u32[]{:S(2)}) collective-permute-start(bf16[768,256]{1,0:T(8,128)(2,1)S(1)} %collective-permute-done.18), channel_id=1, source_target_pairs={{0,1},{1,0},{2,3},{3,2},{4,5},{5,4},{6,7},{7,6},{8,9},{9,8},{10,11... | collective-permute-start | bytes 1179656 | tf_op jit(solution)/shard_map/ppermute | solution.py:57
  118.1 15.9 %collective-permute-start.24 = (bf16[256,1024]{1,0:T(8,128)(2,1)}, bf16[256,1024]{1,0:T(8,128)(2,1)}, u32[]{:S(2)}, u32[]{:S(2)}) collective-permute-start(bf16[256,1024]{1,0:T(8,128)(2,1)} %get-tuple-element.49), channel_id=1, source_target_pairs={{24,16},{25,17},{26,18},{27,19},{28,20},{29,21},{30,22},{31,23}} | collective-permute-start | bytes 1572872 | tf_op jit(solution)/shard_map/ppermute | solution.py:57
  122.8 19.6 %collective-permute-start.28 = (bf16[256,1024]{1,0:T(8,128)(2,1)}, bf16[256,1024]{1,0:T(8,128)(2,1)}, u32[]{:S(2)}, u32[]{:S(2)}) collective-permute-start(bf16[256,1024]{1,0:T(8,128)(2,1)} %get-tuple-element.51), channel_id=1, source_target_pairs={{0,8},{1,9},{2,10},{3,11},{4,12},{5,13},{6,14},{7,15}} | collective-permute-start | bytes 1572872 | tf_op jit(solution)/shard_map/ppermute | solution.py:57
  124.3 21.0 %collective-permute-start.31 = (bf16[256,1024]{1,0:T(8,128)(2,1)}, bf16[256,1024]{1,0:T(8,128)(2,1)}, u32[]{:S(2)}, u32[]{:S(2)}) collective-permute-start(bf16[256,1024]{1,0:T(8,128)(2,1)} %get-tuple-element.51), channel_id=1, source_target_pairs={{24,16},{25,17},{26,18},{27,19},{28,20},{29,21},{30,22},{31,23}} | collective-permute-start | bytes 1572872 | tf_op jit(solution)/shard_map/ppermute | solution.py:57
  137.1 15.9 %collective-permute-start.22 = (bf16[256,1024]{1,0:T(8,128)(2,1)}, bf16[256,1024]{1,0:T(8,128)(2,1)}, u32[]{:S(2)}, u32[]{:S(2)}) collective-permute-start(bf16[256,1024]{1,0:T(8,128)(2,1)} %get-tuple-element.23), channel_id=1, source_target_pairs={{0,8},{1,9},{2,10},{3,11},{4,12},{5,13},{6,14},{7,15},{8,16},{9,17... | collective-permute-start | bytes 1572872 | tf_op jit(solution)/shard_map/ppermute | solution.py:57
  138.4 18.1 %collective-permute-start.25 = (bf16[256,1024]{1,0:T(8,128)(2,1)}, bf16[256,1024]{1,0:T(8,128)(2,1)}, u32[]{:S(2)}, u32[]{:S(2)}) collective-permute-start(bf16[256,1024]{1,0:T(8,128)(2,1)} %get-tuple-element.24), channel_id=1, source_target_pairs={{16,8},{17,9},{18,10},{19,11},{20,12},{21,13},{22,14},{23,15},{24,... | collective-permute-start | bytes 1572872 | tf_op jit(solution)/shard_map/ppermute | solution.py:57
  147.7 19.4 %collective-permute-start.29 = (bf16[256,1024]{1,0:T(8,128)(2,1)S(1)}, bf16[256,1024]{1,0:T(8,128)(2,1)S(1)}, u32[]{:S(2)}, u32[]{:S(2)}) collective-permute-start(bf16[256,1024]{1,0:T(8,128)(2,1)S(1)} %get-tuple-element.21), channel_id=1, source_target_pairs={{0,8},{1,9},{2,10},{3,11},{4,12},{5,13},{6,14},{7,15},{8,16},{9,17... | collective-permute-start | bytes 1572872 | tf_op jit(solution)/shard_map/ppermute | solution.py:57
  149.0 18.7 %collective-permute-start.32 = (bf16[256,1024]{1,0:T(8,128)(2,1)S(1)}, bf16[256,1024]{1,0:T(8,128)(2,1)S(1)}, u32[]{:S(2)}, u32[]{:S(2)}) collective-permute-start(bf16[256,1024]{1,0:T(8,128)(2,1)S(1)} %get-tuple-element.22), channel_id=1, source_target_pairs={{16,8},{17,9},{18,10},{19,11},{20,12},{21,13},{22,14},{23,15},{24,... | collective-permute-start | bytes 1572872 | tf_op jit(solution)/shard_map/ppermute | solution.py:57
  159.5 14.9 %collective-permute-start.23 = (bf16[256,1024]{1,0:T(8,128)(2,1)}, bf16[256,1024]{1,0:T(8,128)(2,1)}, u32[]{:S(2)}, u32[]{:S(2)}) collective-permute-start(bf16[256,1024]{1,0:T(8,128)(2,1)} %get-tuple-element.19), channel_id=1, source_target_pairs={{0,8},{1,9},{2,10},{3,11},{4,12},{5,13},{6,14},{7,15},{8,16},{9,17... | collective-permute-start | bytes 1572872 | tf_op jit(solution)/shard_map/ppermute | solution.py:57
  161.6 17.4 %collective-permute-start.26 = (bf16[256,1024]{1,0:T(8,128)(2,1)}, bf16[256,1024]{1,0:T(8,128)(2,1)}, u32[]{:S(2)}, u32[]{:S(2)}) collective-permute-start(bf16[256,1024]{1,0:T(8,128)(2,1)} %get-tuple-element.20), channel_id=1, source_target_pairs={{8,0},{9,1},{10,2},{11,3},{12,4},{13,5},{14,6},{15,7},{16,8},{17,9... | collective-permute-start | bytes 1572872 | tf_op jit(solution)/shard_map/ppermute | solution.py:57
  169.2 16.3 %collective-permute-start.30 = (bf16[256,1024]{1,0:T(8,128)(2,1)}, bf16[256,1024]{1,0:T(8,128)(2,1)}, u32[]{:S(2)}, u32[]{:S(2)}) collective-permute-start(bf16[256,1024]{1,0:T(8,128)(2,1)} %get-tuple-element.17), channel_id=1, source_target_pairs={{0,8},{1,9},{2,10},{3,11},{4,12},{5,13},{6,14},{7,15},{8,16},{9,17... | collective-permute-start | bytes 1572872 | tf_op jit(solution)/shard_map/ppermute | solution.py:57
  171.1 19.1 %collective-permute-start.33 = (bf16[256,1024]{1,0:T(8,128)(2,1)}, bf16[256,1024]{1,0:T(8,128)(2,1)}, u32[]{:S(2)}, u32[]{:S(2)}) collective-permute-start(bf16[256,1024]{1,0:T(8,128)(2,1)} %get-tuple-element.18), channel_id=1, source_target_pairs={{8,0},{9,1},{10,2},{11,3},{12,4},{13,5},{14,6},{15,7},{16,8},{17,9... | collective-permute-start | bytes 1572872 | tf_op jit(solution)/shard_map/ppermute | solution.py:57
  (29 other events, 277.9 us)

commit v5 on v4

--- a/solution.py
+++ b/solution.py
@@ -178,15 +178,12 @@
         right, left = send(right, to_right(3)), send(left, to_left(3))
         return block(z, cols) + right.astype(F32) + left.astype(F32)
 
-    sums = jnp.stack([summed(columns), summed(core_columns)])
-    out = [
-        lax.dynamic_slice(
-            sums, (c ^ k, 0, (q ^ chip) * piece), (1, piece, piece)
-        ).reshape(piece, piece)
-        for c in range(2)
-        for q in range(4)
-    ]
-    return jnp.concatenate(out, 1)
+    out = []
+    for part in (summed(columns), summed(core_columns)):
+        a = [part[:, q * piece : (q + 1) * piece] for q in range(4)]
+        a = [jnp.where(y == 0, a[q], a[q ^ 1]) for q in range(4)]
+        out.append(jnp.concatenate([jnp.where(x == 0, a[q], a[q ^ 2]) for q in range(4)], 1))
+    return ordered(k, *out, 1)
 
 
 def solution(mesh):

time: 198 us -> 195 us (0.985)
  waiting for transfers between devices: 72.8 us -> 76.3 us
  matrix products: 38.5 us -> 35.5 us
    ppermute x34, waiting for transfers between devices: 72.8 us -> 76.3 us  [send(): return lax.ppermute(value, AXES, pairs)]
    dot_general x8, matrix products: 20.3 us -> 17.3 us  [columns_by_columns(): lax.dot_general(a, b, (((0,), (0,)), ((), ())), preferred_element_type=F32)]
  transfers between devices with their start and end apart: 34 -> 34, of which waited for: 19 -> 20; matrix products, arithmetic and copies ran while one was open for 24% -> 22% of each run, Pallas kernels for 0% -> 0%
where the time goes in v5:
time: 195 us; the launch traced here: 194 us
  waiting for transfers between devices  76.3 us (39%)
  starting transfers between devices  63.4 us (33%)
  matrix products  35.5 us (18%)
  other arithmetic  14 us (7%)
  local copies, waits for them, and re-layouts  3.62 us (2%)
    ppermute x34, waiting for transfers between devices, send(): return lax.ppermute(value, AXES, pairs)  76.3 us
    ppermute x34, starting transfers between devices, send(): return lax.ppermute(value, AXES, pairs)  63.4 us
    dot_general x24, matrix products, rows_by_rows(): lax.dot_general(a, b, (((1,), (1,)), ((), ())), preferred_element_type=F32)  18.2 us
    dot_general x8, matrix products, columns_by_columns(): lax.dot_general(a, b, (((0,), (0,)), ((), ())), preferred_element_type=F32)  17.3 us
  transfers between devices with their start and end apart: 34, of which 20 were waited for; matrix products, arithmetic and copies ran while one was open for 22% of the time, Pallas kernels for 0%

profile of v5, /device:TPU:19, one launch (start us, length us, event | category | flops | bytes accessed | tf_op | source)
XLA Modules:
  0.0 194.2 jit_solution(12976430484400129743)
XLA Ops:
  10.7 5.5 %collective-permute-done.2 = bf16[256,512]{1,0:T(8,128)(2,1)} collective-permute-done((bf16[256,512]{1,0:T(8,128)(2,1)}, bf16[256,512]{1,0:T(8,128)(2,1)}, u32[]{:S(2)}, u32[]{:S(2)}) %collective-permute-start.2) | collective-permute-done | bytes 262176 | tf_op jit(solution)/shard_map/ppermute | solution.py:57
  19.8 3.4 %collective-permute-start.9 = (bf16[256,1024]{1,0:T(8,128)(2,1)}, bf16[256,1024]{1,0:T(8,128)(2,1)}, u32[]{:S(2)}, u32[]{:S(2)}) collective-permute-start(bf16[256,1024]{1,0:T(8,128)(2,1)} %get-tuple-element.35), channel_id=1, source_target_pairs={{0,8},{1,9},{2,10},{3,11},{4,12},{5,13},{6,14},{7,15},{8,16},{9,17... | collective-permute-start | bytes 1572872 | tf_op jit(solution)/shard_map/ppermute | solution.py:57
  24.0 6.0 %collective-permute-start.10 = (bf16[256,1024]{1,0:T(8,128)(2,1)}, bf16[256,1024]{1,0:T(8,128)(2,1)S(1)}, u32[]{:S(2)}, u32[]{:S(2)}) collective-permute-start(bf16[256,1024]{1,0:T(8,128)(2,1)} %get-tuple-element.35), channel_id=1, source_target_pairs={{8,0},{9,1},{10,2},{11,3},{12,4},{13,5},{14,6},{15,7},{16,8},{17,9... | collective-permute-start | bytes 1572872 | tf_op jit(solution)/shard_map/ppermute | solution.py:57
  35.6 4.7 %collective-permute-done.9 = bf16[256,1024]{1,0:T(8,128)(2,1)} collective-permute-done((bf16[256,1024]{1,0:T(8,128)(2,1)}, bf16[256,1024]{1,0:T(8,128)(2,1)}, u32[]{:S(2)}, u32[]{:S(2)}) %collective-permute-start.9) | collective-permute-done | bytes 524320 | tf_op jit(solution)/shard_map/ppermute | solution.py:57
  43.7 4.7 %collective-permute-start.12 = (bf16[256,1024]{1,0:T(8,128)(2,1)S(1)}, bf16[256,1024]{1,0:T(8,128)(2,1)S(1)}, u32[]{:S(2)}, u32[]{:S(2)}) collective-permute-start(bf16[256,1024]{1,0:T(8,128)(2,1)S(1)} %collective-permute-done.10), channel_id=1, source_target_pairs={{8,0},{9,1},{10,2},{11,3},{12,4},{13,5},{14,6},{15,7},{18,10},{19,... | collective-permute-start | bytes 1572872 | tf_op jit(solution)/shard_map/ppermute | solution.py:57
  52.9 3.2 %collective-permute-start.6 = (bf16[256,1024]{1,0:T(8,128)(2,1)S(1)}, bf16[256,1024]{1,0:T(8,128)(2,1)S(1)}, u32[]{:S(2)}, u32[]{:S(2)}) collective-permute-start(bf16[256,1024]{1,0:T(8,128)(2,1)S(1)} %collective-permute-done.5), channel_id=1, source_target_pairs={{16,24},{17,25},{18,26},{19,27},{20,28},{21,29},{22,30},{23,31}} | collective-permute-start | bytes 1572872 | tf_op jit(solution)/shard_map/ppermute | solution.py:57
  56.9 5.3 %collective-permute-done.11 = bf16[256,1024]{1,0:T(8,128)(2,1)S(1)} collective-permute-done((bf16[256,1024]{1,0:T(8,128)(2,1)}, bf16[256,1024]{1,0:T(8,128)(2,1)S(1)}, u32[]{:S(2)}, u32[]{:S(2)}) %collective-permute-start.11) | collective-permute-done | bytes 524320 | tf_op jit(solution)/shard_map/ppermute | solution.py:57
  76.3 2.3 %collective-permute-done.13 = bf16[256,1024]{1,0:T(8,128)(2,1)S(1)} collective-permute-done((bf16[256,1024]{1,0:T(8,128)(2,1)S(1)}, bf16[256,1024]{1,0:T(8,128)(2,1)S(1)}, u32[]{:S(2)}, u32[]{:S(2)}) %collective-permute-start.13) | collective-permute-done | bytes 524320 | tf_op jit(solution)/shard_map/ppermute | solution.py:57
  83.5 6.9 %collective-permute-done.15 = bf16[768,256]{1,0:T(8,128)(2,1)S(1)} collective-permute-done((bf16[768,256]{1,0:T(8,128)(2,1)S(1)}, bf16[768,256]{1,0:T(8,128)(2,1)S(1)}, u32[]{:S(2)}, u32[]{:S(2)}) %collective-permute-start.15) | collective-permute-done | bytes 393248 | tf_op jit(solution)/shard_map/ppermute | solution.py:57
  91.9 6.9 %collective-permute-done.16 = bf16[768,256]{1,0:T(8,128)(2,1)S(1)} collective-permute-done((bf16[768,256]{1,0:T(8,128)(2,1)S(1)}, bf16[768,256]{1,0:T(8,128)(2,1)S(1)}, u32[]{:S(2)}, u32[]{:S(2)}) %collective-permute-start.16) | collective-permute-done | bytes 393248 | tf_op jit(solution)/shard_map/ppermute | solution.py:57
  100.5 7.6 %collective-permute-done.19 = bf16[768,256]{1,0:T(8,128)(2,1)S(1)} collective-permute-done((bf16[768,256]{1,0:T(8,128)(2,1)S(1)}, bf16[768,256]{1,0:T(8,128)(2,1)S(1)}, u32[]{:S(2)}, u32[]{:S(2)}) %collective-permute-start.19) | collective-permute-done | bytes 393248 | tf_op jit(solution)/shard_map/ppermute | solution.py:57
  119.5 3.4 %fusion.85 = (bf16[256,1024]{1,0:T(8,128)(2,1)}, f32[256,1024]{1,0:T(8,128)}) fusion(bf16[768,1024]{1,0:T(8,128)(2,1)} %collective-permute-done.27, bf16[768,1024]{1,0:T(8,128)(2,1)} %copy-done.1, s32[]{:T(128)S(6)} %select_n.329), kind=kOutput, calls=%fused_computation.166 | convolution fusion | flops 402915328 | bytes 3538948 | tf_op jit(solution)/shard_map/dot_general | solution.py:16
  125.7 8.5 %collective-permute-done.24 = bf16[256,1024]{1,0:T(8,128)(2,1)} collective-permute-done((bf16[256,1024]{1,0:T(8,128)(2,1)}, bf16[256,1024]{1,0:T(8,128)(2,1)}, u32[]{:S(2)}, u32[]{:S(2)}) %collective-permute-start.24) | collective-permute-done | bytes 524320 | tf_op jit(solution)/shard_map/ppermute | solution.py:57
  134.2 3.1 %add_convert_fusion.7 = (bf16[256,1024]{1,0:T(8,128)(2,1)}, bf16[256,1024]{1,0:T(8,128)(2,1)}) fusion(bf16[256,1024]{1,0:T(8,128)(2,1)} %collective-permute-done.21, bf16[256,1024]{1,0:T(8,128)(2,1)} %collective-permute-done.24, bf16[768,256]{1,0:T(8,128)(2,1)S(1)} %copy-done.10, bf16[768,256]{1,0:T(8,128)(2,1)S(1)} %copy-done.6, ...), kind=kOutput, calls=%fused_computation.56 | convolution fusion | flops 410517504 | bytes 4063236 | tf_op jit(solution)/shard_map/dot_general | solution.py:16
  138.5 4.0 %collective-permute-start.25 = (bf16[256,1024]{1,0:T(8,128)(2,1)}, bf16[256,1024]{1,0:T(8,128)(2,1)}, u32[]{:S(2)}, u32[]{:S(2)}) collective-permute-start(bf16[256,1024]{1,0:T(8,128)(2,1)} %get-tuple-element.28), channel_id=1, source_target_pairs={{16,8},{17,9},{18,10},{19,11},{20,12},{21,13},{22,14},{23,15},{24,... | collective-permute-start | bytes 1572872 | tf_op jit(solution)/shard_map/ppermute | solution.py:57
  142.6 2.8 %collective-permute-done.31 = bf16[256,1024]{1,0:T(8,128)(2,1)} collective-permute-done((bf16[256,1024]{1,0:T(8,128)(2,1)}, bf16[256,1024]{1,0:T(8,128)(2,1)}, u32[]{:S(2)}, u32[]{:S(2)}) %collective-permute-start.31) | collective-permute-done | bytes 524320 | tf_op jit(solution)/shard_map/ppermute | solution.py:57
  145.4 2.4 %add_convert_fusion.3 = (bf16[256,1024]{1,0:T(8,128)(2,1)S(1)}, bf16[256,1024]{1,0:T(8,128)(2,1)S(1)}) fusion(bf16[256,1024]{1,0:T(8,128)(2,1)} %collective-permute-done.28, bf16[256,1024]{1,0:T(8,128)(2,1)} %collective-permute-done.31, bf16[768,1024]{1,0:T(8,128)(2,1)} %collective-permute-done.27, bf16[768,1024]{1,0:T(8,128)(2,1)} %copy-done.1, ...), kind=kOutput, calls=%fused_computation.52 | convolution fusion | flops 404226048 | bytes 4063236 | tf_op jit(solution)/shard_map/dot_general | solution.py:16
  149.1 4.0 %collective-permute-start.32 = (bf16[256,1024]{1,0:T(8,128)(2,1)S(1)}, bf16[256,1024]{1,0:T(8,128)(2,1)S(1)}, u32[]{:S(2)}, u32[]{:S(2)}) collective-permute-start(bf16[256,1024]{1,0:T(8,128)(2,1)S(1)} %get-tuple-element.34), channel_id=1, source_target_pairs={{16,8},{17,9},{18,10},{19,11},{20,12},{21,13},{22,14},{23,15},{24,... | collective-permute-start | bytes 1572872 | tf_op jit(solution)/shard_map/ppermute | solution.py:57
  153.1 3.5 %collective-permute-done.25 = bf16[256,1024]{1,0:T(8,128)(2,1)} collective-permute-done((bf16[256,1024]{1,0:T(8,128)(2,1)}, bf16[256,1024]{1,0:T(8,128)(2,1)}, u32[]{:S(2)}, u32[]{:S(2)}) %collective-permute-start.25) | collective-permute-done | bytes 524320 | tf_op jit(solution)/shard_map/ppermute | solution.py:57
  160.7 3.6 %collective-permute-start.26 = (bf16[256,1024]{1,0:T(8,128)(2,1)S(1)}, bf16[256,1024]{1,0:T(8,128)(2,1)S(1)}, u32[]{:S(2)}, u32[]{:S(2)}) collective-permute-start(bf16[256,1024]{1,0:T(8,128)(2,1)S(1)} %get-tuple-element.20), channel_id=1, source_target_pairs={{8,0},{9,1},{10,2},{11,3},{12,4},{13,5},{14,6},{15,7},{16,8},{17,9... | collective-permute-start | bytes 1572872 | tf_op jit(solution)/shard_map/ppermute | solution.py:57
  170.1 3.4 %collective-permute-start.33 = (bf16[256,1024]{1,0:T(8,128)(2,1)S(1)}, bf16[256,1024]{1,0:T(8,128)(2,1)S(1)}, u32[]{:S(2)}, u32[]{:S(2)}) collective-permute-start(bf16[256,1024]{1,0:T(8,128)(2,1)S(1)} %get-tuple-element.22), channel_id=1, source_target_pairs={{8,0},{9,1},{10,2},{11,3},{12,4},{13,5},{14,6},{15,7},{16,8},{17,9... | collective-permute-start | bytes 1572872 | tf_op jit(solution)/shard_map/ppermute | solution.py:57
  175.0 4.0 %collective-permute-done.26 = bf16[256,1024]{1,0:T(8,128)(2,1)S(1)} collective-permute-done((bf16[256,1024]{1,0:T(8,128)(2,1)S(1)}, bf16[256,1024]{1,0:T(8,128)(2,1)S(1)}, u32[]{:S(2)}, u32[]{:S(2)}) %collective-permute-start.26) | collective-permute-done | bytes 524320 | tf_op jit(solution)/shard_map/ppermute | solution.py:57
  179.7 6.5 %collective-permute-done.30 = bf16[256,1024]{1,0:T(8,128)(2,1)S(1)} collective-permute-done((bf16[256,1024]{1,0:T(8,128)(2,1)S(1)}, bf16[256,1024]{1,0:T(8,128)(2,1)S(1)}, u32[]{:S(2)}, u32[]{:S(2)}) %collective-permute-start.30) | collective-permute-done | bytes 524320 | tf_op jit(solution)/shard_map/ppermute | solution.py:57
  186.2 4.0 %collective-permute-done.33 = bf16[256,1024]{1,0:T(8,128)(2,1)S(1)} collective-permute-done((bf16[256,1024]{1,0:T(8,128)(2,1)S(1)}, bf16[256,1024]{1,0:T(8,128)(2,1)S(1)}, u32[]{:S(2)}, u32[]{:S(2)}) %collective-permute-start.33) | collective-permute-done | bytes 524320 | tf_op jit(solution)/shard_map/ppermute | solution.py:57
  (131 shorter events, 83.0 us)
Async XLA Ops:
  6.2 42.9 %collective-permute-start.7 = (bf16[192,4096]{1,0:T(8,128)(2,1)}, bf16[192,4096]{1,0:T(8,128)(2,1)}, u32[]{:S(2)}, u32[]{:S(2)}) collective-permute-start(bf16[192,4096]{1,0:T(8,128)(2,1)} %constant_dynamic-slice_fusion), channel_id=1, source_target_pairs={{0,1},{1,0},{2,3},{3,2},{4,5},{5,4},{6,7},{7,6},{8,9},{9,8},{10,11... | collective-permute-start | bytes 4718600 | tf_op jit(solution)/shard_map/ppermute | solution.py:57
  19.8 20.5 %collective-permute-start.9 = (bf16[256,1024]{1,0:T(8,128)(2,1)}, bf16[256,1024]{1,0:T(8,128)(2,1)}, u32[]{:S(2)}, u32[]{:S(2)}) collective-permute-start(bf16[256,1024]{1,0:T(8,128)(2,1)} %get-tuple-element.35), channel_id=1, source_target_pairs={{0,8},{1,9},{2,10},{3,11},{4,12},{5,13},{6,14},{7,15},{8,16},{9,17... | collective-permute-start | bytes 1572872 | tf_op jit(solution)/shard_map/ppermute | solution.py:57
  23.3 29.2 %collective-permute-start.4 = (bf16[256,1024]{1,0:T(8,128)(2,1)}, bf16[256,1024]{1,0:T(8,128)(2,1)S(1)}, u32[]{:S(2)}, u32[]{:S(2)}) collective-permute-start(bf16[256,1024]{1,0:T(8,128)(2,1)} %get-tuple-element.36), channel_id=1, source_target_pairs={{10,2},{11,3},{14,6},{15,7}} | collective-permute-start | bytes 1572872 | tf_op jit(solution)/shard_map/ppermute | solution.py:57
  24.0 19.7 %collective-permute-start.10 = (bf16[256,1024]{1,0:T(8,128)(2,1)}, bf16[256,1024]{1,0:T(8,128)(2,1)S(1)}, u32[]{:S(2)}, u32[]{:S(2)}) collective-permute-start(bf16[256,1024]{1,0:T(8,128)(2,1)} %get-tuple-element.35), channel_id=1, source_target_pairs={{8,0},{9,1},{10,2},{11,3},{12,4},{13,5},{14,6},{15,7},{16,8},{17,9... | collective-permute-start | bytes 1572872 | tf_op jit(solution)/shard_map/ppermute | solution.py:57
  30.8 22.1 %collective-permute-start.5 = (bf16[256,1024]{1,0:T(8,128)(2,1)}, bf16[256,1024]{1,0:T(8,128)(2,1)S(1)}, u32[]{:S(2)}, u32[]{:S(2)}) collective-permute-start(bf16[256,1024]{1,0:T(8,128)(2,1)} %collective-permute-done.3), channel_id=1, source_target_pairs={{8,16},{9,17},{10,18},{11,19},{12,20},{13,21},{14,22},{15,23},{18,... | collective-permute-start | bytes 1572872 | tf_op jit(solution)/shard_map/ppermute | solution.py:57
  41.8 20.4 %collective-permute-start.11 = (bf16[256,1024]{1,0:T(8,128)(2,1)}, bf16[256,1024]{1,0:T(8,128)(2,1)S(1)}, u32[]{:S(2)}, u32[]{:S(2)}) collective-permute-start(bf16[256,1024]{1,0:T(8,128)(2,1)} %collective-permute-done.9), channel_id=1, source_target_pairs={{8,16},{9,17},{10,18},{11,19},{12,20},{13,21},{14,22},{15,23},{16,... | collective-permute-start | bytes 1572872 | tf_op jit(solution)/shard_map/ppermute | solution.py:57
  49.1 16.3 %collective-permute-start.8 = (bf16[192,4096]{1,0:T(8,128)(2,1)}, bf16[192,4096]{1,0:T(8,128)(2,1)S(1)}, u32[]{:S(2)}, u32[]{:S(2)}) collective-permute-start(bf16[192,4096]{1,0:T(8,128)(2,1)} %collective-permute-done.7), channel_id=1, source_target_pairs={{0,2},{1,3},{2,0},{3,1},{4,6},{5,7},{6,4},{7,5},{8,10},{9,11},{10,... | collective-permute-start | bytes 4718600 | tf_op jit(solution)/shard_map/ppermute | solution.py:57
  52.9 22.2 %collective-permute-start.6 = (bf16[256,1024]{1,0:T(8,128)(2,1)S(1)}, bf16[256,1024]{1,0:T(8,128)(2,1)S(1)}, u32[]{:S(2)}, u32[]{:S(2)}) collective-permute-start(bf16[256,1024]{1,0:T(8,128)(2,1)S(1)} %collective-permute-done.5), channel_id=1, source_target_pairs={{16,24},{17,25},{18,26},{19,27},{20,28},{21,29},{22,30},{23,31}} | collective-permute-start | bytes 1572872 | tf_op jit(solution)/shard_map/ppermute | solution.py:57
  62.2 16.5 %collective-permute-start.13 = (bf16[256,1024]{1,0:T(8,128)(2,1)S(1)}, bf16[256,1024]{1,0:T(8,128)(2,1)S(1)}, u32[]{:S(2)}, u32[]{:S(2)}) collective-permute-start(bf16[256,1024]{1,0:T(8,128)(2,1)S(1)} %collective-permute-done.11), channel_id=1, source_target_pairs={{16,24},{17,25},{18,26},{19,27},{20,28},{21,29},{22,30},{23,31}} | collective-permute-start | bytes 1572872 | tf_op jit(solution)/shard_map/ppermute | solution.py:57
  82.0 16.8 %collective-permute-start.16 = (bf16[768,256]{1,0:T(8,128)(2,1)S(1)}, bf16[768,256]{1,0:T(8,128)(2,1)S(1)}, u32[]{:S(2)}, u32[]{:S(2)}) collective-permute-start(bf16[768,256]{1,0:T(8,128)(2,1)S(1)} %get-tuple-element.54), channel_id=1, source_target_pairs={{0,1},{1,0},{2,3},{3,2},{4,5},{5,4},{6,7},{7,6},{8,9},{9,8},{10,11... | collective-permute-start | bytes 1179656 | tf_op jit(solution)/shard_map/ppermute | solution.py:57
  82.3 17.5 %collective-permute-start.17 = (bf16[768,256]{1,0:T(8,128)(2,1)S(1)}, bf16[768,256]{1,0:T(8,128)(2,1)S(1)}, u32[]{:S(2)}, u32[]{:S(2)}) collective-permute-start(bf16[768,256]{1,0:T(8,128)(2,1)S(1)} %get-tuple-element.53), channel_id=1, source_target_pairs={{0,4},{1,5},{2,6},{3,7},{4,0},{5,1},{6,2},{7,3},{8,12},{9,13},{10,... | collective-permute-start | bytes 1179656 | tf_op jit(solution)/shard_map/ppermute | solution.py:57
  90.4 17.8 %collective-permute-start.19 = (bf16[768,256]{1,0:T(8,128)(2,1)S(1)}, bf16[768,256]{1,0:T(8,128)(2,1)S(1)}, u32[]{:S(2)}, u32[]{:S(2)}) collective-permute-start(bf16[768,256]{1,0:T(8,128)(2,1)S(1)} %collective-permute-done.15), channel_id=1, source_target_pairs={{0,4},{1,5},{2,6},{3,7},{4,0},{5,1},{6,2},{7,3},{8,12},{9,13},{10,... | collective-permute-start | bytes 1179656 | tf_op jit(solution)/shard_map/ppermute | solution.py:57
  91.3 16.9 %collective-permute-start.20 = (bf16[768,256]{1,0:T(8,128)(2,1)S(1)}, bf16[768,256]{1,0:T(8,128)(2,1)S(1)}, u32[]{:S(2)}, u32[]{:S(2)}) collective-permute-start(bf16[768,256]{1,0:T(8,128)(2,1)S(1)} %collective-permute-done.18), channel_id=1, source_target_pairs={{0,1},{1,0},{2,3},{3,2},{4,5},{5,4},{6,7},{7,6},{8,9},{9,8},{10,11... | collective-permute-start | bytes 1179656 | tf_op jit(solution)/shard_map/ppermute | solution.py:57
  118.2 16.0 %collective-permute-start.24 = (bf16[256,1024]{1,0:T(8,128)(2,1)}, bf16[256,1024]{1,0:T(8,128)(2,1)}, u32[]{:S(2)}, u32[]{:S(2)}) collective-permute-start(bf16[256,1024]{1,0:T(8,128)(2,1)} %get-tuple-element.61), channel_id=1, source_target_pairs={{24,16},{25,17},{26,18},{27,19},{28,20},{29,21},{30,22},{31,23}} | collective-permute-start | bytes 1572872 | tf_op jit(solution)/shard_map/ppermute | solution.py:57
  122.9 19.7 %collective-permute-start.28 = (bf16[256,1024]{1,0:T(8,128)(2,1)}, bf16[256,1024]{1,0:T(8,128)(2,1)}, u32[]{:S(2)}, u32[]{:S(2)}) collective-permute-start(bf16[256,1024]{1,0:T(8,128)(2,1)} %get-tuple-element.59), channel_id=1, source_target_pairs={{0,8},{1,9},{2,10},{3,11},{4,12},{5,13},{6,14},{7,15}} | collective-permute-start | bytes 1572872 | tf_op jit(solution)/shard_map/ppermute | solution.py:57
  124.4 21.0 %collective-permute-start.31 = (bf16[256,1024]{1,0:T(8,128)(2,1)}, bf16[256,1024]{1,0:T(8,128)(2,1)}, u32[]{:S(2)}, u32[]{:S(2)}) collective-permute-start(bf16[256,1024]{1,0:T(8,128)(2,1)} %get-tuple-element.59), channel_id=1, source_target_pairs={{24,16},{25,17},{26,18},{27,19},{28,20},{29,21},{30,22},{31,23}} | collective-permute-start | bytes 1572872 | tf_op jit(solution)/shard_map/ppermute | solution.py:57
  137.2 15.9 %collective-permute-start.22 = (bf16[256,1024]{1,0:T(8,128)(2,1)}, bf16[256,1024]{1,0:T(8,128)(2,1)}, u32[]{:S(2)}, u32[]{:S(2)}) collective-permute-start(bf16[256,1024]{1,0:T(8,128)(2,1)} %get-tuple-element.27), channel_id=1, source_target_pairs={{0,8},{1,9},{2,10},{3,11},{4,12},{5,13},{6,14},{7,15},{8,16},{9,17... | collective-permute-start | bytes 1572872 | tf_op jit(solution)/shard_map/ppermute | solution.py:57
  138.5 18.1 %collective-permute-start.25 = (bf16[256,1024]{1,0:T(8,128)(2,1)}, bf16[256,1024]{1,0:T(8,128)(2,1)}, u32[]{:S(2)}, u32[]{:S(2)}) collective-permute-start(bf16[256,1024]{1,0:T(8,128)(2,1)} %get-tuple-element.28), channel_id=1, source_target_pairs={{16,8},{17,9},{18,10},{19,11},{20,12},{21,13},{22,14},{23,15},{24,... | collective-permute-start | bytes 1572872 | tf_op jit(solution)/shard_map/ppermute | solution.py:57
  147.8 18.4 %collective-permute-start.29 = (bf16[256,1024]{1,0:T(8,128)(2,1)S(1)}, bf16[256,1024]{1,0:T(8,128)(2,1)S(1)}, u32[]{:S(2)}, u32[]{:S(2)}) collective-permute-start(bf16[256,1024]{1,0:T(8,128)(2,1)S(1)} %get-tuple-element.33), channel_id=1, source_target_pairs={{0,8},{1,9},{2,10},{3,11},{4,12},{5,13},{6,14},{7,15},{8,16},{9,17... | collective-permute-start | bytes 1572872 | tf_op jit(solution)/shard_map/ppermute | solution.py:57
  149.1 18.6 %collective-permute-start.32 = (bf16[256,1024]{1,0:T(8,128)(2,1)S(1)}, bf16[256,1024]{1,0:T(8,128)(2,1)S(1)}, u32[]{:S(2)}, u32[]{:S(2)}) collective-permute-start(bf16[256,1024]{1,0:T(8,128)(2,1)S(1)} %get-tuple-element.34), channel_id=1, source_target_pairs={{16,8},{17,9},{18,10},{19,11},{20,12},{21,13},{22,14},{23,15},{24,... | collective-permute-start | bytes 1572872 | tf_op jit(solution)/shard_map/ppermute | solution.py:57
  158.6 16.4 %collective-permute-start.23 = (bf16[256,1024]{1,0:T(8,128)(2,1)S(1)}, bf16[256,1024]{1,0:T(8,128)(2,1)S(1)}, u32[]{:S(2)}, u32[]{:S(2)}) collective-permute-start(bf16[256,1024]{1,0:T(8,128)(2,1)S(1)} %get-tuple-element.19), channel_id=1, source_target_pairs={{0,8},{1,9},{2,10},{3,11},{4,12},{5,13},{6,14},{7,15},{8,16},{9,17... | collective-permute-start | bytes 1572872 | tf_op jit(solution)/shard_map/ppermute | solution.py:57
  160.7 18.3 %collective-permute-start.26 = (bf16[256,1024]{1,0:T(8,128)(2,1)S(1)}, bf16[256,1024]{1,0:T(8,128)(2,1)S(1)}, u32[]{:S(2)}, u32[]{:S(2)}) collective-permute-start(bf16[256,1024]{1,0:T(8,128)(2,1)S(1)} %get-tuple-element.20), channel_id=1, source_target_pairs={{8,0},{9,1},{10,2},{11,3},{12,4},{13,5},{14,6},{15,7},{16,8},{17,9... | collective-permute-start | bytes 1572872 | tf_op jit(solution)/shard_map/ppermute | solution.py:57
  168.2 18.1 %collective-permute-start.30 = (bf16[256,1024]{1,0:T(8,128)(2,1)S(1)}, bf16[256,1024]{1,0:T(8,128)(2,1)S(1)}, u32[]{:S(2)}, u32[]{:S(2)}) collective-permute-start(bf16[256,1024]{1,0:T(8,128)(2,1)S(1)} %get-tuple-element.21), channel_id=1, source_target_pairs={{0,8},{1,9},{2,10},{3,11},{4,12},{5,13},{6,14},{7,15},{8,16},{9,17... | collective-permute-start | bytes 1572872 | tf_op jit(solution)/shard_map/ppermute | solution.py:57
  170.1 20.1 %collective-permute-start.33 = (bf16[256,1024]{1,0:T(8,128)(2,1)S(1)}, bf16[256,1024]{1,0:T(8,128)(2,1)S(1)}, u32[]{:S(2)}, u32[]{:S(2)}) collective-permute-start(bf16[256,1024]{1,0:T(8,128)(2,1)S(1)} %get-tuple-element.22), channel_id=1, source_target_pairs={{8,0},{9,1},{10,2},{11,3},{12,4},{13,5},{14,6},{15,7},{16,8},{17,9... | collective-permute-start | bytes 1572872 | tf_op jit(solution)/shard_map/ppermute | solution.py:57
  (28 other events, 277.6 us)

commit v6 on v5

--- a/solution.py
+++ b/solution.py
@@ -84,6 +84,12 @@
         return None
 
     return route(target)
+
+
+def after(value, *first):
+    for array in first:
+        value = value + 0 * array[:1, :1]
+    return value
 
 
 def four_planes(integrals, inverse_factor, energies, frequency):
@@ -142,8 +148,9 @@
         ordered(y, t[0].astype(BF16), t[1].astype(BF16), 0) for t in totals
     ]
 
-    straight_y, across_y = send(straight, OVER_Y), send(across, OVER_Y)
-    straight_x, across_x = send(straight, OVER_X), send(across, OVER_X)
+    straight_y, straight_x = send(straight, OVER_Y), send(straight, OVER_X)
+    across = after(across, straight_y, straight_x)
+    across_y, across_x = send(across, OVER_Y), send(across, OVER_X)
     straight_xy, across_xy = send(straight_y, OVER_X), send(across_x, OVER_Y)
     lows = [straight, straight_y, straight_x, straight_xy]
     highs = [across, across_y, across_x, across_xy]

time: 195 us -> 192 us (0.985)
  waiting for transfers between devices: 76.3 us -> 71.3 us
    ppermute x34, waiting for transfers between devices: 76.3 us -> 71.3 us  [send(): return lax.ppermute(value, AXES, pairs)]
  transfers between devices with their start and end apart: 34 -> 34, of which waited for: 20 -> 14; matrix products, arithmetic and copies ran while one was open for 22% -> 23% of each run, Pallas kernels for 0% -> 0%
where the time goes in v6:
time: 192 us; the launch traced here: 191 us
  waiting for transfers between devices  71.3 us (37%)
  starting transfers between devices  62.4 us (32%)
  matrix products  35.5 us (18%)
  other arithmetic  14.2 us (7%)
  local copies, waits for them, and re-layouts  4.67 us (2%)
  between operations  2.78 us (1%)
    ppermute x34, waiting for transfers between devices, send(): return lax.ppermute(value, AXES, pairs)  71.3 us
    ppermute x34, starting transfers between devices, send(): return lax.ppermute(value, AXES, pairs)  62.4 us
    dot_general x24, matrix products, rows_by_rows(): lax.dot_general(a, b, (((1,), (1,)), ((), ())), preferred_element_type=F32)  18.2 us
    dot_general x8, matrix products, columns_by_columns(): lax.dot_general(a, b, (((0,), (0,)), ((), ())), preferred_element_type=F32)  17.3 us
  transfers between devices with their start and end apart: 34, of which 14 were waited for; matrix products, arithmetic and copies ran while one was open for 23% of the time, Pallas kernels for 0%

profile of v6, /device:TPU:19, one launch (start us, length us, event | category | flops | bytes accessed | tf_op | source)
XLA Modules:
  0.0 190.8 jit_solution(3524795998934779078)
XLA Ops:
  7.5 2.3 %collective-permute-done.1 = bf16[256,512]{1,0:T(8,128)(2,1)} collective-permute-done((bf16[256,512]{1,0:T(8,128)(2,1)}, bf16[256,512]{1,0:T(8,128)(2,1)}, u32[]{:S(2)}, u32[]{:S(2)}) %collective-permute-start.1) | collective-permute-done | bytes 262176 | tf_op jit(solution)/shard_map/ppermute | solution.py:57
  9.7 6.6 %collective-permute-done.2 = bf16[256,512]{1,0:T(8,128)(2,1)} collective-permute-done((bf16[256,512]{1,0:T(8,128)(2,1)}, bf16[256,512]{1,0:T(8,128)(2,1)}, u32[]{:S(2)}, u32[]{:S(2)}) %collective-permute-start.2) | collective-permute-done | bytes 262176 | tf_op jit(solution)/shard_map/ppermute | solution.py:57
  20.9 3.4 %collective-permute-start.9 = (bf16[256,1024]{1,0:T(8,128)(2,1)}, bf16[256,1024]{1,0:T(8,128)(2,1)}, u32[]{:S(2)}, u32[]{:S(2)}) collective-permute-start(bf16[256,1024]{1,0:T(8,128)(2,1)} %get-tuple-element.37), channel_id=1, source_target_pairs={{0,8},{1,9},{2,10},{3,11},{4,12},{5,13},{6,14},{7,15},{8,16},{9,17... | collective-permute-start | bytes 1572872 | tf_op jit(solution)/shard_map/ppermute | solution.py:57
  25.1 6.0 %collective-permute-start.10 = (bf16[256,1024]{1,0:T(8,128)(2,1)}, bf16[256,1024]{1,0:T(8,128)(2,1)S(1)}, u32[]{:S(2)}, u32[]{:S(2)}) collective-permute-start(bf16[256,1024]{1,0:T(8,128)(2,1)} %get-tuple-element.37), channel_id=1, source_target_pairs={{8,0},{9,1},{10,2},{11,3},{12,4},{13,5},{14,6},{15,7},{16,8},{17,9... | collective-permute-start | bytes 1572872 | tf_op jit(solution)/shard_map/ppermute | solution.py:57
  34.4 6.9 %collective-permute-done.9 = bf16[256,1024]{1,0:T(8,128)(2,1)} collective-permute-done((bf16[256,1024]{1,0:T(8,128)(2,1)}, bf16[256,1024]{1,0:T(8,128)(2,1)}, u32[]{:S(2)}, u32[]{:S(2)}) %collective-permute-start.9) | collective-permute-done | bytes 524320 | tf_op jit(solution)/shard_map/ppermute | solution.py:57
  46.2 3.4 %collective-permute-start.12 = (bf16[256,1024]{1,0:T(8,128)(2,1)S(1)}, bf16[256,1024]{1,0:T(8,128)(2,1)S(1)}, u32[]{:S(2)}, u32[]{:S(2)}) collective-permute-start(bf16[256,1024]{1,0:T(8,128)(2,1)S(1)} %collective-permute-done.10), channel_id=1, source_target_pairs={{8,0},{9,1},{10,2},{11,3},{12,4},{13,5},{14,6},{15,7},{18,10},{19,... | collective-permute-start | bytes 1572872 | tf_op jit(solution)/shard_map/ppermute | solution.py:57
  55.4 3.2 %collective-permute-start.6 = (bf16[256,1024]{1,0:T(8,128)(2,1)S(1)}, bf16[256,1024]{1,0:T(8,128)(2,1)S(1)}, u32[]{:S(2)}, u32[]{:S(2)}) collective-permute-start(bf16[256,1024]{1,0:T(8,128)(2,1)S(1)} %collective-permute-done.5), channel_id=1, source_target_pairs={{16,24},{17,25},{18,26},{19,27},{20,28},{21,29},{22,30},{23,31}} | collective-permute-start | bytes 1572872 | tf_op jit(solution)/shard_map/ppermute | solution.py:57
  59.3 2.3 %collective-permute-done.11 = bf16[256,1024]{1,0:T(8,128)(2,1)S(1)} collective-permute-done((bf16[256,1024]{1,0:T(8,128)(2,1)}, bf16[256,1024]{1,0:T(8,128)(2,1)S(1)}, u32[]{:S(2)}, u32[]{:S(2)}) %collective-permute-start.11) | collective-permute-done | bytes 524320 | tf_op jit(solution)/shard_map/ppermute | solution.py:57
  76.3 4.8 %collective-permute-done.13 = bf16[256,1024]{1,0:T(8,128)(2,1)S(1)} collective-permute-done((bf16[256,1024]{1,0:T(8,128)(2,1)S(1)}, bf16[256,1024]{1,0:T(8,128)(2,1)S(1)}, u32[]{:S(2)}, u32[]{:S(2)}) %collective-permute-start.13) | collective-permute-done | bytes 524320 | tf_op jit(solution)/shard_map/ppermute | solution.py:57
  87.0 7.8 %collective-permute-done.18 = bf16[768,256]{1,0:T(8,128)(2,1)S(1)} collective-permute-done((bf16[768,256]{1,0:T(8,128)(2,1)S(1)}, bf16[768,256]{1,0:T(8,128)(2,1)S(1)}, u32[]{:S(2)}, u32[]{:S(2)}) %collective-permute-start.18) | collective-permute-done | bytes 393248 | tf_op jit(solution)/shard_map/ppermute | solution.py:57
  96.6 6.7 %collective-permute-done.19 = bf16[768,256]{1,0:T(8,128)(2,1)S(1)} collective-permute-done((bf16[768,256]{1,0:T(8,128)(2,1)S(1)}, bf16[768,256]{1,0:T(8,128)(2,1)S(1)}, u32[]{:S(2)}, u32[]{:S(2)}) %collective-permute-start.19) | collective-permute-done | bytes 393248 | tf_op jit(solution)/shard_map/ppermute | solution.py:57
  105.5 3.1 %collective-permute-start.27 = (bf16[768,1024]{1,0:T(8,128)(2,1)}, bf16[768,1024]{1,0:T(8,128)(2,1)}, u32[]{:S(2)}, u32[]{:S(2)}) collective-permute-start(bf16[768,1024]{1,0:T(8,128)(2,1)} %pad_maximum_fusion.1), channel_id=1, source_target_pairs={{0,2},{1,3},{2,0},{3,1},{4,6},{5,7},{6,4},{7,5},{8,10},{9,11},{10,... | collective-permute-start | bytes 4718600 | tf_op jit(solution)/shard_map/ppermute | solution.py:57
  115.7 3.4 %fusion.87 = (bf16[256,1024]{1,0:T(8,128)(2,1)}, f32[256,1024]{1,0:T(8,128)}) fusion(bf16[768,1024]{1,0:T(8,128)(2,1)} %collective-permute-done.27, bf16[768,1024]{1,0:T(8,128)(2,1)} %copy-done.1, s32[]{:T(128)S(6)} %select_n.329), kind=kOutput, calls=%fused_computation.167 | convolution fusion | flops 402915328 | bytes 3538948 | tf_op jit(solution)/shard_map/dot_general | solution.py:16
  121.9 8.9 %collective-permute-done.24 = bf16[256,1024]{1,0:T(8,128)(2,1)} collective-permute-done((bf16[256,1024]{1,0:T(8,128)(2,1)}, bf16[256,1024]{1,0:T(8,128)(2,1)}, u32[]{:S(2)}, u32[]{:S(2)}) %collective-permute-start.24) | collective-permute-done | bytes 524320 | tf_op jit(solution)/shard_map/ppermute | solution.py:57
  130.8 3.1 %add_convert_fusion.7 = (bf16[256,1024]{1,0:T(8,128)(2,1)}, bf16[256,1024]{1,0:T(8,128)(2,1)}) fusion(bf16[256,1024]{1,0:T(8,128)(2,1)} %collective-permute-done.21, bf16[256,1024]{1,0:T(8,128)(2,1)} %collective-permute-done.24, bf16[768,256]{1,0:T(8,128)(2,1)S(1)} %copy-done.14, bf16[768,256]{1,0:T(8,128)(2,1)S(1)} %copy-done.6, ...), kind=kOutput, calls=%fused_computation.56 | convolution fusion | flops 410517504 | bytes 4063236 | tf_op jit(solution)/shard_map/dot_general | solution.py:16
  135.1 4.0 %collective-permute-start.25 = (bf16[256,1024]{1,0:T(8,128)(2,1)}, bf16[256,1024]{1,0:T(8,128)(2,1)}, u32[]{:S(2)}, u32[]{:S(2)}) collective-permute-start(bf16[256,1024]{1,0:T(8,128)(2,1)} %get-tuple-element.30), channel_id=1, source_target_pairs={{16,8},{17,9},{18,10},{19,11},{20,12},{21,13},{22,14},{23,15},{24,... | collective-permute-start | bytes 1572872 | tf_op jit(solution)/shard_map/ppermute | solution.py:57
  139.2 2.8 %collective-permute-done.31 = bf16[256,1024]{1,0:T(8,128)(2,1)} collective-permute-done((bf16[256,1024]{1,0:T(8,128)(2,1)}, bf16[256,1024]{1,0:T(8,128)(2,1)}, u32[]{:S(2)}, u32[]{:S(2)}) %collective-permute-start.31) | collective-permute-done | bytes 524320 | tf_op jit(solution)/shard_map/ppermute | solution.py:57
  142.0 2.4 %add_convert_fusion.3 = (bf16[256,1024]{1,0:T(8,128)(2,1)S(1)}, bf16[256,1024]{1,0:T(8,128)(2,1)S(1)}) fusion(bf16[256,1024]{1,0:T(8,128)(2,1)} %collective-permute-done.28, bf16[256,1024]{1,0:T(8,128)(2,1)} %collective-permute-done.31, bf16[768,1024]{1,0:T(8,128)(2,1)} %collective-permute-done.27, bf16[768,1024]{1,0:T(8,128)(2,1)} %copy-done.1, ...), kind=kOutput, calls=%fused_computation.52 | convolution fusion | flops 404226048 | bytes 4063236 | tf_op jit(solution)/shard_map/dot_general | solution.py:16
  145.7 4.0 %collective-permute-start.32 = (bf16[256,1024]{1,0:T(8,128)(2,1)S(1)}, bf16[256,1024]{1,0:T(8,128)(2,1)S(1)}, u32[]{:S(2)}, u32[]{:S(2)}) collective-permute-start(bf16[256,1024]{1,0:T(8,128)(2,1)S(1)} %get-tuple-element.36), channel_id=1, source_target_pairs={{16,8},{17,9},{18,10},{19,11},{20,12},{21,13},{22,14},{23,15},{24,... | collective-permute-start | bytes 1572872 | tf_op jit(solution)/shard_map/ppermute | solution.py:57
  149.7 3.5 %collective-permute-done.25 = bf16[256,1024]{1,0:T(8,128)(2,1)} collective-permute-done((bf16[256,1024]{1,0:T(8,128)(2,1)}, bf16[256,1024]{1,0:T(8,128)(2,1)}, u32[]{:S(2)}, u32[]{:S(2)}) %collective-permute-start.25) | collective-permute-done | bytes 524320 | tf_op jit(solution)/shard_map/ppermute | solution.py:57
  157.3 3.6 %collective-permute-start.23 = (bf16[256,1024]{1,0:T(8,128)(2,1)S(1)}, bf16[256,1024]{1,0:T(8,128)(2,1)S(1)}, u32[]{:S(2)}, u32[]{:S(2)}) collective-permute-start(bf16[256,1024]{1,0:T(8,128)(2,1)S(1)} %get-tuple-element.21), channel_id=1, source_target_pairs={{0,8},{1,9},{2,10},{3,11},{4,12},{5,13},{6,14},{7,15},{8,16},{9,17... | collective-permute-start | bytes 1572872 | tf_op jit(solution)/shard_map/ppermute | solution.py:57
  166.7 3.4 %collective-permute-start.30 = (bf16[256,1024]{1,0:T(8,128)(2,1)S(1)}, bf16[256,1024]{1,0:T(8,128)(2,1)S(1)}, u32[]{:S(2)}, u32[]{:S(2)}) collective-permute-start(bf16[256,1024]{1,0:T(8,128)(2,1)S(1)} %get-tuple-element.23), channel_id=1, source_target_pairs={{0,8},{1,9},{2,10},{3,11},{4,12},{5,13},{6,14},{7,15},{8,16},{9,17... | collective-permute-start | bytes 1572872 | tf_op jit(solution)/shard_map/ppermute | solution.py:57
  170.1 5.5 %collective-permute-done.26 = bf16[256,1024]{1,0:T(8,128)(2,1)S(1)} collective-permute-done((bf16[256,1024]{1,0:T(8,128)(2,1)S(1)}, bf16[256,1024]{1,0:T(8,128)(2,1)S(1)}, u32[]{:S(2)}, u32[]{:S(2)}) %collective-permute-start.26) | collective-permute-done | bytes 524320 | tf_op jit(solution)/shard_map/ppermute | solution.py:57
  176.3 10.5 %collective-permute-done.33 = bf16[256,1024]{1,0:T(8,128)(2,1)S(1)} collective-permute-done((bf16[256,1024]{1,0:T(8,128)(2,1)S(1)}, bf16[256,1024]{1,0:T(8,128)(2,1)S(1)}, u32[]{:S(2)}, u32[]{:S(2)}) %collective-permute-start.33) | collective-permute-done | bytes 524320 | tf_op jit(solution)/shard_map/ppermute | solution.py:57
  (135 shorter events, 76.5 us)
Async XLA Ops:
  2.5 13.9 %collective-permute-start.2 = (bf16[256,512]{1,0:T(8,128)(2,1)}, bf16[256,512]{1,0:T(8,128)(2,1)}, u32[]{:S(2)}, u32[]{:S(2)}) collective-permute-start(bf16[256,512]{1,0:T(8,128)(2,1)} %get-tuple-element.12), channel_id=1, source_target_pairs={{0,5},{1,4},{2,7},{3,6},{4,1},{5,0},{6,3},{7,2},{8,13},{9,12},{10,... | collective-permute-start | bytes 786440 | tf_op jit(solution)/shard_map/ppermute | solution.py:57
  4.7 12.8 %collective-permute-start = (bf16[256,512]{1,0:T(8,128)(2,1)}, bf16[256,512]{1,0:T(8,128)(2,1)}, u32[]{:S(2)}, u32[]{:S(2)}) collective-permute-start(bf16[256,512]{1,0:T(8,128)(2,1)} %get-tuple-element.10), channel_id=1, source_target_pairs={{0,1},{1,0},{2,3},{3,2},{4,5},{5,4},{6,7},{7,6},{8,9},{9,8},{10,11... | collective-permute-start | bytes 786440 | tf_op jit(solution)/shard_map/ppermute | solution.py:57
  6.2 44.7 %collective-permute-start.7 = (bf16[192,4096]{1,0:T(8,128)(2,1)}, bf16[192,4096]{1,0:T(8,128)(2,1)}, u32[]{:S(2)}, u32[]{:S(2)}) collective-permute-start(bf16[192,4096]{1,0:T(8,128)(2,1)} %constant_dynamic-slice_fusion), channel_id=1, source_target_pairs={{0,1},{1,0},{2,3},{3,2},{4,5},{5,4},{6,7},{7,6},{8,9},{9,8},{10,11... | collective-permute-start | bytes 4718600 | tf_op jit(solution)/shard_map/ppermute | solution.py:57
  20.9 20.4 %collective-permute-start.9 = (bf16[256,1024]{1,0:T(8,128)(2,1)}, bf16[256,1024]{1,0:T(8,128)(2,1)}, u32[]{:S(2)}, u32[]{:S(2)}) collective-permute-start(bf16[256,1024]{1,0:T(8,128)(2,1)} %get-tuple-element.37), channel_id=1, source_target_pairs={{0,8},{1,9},{2,10},{3,11},{4,12},{5,13},{6,14},{7,15},{8,16},{9,17... | collective-permute-start | bytes 1572872 | tf_op jit(solution)/shard_map/ppermute | solution.py:57
  24.4 30.6 %collective-permute-start.4 = (bf16[256,1024]{1,0:T(8,128)(2,1)}, bf16[256,1024]{1,0:T(8,128)(2,1)S(1)}, u32[]{:S(2)}, u32[]{:S(2)}) collective-permute-start(bf16[256,1024]{1,0:T(8,128)(2,1)} %get-tuple-element.38), channel_id=1, source_target_pairs={{10,2},{11,3},{14,6},{15,7}} | collective-permute-start | bytes 1572872 | tf_op jit(solution)/shard_map/ppermute | solution.py:57
  25.1 21.2 %collective-permute-start.10 = (bf16[256,1024]{1,0:T(8,128)(2,1)}, bf16[256,1024]{1,0:T(8,128)(2,1)S(1)}, u32[]{:S(2)}, u32[]{:S(2)}) collective-permute-start(bf16[256,1024]{1,0:T(8,128)(2,1)} %get-tuple-element.37), channel_id=1, source_target_pairs={{8,0},{9,1},{10,2},{11,3},{12,4},{13,5},{14,6},{15,7},{16,8},{17,9... | collective-permute-start | bytes 1572872 | tf_op jit(solution)/shard_map/ppermute | solution.py:57
  31.1 24.3 %collective-permute-start.5 = (bf16[256,1024]{1,0:T(8,128)(2,1)}, bf16[256,1024]{1,0:T(8,128)(2,1)S(1)}, u32[]{:S(2)}, u32[]{:S(2)}) collective-permute-start(bf16[256,1024]{1,0:T(8,128)(2,1)} %collective-permute-done.3), channel_id=1, source_target_pairs={{8,16},{9,17},{10,18},{11,19},{12,20},{13,21},{14,22},{15,23},{18,... | collective-permute-start | bytes 1572872 | tf_op jit(solution)/shard_map/ppermute | solution.py:57
  41.4 20.2 %collective-permute-start.11 = (bf16[256,1024]{1,0:T(8,128)(2,1)}, bf16[256,1024]{1,0:T(8,128)(2,1)S(1)}, u32[]{:S(2)}, u32[]{:S(2)}) collective-permute-start(bf16[256,1024]{1,0:T(8,128)(2,1)} %collective-permute-done.9), channel_id=1, source_target_pairs={{8,16},{9,17},{10,18},{11,19},{12,20},{13,21},{14,22},{15,23},{16,... | collective-permute-start | bytes 1572872 | tf_op jit(solution)/shard_map/ppermute | solution.py:57
  46.2 12.4 %collective-permute-start.12 = (bf16[256,1024]{1,0:T(8,128)(2,1)S(1)}, bf16[256,1024]{1,0:T(8,128)(2,1)S(1)}, u32[]{:S(2)}, u32[]{:S(2)}) collective-permute-start(bf16[256,1024]{1,0:T(8,128)(2,1)S(1)} %collective-permute-done.10), channel_id=1, source_target_pairs={{8,0},{9,1},{10,2},{11,3},{12,4},{13,5},{14,6},{15,7},{18,10},{19,... | collective-permute-start | bytes 1572872 | tf_op jit(solution)/shard_map/ppermute | solution.py:57
  50.9 13.9 %collective-permute-start.8 = (bf16[192,4096]{1,0:T(8,128)(2,1)}, bf16[192,4096]{1,0:T(8,128)(2,1)S(1)}, u32[]{:S(2)}, u32[]{:S(2)}) collective-permute-start(bf16[192,4096]{1,0:T(8,128)(2,1)} %collective-permute-done.7), channel_id=1, source_target_pairs={{0,2},{1,3},{2,0},{3,1},{4,6},{5,7},{6,4},{7,5},{8,10},{9,11},{10,... | collective-permute-start | bytes 4718600 | tf_op jit(solution)/shard_map/ppermute | solution.py:57
  55.4 15.0 %collective-permute-start.6 = (bf16[256,1024]{1,0:T(8,128)(2,1)S(1)}, bf16[256,1024]{1,0:T(8,128)(2,1)S(1)}, u32[]{:S(2)}, u32[]{:S(2)}) collective-permute-start(bf16[256,1024]{1,0:T(8,128)(2,1)S(1)} %collective-permute-done.5), channel_id=1, source_target_pairs={{16,24},{17,25},{18,26},{19,27},{20,28},{21,29},{22,30},{23,31}} | collective-permute-start | bytes 1572872 | tf_op jit(solution)/shard_map/ppermute | solution.py:57
  61.6 19.5 %collective-permute-start.13 = (bf16[256,1024]{1,0:T(8,128)(2,1)S(1)}, bf16[256,1024]{1,0:T(8,128)(2,1)S(1)}, u32[]{:S(2)}, u32[]{:S(2)}) collective-permute-start(bf16[256,1024]{1,0:T(8,128)(2,1)S(1)} %collective-permute-done.11), channel_id=1, source_target_pairs={{16,24},{17,25},{18,26},{19,27},{20,28},{21,29},{22,30},{23,31}} | collective-permute-start | bytes 1572872 | tf_op jit(solution)/shard_map/ppermute | solution.py:57
  85.7 17.5 %collective-permute-start.19 = (bf16[768,256]{1,0:T(8,128)(2,1)S(1)}, bf16[768,256]{1,0:T(8,128)(2,1)S(1)}, u32[]{:S(2)}, u32[]{:S(2)}) collective-permute-start(bf16[768,256]{1,0:T(8,128)(2,1)S(1)} %collective-permute-done.15), channel_id=1, source_target_pairs={{0,4},{1,5},{2,6},{3,7},{4,0},{5,1},{6,2},{7,3},{8,12},{9,13},{10,... | collective-permute-start | bytes 1179656 | tf_op jit(solution)/shard_map/ppermute | solution.py:57
  114.4 16.4 %collective-permute-start.24 = (bf16[256,1024]{1,0:T(8,128)(2,1)}, bf16[256,1024]{1,0:T(8,128)(2,1)}, u32[]{:S(2)}, u32[]{:S(2)}) collective-permute-start(bf16[256,1024]{1,0:T(8,128)(2,1)} %get-tuple-element.59), channel_id=1, source_target_pairs={{24,16},{25,17},{26,18},{27,19},{28,20},{29,21},{30,22},{31,23}} | collective-permute-start | bytes 1572872 | tf_op jit(solution)/shard_map/ppermute | solution.py:57
  119.1 20.1 %collective-permute-start.28 = (bf16[256,1024]{1,0:T(8,128)(2,1)}, bf16[256,1024]{1,0:T(8,128)(2,1)}, u32[]{:S(2)}, u32[]{:S(2)}) collective-permute-start(bf16[256,1024]{1,0:T(8,128)(2,1)} %get-tuple-element.57), channel_id=1, source_target_pairs={{0,8},{1,9},{2,10},{3,11},{4,12},{5,13},{6,14},{7,15}} | collective-permute-start | bytes 1572872 | tf_op jit(solution)/shard_map/ppermute | solution.py:57
  120.6 21.4 %collective-permute-start.31 = (bf16[256,1024]{1,0:T(8,128)(2,1)}, bf16[256,1024]{1,0:T(8,128)(2,1)}, u32[]{:S(2)}, u32[]{:S(2)}) collective-permute-start(bf16[256,1024]{1,0:T(8,128)(2,1)} %get-tuple-element.57), channel_id=1, source_target_pairs={{24,16},{25,17},{26,18},{27,19},{28,20},{29,21},{30,22},{31,23}} | collective-permute-start | bytes 1572872 | tf_op jit(solution)/shard_map/ppermute | solution.py:57
  133.8 15.9 %collective-permute-start.22 = (bf16[256,1024]{1,0:T(8,128)(2,1)}, bf16[256,1024]{1,0:T(8,128)(2,1)}, u32[]{:S(2)}, u32[]{:S(2)}) collective-permute-start(bf16[256,1024]{1,0:T(8,128)(2,1)} %get-tuple-element.29), channel_id=1, source_target_pairs={{0,8},{1,9},{2,10},{3,11},{4,12},{5,13},{6,14},{7,15},{8,16},{9,17... | collective-permute-start | bytes 1572872 | tf_op jit(solution)/shard_map/ppermute | solution.py:57
  135.1 18.1 %collective-permute-start.25 = (bf16[256,1024]{1,0:T(8,128)(2,1)}, bf16[256,1024]{1,0:T(8,128)(2,1)}, u32[]{:S(2)}, u32[]{:S(2)}) collective-permute-start(bf16[256,1024]{1,0:T(8,128)(2,1)} %get-tuple-element.30), channel_id=1, source_target_pairs={{16,8},{17,9},{18,10},{19,11},{20,12},{21,13},{22,14},{23,15},{24,... | collective-permute-start | bytes 1572872 | tf_op jit(solution)/shard_map/ppermute | solution.py:57
  144.4 18.5 %collective-permute-start.29 = (bf16[256,1024]{1,0:T(8,128)(2,1)S(1)}, bf16[256,1024]{1,0:T(8,128)(2,1)S(1)}, u32[]{:S(2)}, u32[]{:S(2)}) collective-permute-start(bf16[256,1024]{1,0:T(8,128)(2,1)S(1)} %get-tuple-element.35), channel_id=1, source_target_pairs={{0,8},{1,9},{2,10},{3,11},{4,12},{5,13},{6,14},{7,15},{8,16},{9,17... | collective-permute-start | bytes 1572872 | tf_op jit(solution)/shard_map/ppermute | solution.py:57
  145.7 18.6 %collective-permute-start.32 = (bf16[256,1024]{1,0:T(8,128)(2,1)S(1)}, bf16[256,1024]{1,0:T(8,128)(2,1)S(1)}, u32[]{:S(2)}, u32[]{:S(2)}) collective-permute-start(bf16[256,1024]{1,0:T(8,128)(2,1)S(1)} %get-tuple-element.36), channel_id=1, source_target_pairs={{16,8},{17,9},{18,10},{19,11},{20,12},{21,13},{22,14},{23,15},{24,... | collective-permute-start | bytes 1572872 | tf_op jit(solution)/shard_map/ppermute | solution.py:57
  155.2 20.4 %collective-permute-start.26 = (bf16[256,1024]{1,0:T(8,128)(2,1)S(1)}, bf16[256,1024]{1,0:T(8,128)(2,1)S(1)}, u32[]{:S(2)}, u32[]{:S(2)}) collective-permute-start(bf16[256,1024]{1,0:T(8,128)(2,1)S(1)} %get-tuple-element.22), channel_id=1, source_target_pairs={{8,0},{9,1},{10,2},{11,3},{12,4},{13,5},{14,6},{15,7},{16,8},{17,9... | collective-permute-start | bytes 1572872 | tf_op jit(solution)/shard_map/ppermute | solution.py:57
  157.3 18.3 %collective-permute-start.23 = (bf16[256,1024]{1,0:T(8,128)(2,1)S(1)}, bf16[256,1024]{1,0:T(8,128)(2,1)S(1)}, u32[]{:S(2)}, u32[]{:S(2)}) collective-permute-start(bf16[256,1024]{1,0:T(8,128)(2,1)S(1)} %get-tuple-element.21), channel_id=1, source_target_pairs={{0,8},{1,9},{2,10},{3,11},{4,12},{5,13},{6,14},{7,15},{8,16},{9,17... | collective-permute-start | bytes 1572872 | tf_op jit(solution)/shard_map/ppermute | solution.py:57
  164.8 22.1 %collective-permute-start.33 = (bf16[256,1024]{1,0:T(8,128)(2,1)S(1)}, bf16[256,1024]{1,0:T(8,128)(2,1)S(1)}, u32[]{:S(2)}, u32[]{:S(2)}) collective-permute-start(bf16[256,1024]{1,0:T(8,128)(2,1)S(1)} %get-tuple-element.24), channel_id=1, source_target_pairs={{8,0},{9,1},{10,2},{11,3},{12,4},{13,5},{14,6},{15,7},{16,8},{17,9... | collective-permute-start | bytes 1572872 | tf_op jit(solution)/shard_map/ppermute | solution.py:57
  166.7 20.1 %collective-permute-start.30 = (bf16[256,1024]{1,0:T(8,128)(2,1)S(1)}, bf16[256,1024]{1,0:T(8,128)(2,1)S(1)}, u32[]{:S(2)}, u32[]{:S(2)}) collective-permute-start(bf16[256,1024]{1,0:T(8,128)(2,1)S(1)} %get-tuple-element.23), channel_id=1, source_target_pairs={{0,8},{1,9},{2,10},{3,11},{4,12},{5,13},{6,14},{7,15},{8,16},{9,17... | collective-permute-start | bytes 1572872 | tf_op jit(solution)/shard_map/ppermute | solution.py:57
  (28 other events, 255.2 us)

commit v7 on v6

--- a/solution.py
+++ b/solution.py
@@ -88,7 +88,7 @@
 
 def after(value, *first):
     for array in first:
-        value = value + 0 * array[:1, :1]
+        value = value + 0 * array[:1]
     return value
 
 
@@ -149,7 +149,7 @@
     ]
 
     straight_y, straight_x = send(straight, OVER_Y), send(straight, OVER_X)
-    across = after(across, straight_y, straight_x)
+    across = after(across, straight_x)
     across_y, across_x = send(across, OVER_Y), send(across, OVER_X)
     straight_xy, across_xy = send(straight_y, OVER_X), send(across_x, OVER_Y)
     lows = [straight, straight_y, straight_x, straight_xy]

time: 192 us -> 190 us (0.990)
  transfers between devices with their start and end apart: 34 -> 34, of which waited for: 14 -> 14; matrix products, arithmetic and copies ran while one was open for 23% -> 24% of each run, Pallas kernels for 0% -> 0%
where the time goes in v7:
time: 190 us; the launch traced here: 188 us
  waiting for transfers between devices  71.2 us (37%)
  starting transfers between devices  62.4 us (33%)
  matrix products  35.5 us (19%)
  other arithmetic  14.2 us (7%)
  local copies, waits for them, and re-layouts  3.62 us (2%)
    ppermute x34, waiting for transfers between devices, send(): return lax.ppermute(value, AXES, pairs)  71.2 us
    ppermute x34, starting transfers between devices, send(): return lax.ppermute(value, AXES, pairs)  62.4 us
    dot_general x24, matrix products, rows_by_rows(): lax.dot_general(a, b, (((1,), (1,)), ((), ())), preferred_element_type=F32)  18.2 us
    dot_general x8, matrix products, columns_by_columns(): lax.dot_general(a, b, (((0,), (0,)), ((), ())), preferred_element_type=F32)  17.3 us
  transfers between devices with their start and end apart: 34, of which 14 were waited for; matrix products, arithmetic and copies ran while one was open for 24% of the time, Pallas kernels for 0%

profile of v7, /device:TPU:19, one launch (start us, length us, event | category | flops | bytes accessed | tf_op | source)
XLA Modules:
  0.0 188.4 jit_solution(12250508423222525828)
XLA Ops:
  7.4 2.3 %collective-permute-done.1 = bf16[256,512]{1,0:T(8,128)(2,1)} collective-permute-done((bf16[256,512]{1,0:T(8,128)(2,1)}, bf16[256,512]{1,0:T(8,128)(2,1)}, u32[]{:S(2)}, u32[]{:S(2)}) %collective-permute-start.1) | collective-permute-done | bytes 262176 | tf_op jit(solution)/shard_map/ppermute | solution.py:57
  9.7 6.6 %collective-permute-done.2 = bf16[256,512]{1,0:T(8,128)(2,1)} collective-permute-done((bf16[256,512]{1,0:T(8,128)(2,1)}, bf16[256,512]{1,0:T(8,128)(2,1)}, u32[]{:S(2)}, u32[]{:S(2)}) %collective-permute-start.2) | collective-permute-done | bytes 262176 | tf_op jit(solution)/shard_map/ppermute | solution.py:57
  20.9 3.4 %collective-permute-start.9 = (bf16[256,1024]{1,0:T(8,128)(2,1)}, bf16[256,1024]{1,0:T(8,128)(2,1)}, u32[]{:S(2)}, u32[]{:S(2)}) collective-permute-start(bf16[256,1024]{1,0:T(8,128)(2,1)} %get-tuple-element.37), channel_id=1, source_target_pairs={{0,8},{1,9},{2,10},{3,11},{4,12},{5,13},{6,14},{7,15},{8,16},{9,17... | collective-permute-start | bytes 1572872 | tf_op jit(solution)/shard_map/ppermute | solution.py:57
  25.0 6.0 %collective-permute-start.10 = (bf16[256,1024]{1,0:T(8,128)(2,1)}, bf16[256,1024]{1,0:T(8,128)(2,1)S(1)}, u32[]{:S(2)}, u32[]{:S(2)}) collective-permute-start(bf16[256,1024]{1,0:T(8,128)(2,1)} %get-tuple-element.37), channel_id=1, source_target_pairs={{8,0},{9,1},{10,2},{11,3},{12,4},{13,5},{14,6},{15,7},{16,8},{17,9... | collective-permute-start | bytes 1572872 | tf_op jit(solution)/shard_map/ppermute | solution.py:57
  34.4 6.9 %collective-permute-done.9 = bf16[256,1024]{1,0:T(8,128)(2,1)} collective-permute-done((bf16[256,1024]{1,0:T(8,128)(2,1)}, bf16[256,1024]{1,0:T(8,128)(2,1)}, u32[]{:S(2)}, u32[]{:S(2)}) %collective-permute-start.9) | collective-permute-done | bytes 524320 | tf_op jit(solution)/shard_map/ppermute | solution.py:57
  46.2 3.4 %collective-permute-start.12 = (bf16[256,1024]{1,0:T(8,128)(2,1)S(1)}, bf16[256,1024]{1,0:T(8,128)(2,1)S(1)}, u32[]{:S(2)}, u32[]{:S(2)}) collective-permute-start(bf16[256,1024]{1,0:T(8,128)(2,1)S(1)} %collective-permute-done.10), channel_id=1, source_target_pairs={{8,0},{9,1},{10,2},{11,3},{12,4},{13,5},{14,6},{15,7},{18,10},{19,... | collective-permute-start | bytes 1572872 | tf_op jit(solution)/shard_map/ppermute | solution.py:57
  55.3 3.2 %collective-permute-start.6 = (bf16[256,1024]{1,0:T(8,128)(2,1)S(1)}, bf16[256,1024]{1,0:T(8,128)(2,1)S(1)}, u32[]{:S(2)}, u32[]{:S(2)}) collective-permute-start(bf16[256,1024]{1,0:T(8,128)(2,1)S(1)} %collective-permute-done.5), channel_id=1, source_target_pairs={{16,24},{17,25},{18,26},{19,27},{20,28},{21,29},{22,30},{23,31}} | collective-permute-start | bytes 1572872 | tf_op jit(solution)/shard_map/ppermute | solution.py:57
  59.3 2.3 %collective-permute-done.11 = bf16[256,1024]{1,0:T(8,128)(2,1)S(1)} collective-permute-done((bf16[256,1024]{1,0:T(8,128)(2,1)}, bf16[256,1024]{1,0:T(8,128)(2,1)S(1)}, u32[]{:S(2)}, u32[]{:S(2)}) %collective-permute-start.11) | collective-permute-done | bytes 524320 | tf_op jit(solution)/shard_map/ppermute | solution.py:57
  76.3 4.8 %collective-permute-done.13 = bf16[256,1024]{1,0:T(8,128)(2,1)S(1)} collective-permute-done((bf16[256,1024]{1,0:T(8,128)(2,1)S(1)}, bf16[256,1024]{1,0:T(8,128)(2,1)S(1)}, u32[]{:S(2)}, u32[]{:S(2)}) %collective-permute-start.13) | collective-permute-done | bytes 524320 | tf_op jit(solution)/shard_map/ppermute | solution.py:57
  84.7 7.8 %collective-permute-done.18 = bf16[768,256]{1,0:T(8,128)(2,1)S(1)} collective-permute-done((bf16[768,256]{1,0:T(8,128)(2,1)S(1)}, bf16[768,256]{1,0:T(8,128)(2,1)S(1)}, u32[]{:S(2)}, u32[]{:S(2)}) %collective-permute-start.18) | collective-permute-done | bytes 393248 | tf_op jit(solution)/shard_map/ppermute | solution.py:57
  94.3 6.7 %collective-permute-done.19 = bf16[768,256]{1,0:T(8,128)(2,1)S(1)} collective-permute-done((bf16[768,256]{1,0:T(8,128)(2,1)S(1)}, bf16[768,256]{1,0:T(8,128)(2,1)S(1)}, u32[]{:S(2)}, u32[]{:S(2)}) %collective-permute-start.19) | collective-permute-done | bytes 393248 | tf_op jit(solution)/shard_map/ppermute | solution.py:57
  103.1 3.1 %collective-permute-start.27 = (bf16[768,1024]{1,0:T(8,128)(2,1)}, bf16[768,1024]{1,0:T(8,128)(2,1)}, u32[]{:S(2)}, u32[]{:S(2)}) collective-permute-start(bf16[768,1024]{1,0:T(8,128)(2,1)} %pad_maximum_fusion.1), channel_id=1, source_target_pairs={{0,2},{1,3},{2,0},{3,1},{4,6},{5,7},{6,4},{7,5},{8,10},{9,11},{10,... | collective-permute-start | bytes 4718600 | tf_op jit(solution)/shard_map/ppermute | solution.py:57
  113.4 3.4 %fusion.86 = (bf16[256,1024]{1,0:T(8,128)(2,1)}, f32[256,1024]{1,0:T(8,128)}) fusion(bf16[768,1024]{1,0:T(8,128)(2,1)} %collective-permute-done.27, bf16[768,1024]{1,0:T(8,128)(2,1)} %copy-done.1, s32[]{:T(128)S(6)} %select_n.329), kind=kOutput, calls=%fused_computation.168 | convolution fusion | flops 402915328 | bytes 3538948 | tf_op jit(solution)/shard_map/dot_general | solution.py:16
  119.5 8.9 %collective-permute-done.24 = bf16[256,1024]{1,0:T(8,128)(2,1)} collective-permute-done((bf16[256,1024]{1,0:T(8,128)(2,1)}, bf16[256,1024]{1,0:T(8,128)(2,1)}, u32[]{:S(2)}, u32[]{:S(2)}) %collective-permute-start.24) | collective-permute-done | bytes 524320 | tf_op jit(solution)/shard_map/ppermute | solution.py:57
  128.4 3.0 %add_convert_fusion.7 = (bf16[256,1024]{1,0:T(8,128)(2,1)}, bf16[256,1024]{1,0:T(8,128)(2,1)}) fusion(bf16[256,1024]{1,0:T(8,128)(2,1)} %collective-permute-done.21, bf16[256,1024]{1,0:T(8,128)(2,1)} %collective-permute-done.24, bf16[768,256]{1,0:T(8,128)(2,1)S(1)} %copy-done.14, bf16[768,256]{1,0:T(8,128)(2,1)S(1)} %copy-done.6, ...), kind=kOutput, calls=%fused_computation.56 | convolution fusion | flops 410517504 | bytes 4063236 | tf_op jit(solution)/shard_map/dot_general | solution.py:16
  132.7 4.0 %collective-permute-start.25 = (bf16[256,1024]{1,0:T(8,128)(2,1)}, bf16[256,1024]{1,0:T(8,128)(2,1)}, u32[]{:S(2)}, u32[]{:S(2)}) collective-permute-start(bf16[256,1024]{1,0:T(8,128)(2,1)} %get-tuple-element.30), channel_id=1, source_target_pairs={{16,8},{17,9},{18,10},{19,11},{20,12},{21,13},{22,14},{23,15},{24,... | collective-permute-start | bytes 1572872 | tf_op jit(solution)/shard_map/ppermute | solution.py:57
  136.8 2.8 %collective-permute-done.31 = bf16[256,1024]{1,0:T(8,128)(2,1)} collective-permute-done((bf16[256,1024]{1,0:T(8,128)(2,1)}, bf16[256,1024]{1,0:T(8,128)(2,1)}, u32[]{:S(2)}, u32[]{:S(2)}) %collective-permute-start.31) | collective-permute-done | bytes 524320 | tf_op jit(solution)/shard_map/ppermute | solution.py:57
  139.6 2.4 %add_convert_fusion.3 = (bf16[256,1024]{1,0:T(8,128)(2,1)S(1)}, bf16[256,1024]{1,0:T(8,128)(2,1)S(1)}) fusion(bf16[256,1024]{1,0:T(8,128)(2,1)} %collective-permute-done.28, bf16[256,1024]{1,0:T(8,128)(2,1)} %collective-permute-done.31, bf16[768,1024]{1,0:T(8,128)(2,1)} %collective-permute-done.27, bf16[768,1024]{1,0:T(8,128)(2,1)} %copy-done.1, ...), kind=kOutput, calls=%fused_computation.52 | convolution fusion | flops 404226048 | bytes 4063236 | tf_op jit(solution)/shard_map/dot_general | solution.py:16
  143.4 4.0 %collective-permute-start.32 = (bf16[256,1024]{1,0:T(8,128)(2,1)S(1)}, bf16[256,1024]{1,0:T(8,128)(2,1)S(1)}, u32[]{:S(2)}, u32[]{:S(2)}) collective-permute-start(bf16[256,1024]{1,0:T(8,128)(2,1)S(1)} %get-tuple-element.36), channel_id=1, source_target_pairs={{16,8},{17,9},{18,10},{19,11},{20,12},{21,13},{22,14},{23,15},{24,... | collective-permute-start | bytes 1572872 | tf_op jit(solution)/shard_map/ppermute | solution.py:57
  147.4 3.5 %collective-permute-done.25 = bf16[256,1024]{1,0:T(8,128)(2,1)} collective-permute-done((bf16[256,1024]{1,0:T(8,128)(2,1)}, bf16[256,1024]{1,0:T(8,128)(2,1)}, u32[]{:S(2)}, u32[]{:S(2)}) %collective-permute-start.25) | collective-permute-done | bytes 524320 | tf_op jit(solution)/shard_map/ppermute | solution.py:57
  154.9 3.6 %collective-permute-start.23 = (bf16[256,1024]{1,0:T(8,128)(2,1)S(1)}, bf16[256,1024]{1,0:T(8,128)(2,1)S(1)}, u32[]{:S(2)}, u32[]{:S(2)}) collective-permute-start(bf16[256,1024]{1,0:T(8,128)(2,1)S(1)} %get-tuple-element.21), channel_id=1, source_target_pairs={{0,8},{1,9},{2,10},{3,11},{4,12},{5,13},{6,14},{7,15},{8,16},{9,17... | collective-permute-start | bytes 1572872 | tf_op jit(solution)/shard_map/ppermute | solution.py:57
  164.3 3.4 %collective-permute-start.30 = (bf16[256,1024]{1,0:T(8,128)(2,1)S(1)}, bf16[256,1024]{1,0:T(8,128)(2,1)S(1)}, u32[]{:S(2)}, u32[]{:S(2)}) collective-permute-start(bf16[256,1024]{1,0:T(8,128)(2,1)S(1)} %get-tuple-element.23), channel_id=1, source_target_pairs={{0,8},{1,9},{2,10},{3,11},{4,12},{5,13},{6,14},{7,15},{8,16},{9,17... | collective-permute-start | bytes 1572872 | tf_op jit(solution)/shard_map/ppermute | solution.py:57
  167.7 5.5 %collective-permute-done.26 = bf16[256,1024]{1,0:T(8,128)(2,1)S(1)} collective-permute-done((bf16[256,1024]{1,0:T(8,128)(2,1)S(1)}, bf16[256,1024]{1,0:T(8,128)(2,1)S(1)}, u32[]{:S(2)}, u32[]{:S(2)}) %collective-permute-start.26) | collective-permute-done | bytes 524320 | tf_op jit(solution)/shard_map/ppermute | solution.py:57
  174.0 10.5 %collective-permute-done.33 = bf16[256,1024]{1,0:T(8,128)(2,1)S(1)} collective-permute-done((bf16[256,1024]{1,0:T(8,128)(2,1)S(1)}, bf16[256,1024]{1,0:T(8,128)(2,1)S(1)}, u32[]{:S(2)}, u32[]{:S(2)}) %collective-permute-start.33) | collective-permute-done | bytes 524320 | tf_op jit(solution)/shard_map/ppermute | solution.py:57
  (134 shorter events, 75.4 us)
Async XLA Ops:
  2.5 13.9 %collective-permute-start.2 = (bf16[256,512]{1,0:T(8,128)(2,1)}, bf16[256,512]{1,0:T(8,128)(2,1)}, u32[]{:S(2)}, u32[]{:S(2)}) collective-permute-start(bf16[256,512]{1,0:T(8,128)(2,1)} %get-tuple-element.12), channel_id=1, source_target_pairs={{0,5},{1,4},{2,7},{3,6},{4,1},{5,0},{6,3},{7,2},{8,13},{9,12},{10,... | collective-permute-start | bytes 786440 | tf_op jit(solution)/shard_map/ppermute | solution.py:57
  4.7 12.8 %collective-permute-start = (bf16[256,512]{1,0:T(8,128)(2,1)}, bf16[256,512]{1,0:T(8,128)(2,1)}, u32[]{:S(2)}, u32[]{:S(2)}) collective-permute-start(bf16[256,512]{1,0:T(8,128)(2,1)} %get-tuple-element.10), channel_id=1, source_target_pairs={{0,1},{1,0},{2,3},{3,2},{4,5},{5,4},{6,7},{7,6},{8,9},{9,8},{10,11... | collective-permute-start | bytes 786440 | tf_op jit(solution)/shard_map/ppermute | solution.py:57
  6.2 44.7 %collective-permute-start.7 = (bf16[192,4096]{1,0:T(8,128)(2,1)}, bf16[192,4096]{1,0:T(8,128)(2,1)}, u32[]{:S(2)}, u32[]{:S(2)}) collective-permute-start(bf16[192,4096]{1,0:T(8,128)(2,1)} %constant_dynamic-slice_fusion), channel_id=1, source_target_pairs={{0,1},{1,0},{2,3},{3,2},{4,5},{5,4},{6,7},{7,6},{8,9},{9,8},{10,11... | collective-permute-start | bytes 4718600 | tf_op jit(solution)/shard_map/ppermute | solution.py:57
  20.9 20.5 %collective-permute-start.9 = (bf16[256,1024]{1,0:T(8,128)(2,1)}, bf16[256,1024]{1,0:T(8,128)(2,1)}, u32[]{:S(2)}, u32[]{:S(2)}) collective-permute-start(bf16[256,1024]{1,0:T(8,128)(2,1)} %get-tuple-element.37), channel_id=1, source_target_pairs={{0,8},{1,9},{2,10},{3,11},{4,12},{5,13},{6,14},{7,15},{8,16},{9,17... | collective-permute-start | bytes 1572872 | tf_op jit(solution)/shard_map/ppermute | solution.py:57
  24.3 30.6 %collective-permute-start.4 = (bf16[256,1024]{1,0:T(8,128)(2,1)}, bf16[256,1024]{1,0:T(8,128)(2,1)S(1)}, u32[]{:S(2)}, u32[]{:S(2)}) collective-permute-start(bf16[256,1024]{1,0:T(8,128)(2,1)} %get-tuple-element.38), channel_id=1, source_target_pairs={{10,2},{11,3},{14,6},{15,7}} | collective-permute-start | bytes 1572872 | tf_op jit(solution)/shard_map/ppermute | solution.py:57
  25.0 21.2 %collective-permute-start.10 = (bf16[256,1024]{1,0:T(8,128)(2,1)}, bf16[256,1024]{1,0:T(8,128)(2,1)S(1)}, u32[]{:S(2)}, u32[]{:S(2)}) collective-permute-start(bf16[256,1024]{1,0:T(8,128)(2,1)} %get-tuple-element.37), channel_id=1, source_target_pairs={{8,0},{9,1},{10,2},{11,3},{12,4},{13,5},{14,6},{15,7},{16,8},{17,9... | collective-permute-start | bytes 1572872 | tf_op jit(solution)/shard_map/ppermute | solution.py:57
  31.1 24.3 %collective-permute-start.5 = (bf16[256,1024]{1,0:T(8,128)(2,1)}, bf16[256,1024]{1,0:T(8,128)(2,1)S(1)}, u32[]{:S(2)}, u32[]{:S(2)}) collective-permute-start(bf16[256,1024]{1,0:T(8,128)(2,1)} %collective-permute-done.3), channel_id=1, source_target_pairs={{8,16},{9,17},{10,18},{11,19},{12,20},{13,21},{14,22},{15,23},{18,... | collective-permute-start | bytes 1572872 | tf_op jit(solution)/shard_map/ppermute | solution.py:57
  41.4 20.2 %collective-permute-start.11 = (bf16[256,1024]{1,0:T(8,128)(2,1)}, bf16[256,1024]{1,0:T(8,128)(2,1)S(1)}, u32[]{:S(2)}, u32[]{:S(2)}) collective-permute-start(bf16[256,1024]{1,0:T(8,128)(2,1)} %collective-permute-done.9), channel_id=1, source_target_pairs={{8,16},{9,17},{10,18},{11,19},{12,20},{13,21},{14,22},{15,23},{16,... | collective-permute-start | bytes 1572872 | tf_op jit(solution)/shard_map/ppermute | solution.py:57
  46.2 12.3 %collective-permute-start.12 = (bf16[256,1024]{1,0:T(8,128)(2,1)S(1)}, bf16[256,1024]{1,0:T(8,128)(2,1)S(1)}, u32[]{:S(2)}, u32[]{:S(2)}) collective-permute-start(bf16[256,1024]{1,0:T(8,128)(2,1)S(1)} %collective-permute-done.10), channel_id=1, source_target_pairs={{8,0},{9,1},{10,2},{11,3},{12,4},{13,5},{14,6},{15,7},{18,10},{19,... | collective-permute-start | bytes 1572872 | tf_op jit(solution)/shard_map/ppermute | solution.py:57
  50.9 13.9 %collective-permute-start.8 = (bf16[192,4096]{1,0:T(8,128)(2,1)}, bf16[192,4096]{1,0:T(8,128)(2,1)S(1)}, u32[]{:S(2)}, u32[]{:S(2)}) collective-permute-start(bf16[192,4096]{1,0:T(8,128)(2,1)} %collective-permute-done.7), channel_id=1, source_target_pairs={{0,2},{1,3},{2,0},{3,1},{4,6},{5,7},{6,4},{7,5},{8,10},{9,11},{10,... | collective-permute-start | bytes 4718600 | tf_op jit(solution)/shard_map/ppermute | solution.py:57
  55.3 14.9 %collective-permute-start.6 = (bf16[256,1024]{1,0:T(8,128)(2,1)S(1)}, bf16[256,1024]{1,0:T(8,128)(2,1)S(1)}, u32[]{:S(2)}, u32[]{:S(2)}) collective-permute-start(bf16[256,1024]{1,0:T(8,128)(2,1)S(1)} %collective-permute-done.5), channel_id=1, source_target_pairs={{16,24},{17,25},{18,26},{19,27},{20,28},{21,29},{22,30},{23,31}} | collective-permute-start | bytes 1572872 | tf_op jit(solution)/shard_map/ppermute | solution.py:57
  61.6 19.5 %collective-permute-start.13 = (bf16[256,1024]{1,0:T(8,128)(2,1)S(1)}, bf16[256,1024]{1,0:T(8,128)(2,1)S(1)}, u32[]{:S(2)}, u32[]{:S(2)}) collective-permute-start(bf16[256,1024]{1,0:T(8,128)(2,1)S(1)} %collective-permute-done.11), channel_id=1, source_target_pairs={{16,24},{17,25},{18,26},{19,27},{20,28},{21,29},{22,30},{23,31}} | collective-permute-start | bytes 1572872 | tf_op jit(solution)/shard_map/ppermute | solution.py:57
  83.4 17.5 %collective-permute-start.19 = (bf16[768,256]{1,0:T(8,128)(2,1)S(1)}, bf16[768,256]{1,0:T(8,128)(2,1)S(1)}, u32[]{:S(2)}, u32[]{:S(2)}) collective-permute-start(bf16[768,256]{1,0:T(8,128)(2,1)S(1)} %collective-permute-done.16), channel_id=1, source_target_pairs={{0,4},{1,5},{2,6},{3,7},{4,0},{5,1},{6,2},{7,3},{8,12},{9,13},{10,... | collective-permute-start | bytes 1179656 | tf_op jit(solution)/shard_map/ppermute | solution.py:57
  112.0 16.4 %collective-permute-start.24 = (bf16[256,1024]{1,0:T(8,128)(2,1)}, bf16[256,1024]{1,0:T(8,128)(2,1)}, u32[]{:S(2)}, u32[]{:S(2)}) collective-permute-start(bf16[256,1024]{1,0:T(8,128)(2,1)} %get-tuple-element.59), channel_id=1, source_target_pairs={{24,16},{25,17},{26,18},{27,19},{28,20},{29,21},{30,22},{31,23}} | collective-permute-start | bytes 1572872 | tf_op jit(solution)/shard_map/ppermute | solution.py:57
  116.8 20.0 %collective-permute-start.28 = (bf16[256,1024]{1,0:T(8,128)(2,1)}, bf16[256,1024]{1,0:T(8,128)(2,1)}, u32[]{:S(2)}, u32[]{:S(2)}) collective-permute-start(bf16[256,1024]{1,0:T(8,128)(2,1)} %get-tuple-element.57), channel_id=1, source_target_pairs={{0,8},{1,9},{2,10},{3,11},{4,12},{5,13},{6,14},{7,15}} | collective-permute-start | bytes 1572872 | tf_op jit(solution)/shard_map/ppermute | solution.py:57
  118.2 21.4 %collective-permute-start.31 = (bf16[256,1024]{1,0:T(8,128)(2,1)}, bf16[256,1024]{1,0:T(8,128)(2,1)}, u32[]{:S(2)}, u32[]{:S(2)}) collective-permute-start(bf16[256,1024]{1,0:T(8,128)(2,1)} %get-tuple-element.57), channel_id=1, source_target_pairs={{24,16},{25,17},{26,18},{27,19},{28,20},{29,21},{30,22},{31,23}} | collective-permute-start | bytes 1572872 | tf_op jit(solution)/shard_map/ppermute | solution.py:57
  131.4 15.9 %collective-permute-start.22 = (bf16[256,1024]{1,0:T(8,128)(2,1)}, bf16[256,1024]{1,0:T(8,128)(2,1)}, u32[]{:S(2)}, u32[]{:S(2)}) collective-permute-start(bf16[256,1024]{1,0:T(8,128)(2,1)} %get-tuple-element.29), channel_id=1, source_target_pairs={{0,8},{1,9},{2,10},{3,11},{4,12},{5,13},{6,14},{7,15},{8,16},{9,17... | collective-permute-start | bytes 1572872 | tf_op jit(solution)/shard_map/ppermute | solution.py:57
  132.7 18.1 %collective-permute-start.25 = (bf16[256,1024]{1,0:T(8,128)(2,1)}, bf16[256,1024]{1,0:T(8,128)(2,1)}, u32[]{:S(2)}, u32[]{:S(2)}) collective-permute-start(bf16[256,1024]{1,0:T(8,128)(2,1)} %get-tuple-element.30), channel_id=1, source_target_pairs={{16,8},{17,9},{18,10},{19,11},{20,12},{21,13},{22,14},{23,15},{24,... | collective-permute-start | bytes 1572872 | tf_op jit(solution)/shard_map/ppermute | solution.py:57
  142.1 18.5 %collective-permute-start.29 = (bf16[256,1024]{1,0:T(8,128)(2,1)S(1)}, bf16[256,1024]{1,0:T(8,128)(2,1)S(1)}, u32[]{:S(2)}, u32[]{:S(2)}) collective-permute-start(bf16[256,1024]{1,0:T(8,128)(2,1)S(1)} %get-tuple-element.35), channel_id=1, source_target_pairs={{0,8},{1,9},{2,10},{3,11},{4,12},{5,13},{6,14},{7,15},{8,16},{9,17... | collective-permute-start | bytes 1572872 | tf_op jit(solution)/shard_map/ppermute | solution.py:57
  143.4 18.6 %collective-permute-start.32 = (bf16[256,1024]{1,0:T(8,128)(2,1)S(1)}, bf16[256,1024]{1,0:T(8,128)(2,1)S(1)}, u32[]{:S(2)}, u32[]{:S(2)}) collective-permute-start(bf16[256,1024]{1,0:T(8,128)(2,1)S(1)} %get-tuple-element.36), channel_id=1, source_target_pairs={{16,8},{17,9},{18,10},{19,11},{20,12},{21,13},{22,14},{23,15},{24,... | collective-permute-start | bytes 1572872 | tf_op jit(solution)/shard_map/ppermute | solution.py:57
  152.8 20.4 %collective-permute-start.26 = (bf16[256,1024]{1,0:T(8,128)(2,1)S(1)}, bf16[256,1024]{1,0:T(8,128)(2,1)S(1)}, u32[]{:S(2)}, u32[]{:S(2)}) collective-permute-start(bf16[256,1024]{1,0:T(8,128)(2,1)S(1)} %get-tuple-element.22), channel_id=1, source_target_pairs={{8,0},{9,1},{10,2},{11,3},{12,4},{13,5},{14,6},{15,7},{16,8},{17,9... | collective-permute-start | bytes 1572872 | tf_op jit(solution)/shard_map/ppermute | solution.py:57
  154.9 18.3 %collective-permute-start.23 = (bf16[256,1024]{1,0:T(8,128)(2,1)S(1)}, bf16[256,1024]{1,0:T(8,128)(2,1)S(1)}, u32[]{:S(2)}, u32[]{:S(2)}) collective-permute-start(bf16[256,1024]{1,0:T(8,128)(2,1)S(1)} %get-tuple-element.21), channel_id=1, source_target_pairs={{0,8},{1,9},{2,10},{3,11},{4,12},{5,13},{6,14},{7,15},{8,16},{9,17... | collective-permute-start | bytes 1572872 | tf_op jit(solution)/shard_map/ppermute | solution.py:57
  162.4 22.1 %collective-permute-start.33 = (bf16[256,1024]{1,0:T(8,128)(2,1)S(1)}, bf16[256,1024]{1,0:T(8,128)(2,1)S(1)}, u32[]{:S(2)}, u32[]{:S(2)}) collective-permute-start(bf16[256,1024]{1,0:T(8,128)(2,1)S(1)} %get-tuple-element.24), channel_id=1, source_target_pairs={{8,0},{9,1},{10,2},{11,3},{12,4},{13,5},{14,6},{15,7},{16,8},{17,9... | collective-permute-start | bytes 1572872 | tf_op jit(solution)/shard_map/ppermute | solution.py:57
  164.3 20.1 %collective-permute-start.30 = (bf16[256,1024]{1,0:T(8,128)(2,1)S(1)}, bf16[256,1024]{1,0:T(8,128)(2,1)S(1)}, u32[]{:S(2)}, u32[]{:S(2)}) collective-permute-start(bf16[256,1024]{1,0:T(8,128)(2,1)S(1)} %get-tuple-element.23), channel_id=1, source_target_pairs={{0,8},{1,9},{2,10},{3,11},{4,12},{5,13},{6,14},{7,15},{8,16},{9,17... | collective-permute-start | bytes 1572872 | tf_op jit(solution)/shard_map/ppermute | solution.py:57
  (28 other events, 255.5 us)

commit v8 on v7

--- a/solution.py
+++ b/solution.py
@@ -174,11 +174,9 @@
 
     def summed(cols):
         far = block(z ^ 3, cols)
-        right = send(far.astype(BF16), to_right(1))
-        left = send(far.astype(BF16), to_left(1))
-        next_far = block(z ^ 2, cols)
-        right = send((next_far + right.astype(F32)).astype(BF16), to_right(2))
-        left = send((next_far + left.astype(F32)).astype(BF16), to_left(2))
+        ends = send(far.astype(BF16), to_right(1) + to_left(1))
+        message = (block(z ^ 2, cols) + ends.astype(F32)).astype(BF16)
+        right, left = send(message, to_right(2)), send(message, to_left(2))
         near = block(z ^ 1, cols)
         right = (jnp.where(z == 1, far, near) + right.astype(F32)).astype(BF16)
         left = (jnp.where(z == 2, far, near) + left.astype(F32)).astype(BF16)

time: 190 us -> 188 us (0.989)
  starting transfers between devices: 62.4 us -> 59.3 us
  waiting for transfers between devices: 71.2 us -> 73.4 us
    ppermute x34 -> x32, starting transfers between devices: 62.4 us -> 59.3 us  [send(): return lax.ppermute(value, AXES, pairs)]
    ppermute x34 -> x32, waiting for transfers between devices: 71.2 us -> 73.4 us  [send(): return lax.ppermute(value, AXES, pairs)]
  transfers between devices with their start and end apart: 34 -> 32, of which waited for: 14 -> 14; matrix products, arithmetic and copies ran while one was open for 24% -> 24% of each run, Pallas kernels for 0% -> 0%
where the time goes in v8:
time: 188 us; the launch traced here: 187 us
  waiting for transfers between devices  73.4 us (39%)
  starting transfers between devices  59.3 us (32%)
  matrix products  35.1 us (19%)
  other arithmetic  14.2 us (8%)
  local copies, waits for them, and re-layouts  3.61 us (2%)
    ppermute x32, waiting for transfers between devices, send(): return lax.ppermute(value, AXES, pairs)  73.4 us
    ppermute x32, starting transfers between devices, send(): return lax.ppermute(value, AXES, pairs)  59.3 us
    dot_general x24, matrix products, rows_by_rows(): lax.dot_general(a, b, (((1,), (1,)), ((), ())), preferred_element_type=F32)  18.2 us
    dot_general x8, matrix products, columns_by_columns(): lax.dot_general(a, b, (((0,), (0,)), ((), ())), preferred_element_type=F32)  16.9 us
  transfers between devices with their start and end apart: 32, of which 14 were waited for; matrix products, arithmetic and copies ran while one was open for 24% of the time, Pallas kernels for 0%

profile of v8, /device:TPU:19, one launch (start us, length us, event | category | flops | bytes accessed | tf_op | source)
XLA Modules:
  0.0 186.9 jit_solution(5193073426947292060)
XLA Ops:
  7.4 2.3 %collective-permute-done.1 = bf16[256,512]{1,0:T(8,128)(2,1)} collective-permute-done((bf16[256,512]{1,0:T(8,128)(2,1)}, bf16[256,512]{1,0:T(8,128)(2,1)}, u32[]{:S(2)}, u32[]{:S(2)}) %collective-permute-start.1) | collective-permute-done | bytes 262176 | tf_op jit(solution)/shard_map/ppermute | solution.py:57
  9.7 6.6 %collective-permute-done.2 = bf16[256,512]{1,0:T(8,128)(2,1)} collective-permute-done((bf16[256,512]{1,0:T(8,128)(2,1)}, bf16[256,512]{1,0:T(8,128)(2,1)}, u32[]{:S(2)}, u32[]{:S(2)}) %collective-permute-start.2) | collective-permute-done | bytes 262176 | tf_op jit(solution)/shard_map/ppermute | solution.py:57
  20.9 3.4 %collective-permute-start.9 = (bf16[256,1024]{1,0:T(8,128)(2,1)}, bf16[256,1024]{1,0:T(8,128)(2,1)}, u32[]{:S(2)}, u32[]{:S(2)}) collective-permute-start(bf16[256,1024]{1,0:T(8,128)(2,1)} %get-tuple-element.33), channel_id=1, source_target_pairs={{0,8},{1,9},{2,10},{3,11},{4,12},{5,13},{6,14},{7,15},{8,16},{9,17... | collective-permute-start | bytes 1572872 | tf_op jit(solution)/shard_map/ppermute | solution.py:57
  25.0 6.0 %collective-permute-start.10 = (bf16[256,1024]{1,0:T(8,128)(2,1)}, bf16[256,1024]{1,0:T(8,128)(2,1)S(1)}, u32[]{:S(2)}, u32[]{:S(2)}) collective-permute-start(bf16[256,1024]{1,0:T(8,128)(2,1)} %get-tuple-element.33), channel_id=1, source_target_pairs={{8,0},{9,1},{10,2},{11,3},{12,4},{13,5},{14,6},{15,7},{16,8},{17,9... | collective-permute-start | bytes 1572872 | tf_op jit(solution)/shard_map/ppermute | solution.py:57
  34.4 6.9 %collective-permute-done.9 = bf16[256,1024]{1,0:T(8,128)(2,1)} collective-permute-done((bf16[256,1024]{1,0:T(8,128)(2,1)}, bf16[256,1024]{1,0:T(8,128)(2,1)}, u32[]{:S(2)}, u32[]{:S(2)}) %collective-permute-start.9) | collective-permute-done | bytes 524320 | tf_op jit(solution)/shard_map/ppermute | solution.py:57
  46.2 3.4 %collective-permute-start.12 = (bf16[256,1024]{1,0:T(8,128)(2,1)S(1)}, bf16[256,1024]{1,0:T(8,128)(2,1)S(1)}, u32[]{:S(2)}, u32[]{:S(2)}) collective-permute-start(bf16[256,1024]{1,0:T(8,128)(2,1)S(1)} %collective-permute-done.10), channel_id=1, source_target_pairs={{8,0},{9,1},{10,2},{11,3},{12,4},{13,5},{14,6},{15,7},{18,10},{19,... | collective-permute-start | bytes 1572872 | tf_op jit(solution)/shard_map/ppermute | solution.py:57
  55.3 3.2 %collective-permute-start.6 = (bf16[256,1024]{1,0:T(8,128)(2,1)S(1)}, bf16[256,1024]{1,0:T(8,128)(2,1)S(1)}, u32[]{:S(2)}, u32[]{:S(2)}) collective-permute-start(bf16[256,1024]{1,0:T(8,128)(2,1)S(1)} %collective-permute-done.5), channel_id=1, source_target_pairs={{16,24},{17,25},{18,26},{19,27},{20,28},{21,29},{22,30},{23,31}} | collective-permute-start | bytes 1572872 | tf_op jit(solution)/shard_map/ppermute | solution.py:57
  59.3 2.3 %collective-permute-done.11 = bf16[256,1024]{1,0:T(8,128)(2,1)S(1)} collective-permute-done((bf16[256,1024]{1,0:T(8,128)(2,1)}, bf16[256,1024]{1,0:T(8,128)(2,1)S(1)}, u32[]{:S(2)}, u32[]{:S(2)}) %collective-permute-start.11) | collective-permute-done | bytes 524320 | tf_op jit(solution)/shard_map/ppermute | solution.py:57
  76.3 4.8 %collective-permute-done.13 = bf16[256,1024]{1,0:T(8,128)(2,1)S(1)} collective-permute-done((bf16[256,1024]{1,0:T(8,128)(2,1)S(1)}, bf16[256,1024]{1,0:T(8,128)(2,1)S(1)}, u32[]{:S(2)}, u32[]{:S(2)}) %collective-permute-start.13) | collective-permute-done | bytes 524320 | tf_op jit(solution)/shard_map/ppermute | solution.py:57
  84.7 7.8 %collective-permute-done.18 = bf16[768,256]{1,0:T(8,128)(2,1)S(1)} collective-permute-done((bf16[768,256]{1,0:T(8,128)(2,1)S(1)}, bf16[768,256]{1,0:T(8,128)(2,1)S(1)}, u32[]{:S(2)}, u32[]{:S(2)}) %collective-permute-start.18) | collective-permute-done | bytes 393248 | tf_op jit(solution)/shard_map/ppermute | solution.py:57
  94.2 6.7 %collective-permute-done.19 = bf16[768,256]{1,0:T(8,128)(2,1)S(1)} collective-permute-done((bf16[768,256]{1,0:T(8,128)(2,1)S(1)}, bf16[768,256]{1,0:T(8,128)(2,1)S(1)}, u32[]{:S(2)}, u32[]{:S(2)}) %collective-permute-start.19) | collective-permute-done | bytes 393248 | tf_op jit(solution)/shard_map/ppermute | solution.py:57
  103.1 3.1 %collective-permute-start.26 = (bf16[768,1024]{1,0:T(8,128)(2,1)}, bf16[768,1024]{1,0:T(8,128)(2,1)}, u32[]{:S(2)}, u32[]{:S(2)}) collective-permute-start(bf16[768,1024]{1,0:T(8,128)(2,1)} %pad_maximum_fusion.1), channel_id=1, source_target_pairs={{0,2},{1,3},{2,0},{3,1},{4,6},{5,7},{6,4},{7,5},{8,10},{9,11},{10,... | collective-permute-start | bytes 4718600 | tf_op jit(solution)/shard_map/ppermute | solution.py:57
  111.9 3.4 %fusion.86 = (bf16[256,1024]{1,0:T(8,128)(2,1)}, f32[256,1024]{1,0:T(8,128)}) fusion(bf16[768,1024]{1,0:T(8,128)(2,1)} %collective-permute-done.26, bf16[768,1024]{1,0:T(8,128)(2,1)} %copy-done.1, s32[]{:T(128)S(6)} %select_n.329), kind=kOutput, calls=%fused_computation.166 | convolution fusion | flops 402915328 | bytes 3538948 | tf_op jit(solution)/shard_map/dot_general | solution.py:16
  116.5 10.3 %collective-permute-done.21 = bf16[256,1024]{1,0:T(8,128)(2,1)} collective-permute-done((bf16[256,1024]{1,0:T(8,128)(2,1)}, bf16[256,1024]{1,0:T(8,128)(2,1)}, u32[]{:S(2)}, u32[]{:S(2)}) %collective-permute-start.21) | collective-permute-done | bytes 524320 | tf_op jit(solution)/shard_map/ppermute | solution.py:57
  126.9 2.6 %fusion.2 = bf16[256,1024]{1,0:T(8,128)(2,1)} fusion(bf16[256,1024]{1,0:T(8,128)(2,1)} %collective-permute-done.21, bf16[768,1024]{1,0:T(8,128)(2,1)} %copy-done.1, s32[]{:T(128)S(6)} %select_n.332, bf16[768,256]{1,0:T(8,128)(2,1)S(1)} %copy-done.14, bf16[768,256]{1,0:T(8,128)(2,1)S(1)} %copy-done.6, bf16[768,256]{1,0:T(8,128)(2,1)S(1)} %copy-done.10, ...), kind=kOutput, calls=%fused_computation.25 | convolution fusion | flops 409731072 | bytes 3014660 | tf_op jit(solution)/shard_map/dot_general | solution.py:16
  130.7 4.0 %collective-permute-start.24 = (bf16[256,1024]{1,0:T(8,128)(2,1)}, bf16[256,1024]{1,0:T(8,128)(2,1)}, u32[]{:S(2)}, u32[]{:S(2)}) collective-permute-start(bf16[256,1024]{1,0:T(8,128)(2,1)} %fusion.2), channel_id=1, source_target_pairs={{16,8},{17,9},{18,10},{19,11},{20,12},{21,13},{22,14},{23,15},{24,... | collective-permute-start | bytes 1572872 | tf_op jit(solution)/shard_map/ppermute | solution.py:57
  134.8 3.3 %collective-permute-done.27 = bf16[256,1024]{1,0:T(8,128)(2,1)} collective-permute-done((bf16[256,1024]{1,0:T(8,128)(2,1)}, bf16[256,1024]{1,0:T(8,128)(2,1)}, u32[]{:S(2)}, u32[]{:S(2)}) %collective-permute-start.27) | collective-permute-done | bytes 524320 | tf_op jit(solution)/shard_map/ppermute | solution.py:57
  138.1 2.2 %fusion.3 = bf16[256,1024]{1,0:T(8,128)(2,1)S(1)} fusion(bf16[768,1024]{1,0:T(8,128)(2,1)} %collective-permute-done.26, bf16[256,1024]{1,0:T(8,128)(2,1)} %collective-permute-done.27, bf16[768,1024]{1,0:T(8,128)(2,1)} %copy-done.1, s32[]{:T(128)S(6)} %select_n.332), kind=kOutput, calls=%fused_computation.26 | convolution fusion | flops 403439616 | bytes 3014660 | tf_op jit(solution)/shard_map/dot_general | solution.py:16
  141.7 4.0 %collective-permute-start.30 = (bf16[256,1024]{1,0:T(8,128)(2,1)S(1)}, bf16[256,1024]{1,0:T(8,128)(2,1)S(1)}, u32[]{:S(2)}, u32[]{:S(2)}) collective-permute-start(bf16[256,1024]{1,0:T(8,128)(2,1)S(1)} %fusion.3), channel_id=1, source_target_pairs={{16,8},{17,9},{18,10},{19,11},{20,12},{21,13},{22,14},{23,15},{24,... | collective-permute-start | bytes 1572872 | tf_op jit(solution)/shard_map/ppermute | solution.py:57
  145.7 3.7 %collective-permute-done.24 = bf16[256,1024]{1,0:T(8,128)(2,1)} collective-permute-done((bf16[256,1024]{1,0:T(8,128)(2,1)}, bf16[256,1024]{1,0:T(8,128)(2,1)}, u32[]{:S(2)}, u32[]{:S(2)}) %collective-permute-start.24) | collective-permute-done | bytes 524320 | tf_op jit(solution)/shard_map/ppermute | solution.py:57
  153.7 3.4 %collective-permute-start.23 = (bf16[256,1024]{1,0:T(8,128)(2,1)S(1)}, bf16[256,1024]{1,0:T(8,128)(2,1)S(1)}, u32[]{:S(2)}, u32[]{:S(2)}) collective-permute-start(bf16[256,1024]{1,0:T(8,128)(2,1)S(1)} %get-tuple-element.21), channel_id=1, source_target_pairs={{0,8},{1,9},{2,10},{3,11},{4,12},{5,13},{6,14},{7,15},{8,16},{9,17... | collective-permute-start | bytes 1572872 | tf_op jit(solution)/shard_map/ppermute | solution.py:57
  162.8 3.4 %collective-permute-start.29 = (bf16[256,1024]{1,0:T(8,128)(2,1)S(1)}, bf16[256,1024]{1,0:T(8,128)(2,1)S(1)}, u32[]{:S(2)}, u32[]{:S(2)}) collective-permute-start(bf16[256,1024]{1,0:T(8,128)(2,1)S(1)} %get-tuple-element.23), channel_id=1, source_target_pairs={{0,8},{1,9},{2,10},{3,11},{4,12},{5,13},{6,14},{7,15},{8,16},{9,17... | collective-permute-start | bytes 1572872 | tf_op jit(solution)/shard_map/ppermute | solution.py:57
  166.2 5.5 %collective-permute-done.25 = bf16[256,1024]{1,0:T(8,128)(2,1)S(1)} collective-permute-done((bf16[256,1024]{1,0:T(8,128)(2,1)S(1)}, bf16[256,1024]{1,0:T(8,128)(2,1)S(1)}, u32[]{:S(2)}, u32[]{:S(2)}) %collective-permute-start.25) | collective-permute-done | bytes 524320 | tf_op jit(solution)/shard_map/ppermute | solution.py:57
  172.4 10.5 %collective-permute-done.31 = bf16[256,1024]{1,0:T(8,128)(2,1)S(1)} collective-permute-done((bf16[256,1024]{1,0:T(8,128)(2,1)S(1)}, bf16[256,1024]{1,0:T(8,128)(2,1)S(1)}, u32[]{:S(2)}, u32[]{:S(2)}) %collective-permute-start.31) | collective-permute-done | bytes 524320 | tf_op jit(solution)/shard_map/ppermute | solution.py:57
  (128 shorter events, 72.6 us)
Async XLA Ops:
  2.5 13.9 %collective-permute-start.2 = (bf16[256,512]{1,0:T(8,128)(2,1)}, bf16[256,512]{1,0:T(8,128)(2,1)}, u32[]{:S(2)}, u32[]{:S(2)}) collective-permute-start(bf16[256,512]{1,0:T(8,128)(2,1)} %get-tuple-element.12), channel_id=1, source_target_pairs={{0,5},{1,4},{2,7},{3,6},{4,1},{5,0},{6,3},{7,2},{8,13},{9,12},{10,... | collective-permute-start | bytes 786440 | tf_op jit(solution)/shard_map/ppermute | solution.py:57
  4.7 12.8 %collective-permute-start = (bf16[256,512]{1,0:T(8,128)(2,1)}, bf16[256,512]{1,0:T(8,128)(2,1)}, u32[]{:S(2)}, u32[]{:S(2)}) collective-permute-start(bf16[256,512]{1,0:T(8,128)(2,1)} %get-tuple-element.10), channel_id=1, source_target_pairs={{0,1},{1,0},{2,3},{3,2},{4,5},{5,4},{6,7},{7,6},{8,9},{9,8},{10,11... | collective-permute-start | bytes 786440 | tf_op jit(solution)/shard_map/ppermute | solution.py:57
  6.2 44.7 %collective-permute-start.7 = (bf16[192,4096]{1,0:T(8,128)(2,1)}, bf16[192,4096]{1,0:T(8,128)(2,1)}, u32[]{:S(2)}, u32[]{:S(2)}) collective-permute-start(bf16[192,4096]{1,0:T(8,128)(2,1)} %constant_dynamic-slice_fusion), channel_id=1, source_target_pairs={{0,1},{1,0},{2,3},{3,2},{4,5},{5,4},{6,7},{7,6},{8,9},{9,8},{10,11... | collective-permute-start | bytes 4718600 | tf_op jit(solution)/shard_map/ppermute | solution.py:57
  20.9 20.5 %collective-permute-start.9 = (bf16[256,1024]{1,0:T(8,128)(2,1)}, bf16[256,1024]{1,0:T(8,128)(2,1)}, u32[]{:S(2)}, u32[]{:S(2)}) collective-permute-start(bf16[256,1024]{1,0:T(8,128)(2,1)} %get-tuple-element.33), channel_id=1, source_target_pairs={{0,8},{1,9},{2,10},{3,11},{4,12},{5,13},{6,14},{7,15},{8,16},{9,17... | collective-permute-start | bytes 1572872 | tf_op jit(solution)/shard_map/ppermute | solution.py:57
  24.3 30.6 %collective-permute-start.4 = (bf16[256,1024]{1,0:T(8,128)(2,1)}, bf16[256,1024]{1,0:T(8,128)(2,1)S(1)}, u32[]{:S(2)}, u32[]{:S(2)}) collective-permute-start(bf16[256,1024]{1,0:T(8,128)(2,1)} %get-tuple-element.34), channel_id=1, source_target_pairs={{10,2},{11,3},{14,6},{15,7}} | collective-permute-start | bytes 1572872 | tf_op jit(solution)/shard_map/ppermute | solution.py:57
  25.0 21.2 %collective-permute-start.10 = (bf16[256,1024]{1,0:T(8,128)(2,1)}, bf16[256,1024]{1,0:T(8,128)(2,1)S(1)}, u32[]{:S(2)}, u32[]{:S(2)}) collective-permute-start(bf16[256,1024]{1,0:T(8,128)(2,1)} %get-tuple-element.33), channel_id=1, source_target_pairs={{8,0},{9,1},{10,2},{11,3},{12,4},{13,5},{14,6},{15,7},{16,8},{17,9... | collective-permute-start | bytes 1572872 | tf_op jit(solution)/shard_map/ppermute | solution.py:57
  31.1 24.3 %collective-permute-start.5 = (bf16[256,1024]{1,0:T(8,128)(2,1)}, bf16[256,1024]{1,0:T(8,128)(2,1)S(1)}, u32[]{:S(2)}, u32[]{:S(2)}) collective-permute-start(bf16[256,1024]{1,0:T(8,128)(2,1)} %collective-permute-done.3), channel_id=1, source_target_pairs={{8,16},{9,17},{10,18},{11,19},{12,20},{13,21},{14,22},{15,23},{18,... | collective-permute-start | bytes 1572872 | tf_op jit(solution)/shard_map/ppermute | solution.py:57
  41.4 20.2 %collective-permute-start.11 = (bf16[256,1024]{1,0:T(8,128)(2,1)}, bf16[256,1024]{1,0:T(8,128)(2,1)S(1)}, u32[]{:S(2)}, u32[]{:S(2)}) collective-permute-start(bf16[256,1024]{1,0:T(8,128)(2,1)} %collective-permute-done.9), channel_id=1, source_target_pairs={{8,16},{9,17},{10,18},{11,19},{12,20},{13,21},{14,22},{15,23},{16,... | collective-permute-start | bytes 1572872 | tf_op jit(solution)/shard_map/ppermute | solution.py:57
  46.2 12.3 %collective-permute-start.12 = (bf16[256,1024]{1,0:T(8,128)(2,1)S(1)}, bf16[256,1024]{1,0:T(8,128)(2,1)S(1)}, u32[]{:S(2)}, u32[]{:S(2)}) collective-permute-start(bf16[256,1024]{1,0:T(8,128)(2,1)S(1)} %collective-permute-done.10), channel_id=1, source_target_pairs={{8,0},{9,1},{10,2},{11,3},{12,4},{13,5},{14,6},{15,7},{18,10},{19,... | collective-permute-start | bytes 1572872 | tf_op jit(solution)/shard_map/ppermute | solution.py:57
  50.9 13.9 %collective-permute-start.8 = (bf16[192,4096]{1,0:T(8,128)(2,1)}, bf16[192,4096]{1,0:T(8,128)(2,1)S(1)}, u32[]{:S(2)}, u32[]{:S(2)}) collective-permute-start(bf16[192,4096]{1,0:T(8,128)(2,1)} %collective-permute-done.7), channel_id=1, source_target_pairs={{0,2},{1,3},{2,0},{3,1},{4,6},{5,7},{6,4},{7,5},{8,10},{9,11},{10,... | collective-permute-start | bytes 4718600 | tf_op jit(solution)/shard_map/ppermute | solution.py:57
  55.3 14.9 %collective-permute-start.6 = (bf16[256,1024]{1,0:T(8,128)(2,1)S(1)}, bf16[256,1024]{1,0:T(8,128)(2,1)S(1)}, u32[]{:S(2)}, u32[]{:S(2)}) collective-permute-start(bf16[256,1024]{1,0:T(8,128)(2,1)S(1)} %collective-permute-done.5), channel_id=1, source_target_pairs={{16,24},{17,25},{18,26},{19,27},{20,28},{21,29},{22,30},{23,31}} | collective-permute-start | bytes 1572872 | tf_op jit(solution)/shard_map/ppermute | solution.py:57
  61.6 19.5 %collective-permute-start.13 = (bf16[256,1024]{1,0:T(8,128)(2,1)S(1)}, bf16[256,1024]{1,0:T(8,128)(2,1)S(1)}, u32[]{:S(2)}, u32[]{:S(2)}) collective-permute-start(bf16[256,1024]{1,0:T(8,128)(2,1)S(1)} %collective-permute-done.11), channel_id=1, source_target_pairs={{16,24},{17,25},{18,26},{19,27},{20,28},{21,29},{22,30},{23,31}} | collective-permute-start | bytes 1572872 | tf_op jit(solution)/shard_map/ppermute | solution.py:57
  71.2 12.2 %collective-permute-start.16 = (bf16[768,256]{1,0:T(8,128)(2,1)S(1)}, bf16[768,256]{1,0:T(8,128)(2,1)S(1)}, u32[]{:S(2)}, u32[]{:S(2)}) collective-permute-start(bf16[768,256]{1,0:T(8,128)(2,1)S(1)} %pad_maximum_fusion.6), channel_id=1, source_target_pairs={{0,1},{1,0},{2,3},{3,2},{4,5},{5,4},{6,7},{7,6},{8,9},{9,8},{10,11... | collective-permute-start | bytes 1179656 | tf_op jit(solution)/shard_map/ppermute | solution.py:57
  83.4 17.5 %collective-permute-start.19 = (bf16[768,256]{1,0:T(8,128)(2,1)S(1)}, bf16[768,256]{1,0:T(8,128)(2,1)S(1)}, u32[]{:S(2)}, u32[]{:S(2)}) collective-permute-start(bf16[768,256]{1,0:T(8,128)(2,1)S(1)} %collective-permute-done.16), channel_id=1, source_target_pairs={{0,4},{1,5},{2,6},{3,7},{4,0},{5,1},{6,2},{7,3},{8,12},{9,13},{10,... | collective-permute-start | bytes 1179656 | tf_op jit(solution)/shard_map/ppermute | solution.py:57
  110.5 16.3 %collective-permute-start.21 = (bf16[256,1024]{1,0:T(8,128)(2,1)}, bf16[256,1024]{1,0:T(8,128)(2,1)}, u32[]{:S(2)}, u32[]{:S(2)}) collective-permute-start(bf16[256,1024]{1,0:T(8,128)(2,1)} %get-tuple-element.55), channel_id=1, source_target_pairs={{0,8},{1,9},{2,10},{3,11},{4,12},{5,13},{6,14},{7,15},{24,16},{25,... | collective-permute-start | bytes 1572872 | tf_op jit(solution)/shard_map/ppermute | solution.py:57
  115.2 22.8 %collective-permute-start.27 = (bf16[256,1024]{1,0:T(8,128)(2,1)}, bf16[256,1024]{1,0:T(8,128)(2,1)}, u32[]{:S(2)}, u32[]{:S(2)}) collective-permute-start(bf16[256,1024]{1,0:T(8,128)(2,1)} %get-tuple-element.53), channel_id=1, source_target_pairs={{0,8},{1,9},{2,10},{3,11},{4,12},{5,13},{6,14},{7,15},{24,16},{25,... | collective-permute-start | bytes 1572872 | tf_op jit(solution)/shard_map/ppermute | solution.py:57
  129.4 16.2 %collective-permute-start.22 = (bf16[256,1024]{1,0:T(8,128)(2,1)}, bf16[256,1024]{1,0:T(8,128)(2,1)}, u32[]{:S(2)}, u32[]{:S(2)}) collective-permute-start(bf16[256,1024]{1,0:T(8,128)(2,1)} %fusion.2), channel_id=1, source_target_pairs={{0,8},{1,9},{2,10},{3,11},{4,12},{5,13},{6,14},{7,15},{8,16},{9,17... | collective-permute-start | bytes 1572872 | tf_op jit(solution)/shard_map/ppermute | solution.py:57
  130.7 18.6 %collective-permute-start.24 = (bf16[256,1024]{1,0:T(8,128)(2,1)}, bf16[256,1024]{1,0:T(8,128)(2,1)}, u32[]{:S(2)}, u32[]{:S(2)}) collective-permute-start(bf16[256,1024]{1,0:T(8,128)(2,1)} %fusion.2), channel_id=1, source_target_pairs={{16,8},{17,9},{18,10},{19,11},{20,12},{21,13},{22,14},{23,15},{24,... | collective-permute-start | bytes 1572872 | tf_op jit(solution)/shard_map/ppermute | solution.py:57
  140.4 18.8 %collective-permute-start.28 = (bf16[256,1024]{1,0:T(8,128)(2,1)S(1)}, bf16[256,1024]{1,0:T(8,128)(2,1)S(1)}, u32[]{:S(2)}, u32[]{:S(2)}) collective-permute-start(bf16[256,1024]{1,0:T(8,128)(2,1)S(1)} %fusion.3), channel_id=1, source_target_pairs={{0,8},{1,9},{2,10},{3,11},{4,12},{5,13},{6,14},{7,15},{8,16},{9,17... | collective-permute-start | bytes 1572872 | tf_op jit(solution)/shard_map/ppermute | solution.py:57
  141.7 18.8 %collective-permute-start.30 = (bf16[256,1024]{1,0:T(8,128)(2,1)S(1)}, bf16[256,1024]{1,0:T(8,128)(2,1)S(1)}, u32[]{:S(2)}, u32[]{:S(2)}) collective-permute-start(bf16[256,1024]{1,0:T(8,128)(2,1)S(1)} %fusion.3), channel_id=1, source_target_pairs={{16,8},{17,9},{18,10},{19,11},{20,12},{21,13},{22,14},{23,15},{24,... | collective-permute-start | bytes 1572872 | tf_op jit(solution)/shard_map/ppermute | solution.py:57
  151.6 20.1 %collective-permute-start.25 = (bf16[256,1024]{1,0:T(8,128)(2,1)S(1)}, bf16[256,1024]{1,0:T(8,128)(2,1)S(1)}, u32[]{:S(2)}, u32[]{:S(2)}) collective-permute-start(bf16[256,1024]{1,0:T(8,128)(2,1)S(1)} %get-tuple-element.22), channel_id=1, source_target_pairs={{8,0},{9,1},{10,2},{11,3},{12,4},{13,5},{14,6},{15,7},{16,8},{17,9... | collective-permute-start | bytes 1572872 | tf_op jit(solution)/shard_map/ppermute | solution.py:57
  153.7 18.0 %collective-permute-start.23 = (bf16[256,1024]{1,0:T(8,128)(2,1)S(1)}, bf16[256,1024]{1,0:T(8,128)(2,1)S(1)}, u32[]{:S(2)}, u32[]{:S(2)}) collective-permute-start(bf16[256,1024]{1,0:T(8,128)(2,1)S(1)} %get-tuple-element.21), channel_id=1, source_target_pairs={{0,8},{1,9},{2,10},{3,11},{4,12},{5,13},{6,14},{7,15},{8,16},{9,17... | collective-permute-start | bytes 1572872 | tf_op jit(solution)/shard_map/ppermute | solution.py:57
  160.9 22.1 %collective-permute-start.31 = (bf16[256,1024]{1,0:T(8,128)(2,1)S(1)}, bf16[256,1024]{1,0:T(8,128)(2,1)S(1)}, u32[]{:S(2)}, u32[]{:S(2)}) collective-permute-start(bf16[256,1024]{1,0:T(8,128)(2,1)S(1)} %get-tuple-element.24), channel_id=1, source_target_pairs={{8,0},{9,1},{10,2},{11,3},{12,4},{13,5},{14,6},{15,7},{16,8},{17,9... | collective-permute-start | bytes 1572872 | tf_op jit(solution)/shard_map/ppermute | solution.py:57
  162.8 20.1 %collective-permute-start.29 = (bf16[256,1024]{1,0:T(8,128)(2,1)S(1)}, bf16[256,1024]{1,0:T(8,128)(2,1)S(1)}, u32[]{:S(2)}, u32[]{:S(2)}) collective-permute-start(bf16[256,1024]{1,0:T(8,128)(2,1)S(1)} %get-tuple-element.23), channel_id=1, source_target_pairs={{0,8},{1,9},{2,10},{3,11},{4,12},{5,13},{6,14},{7,15},{8,16},{9,17... | collective-permute-start | bytes 1572872 | tf_op jit(solution)/shard_map/ppermute | solution.py:57
  (25 other events, 220.3 us)
